TPU v7x, 32 devices: a whole 2x2x4 slice. The times are simulated.
32 devices in a mesh: grp: 4 (over y, x), seq: 8 (over z, core).
Axes of the slice: x: 2, y: 2, z: 4, core: 2. Of those that a mesh axis runs over, the one named last changes fastest.
Arguments:
- tokens: bfloat16 [8192, 2048], P(('grp', 'seq')), may hold values from -6 to 6
- seq_lengths: int32 [4, 4], P('grp'), may hold values from 1 to 2045, as said below
- cotangent: bfloat16 [8192, 2048], P(('grp', 'seq')), may hold values from -6 to 6
- norm_gain: float32 [2048], replicated, may hold values from 0.5 to 1.5
- input_proj: bfloat16 [2048, 2048], P('seq'), may hold values from -0.125 to 0.125
- forget_proj: bfloat16 [2048, 2048], P('seq'), may hold values from -0.125 to 0.125
- forget_bias: float32 [2048], replicated, may hold values from -2 to 10
- gate_proj: bfloat16 [2048, 2048], P('seq'), may hold values from -0.125 to 0.125
- state_gain: float32 [2048], replicated, may hold values from 0.5 to 1.5
- out_proj: bfloat16 [2048, 2048], P('seq'), may hold values from -0.125 to 0.125
- mlp_gain: float32 [2048], replicated, may hold values from 0.5 to 1.5
- mlp_gate: bfloat16 [2048, 5632], P('seq'), may hold values from -0.125 to 0.125
- mlp_up: bfloat16 [2048, 5632], P('seq'), may hold values from -0.125 to 0.125
- mlp_down: bfloat16 [5632, 2048], P('seq'), may hold values from -0.078125 to 0.078125
Outputs:
- block_out: bfloat16 [8192, 2048], P(('grp', 'seq'))
- grad_tokens: float32 [8192, 2048], P(('grp', 'seq'))
- grad_norm_gain: float32 [2048], replicated
- grad_input_proj: float32 [2048, 2048], P('seq')
- grad_forget_proj: float32 [2048, 2048], P('seq')
- grad_forget_bias: float32 [2048], replicated
- grad_gate_proj: float32 [2048, 2048], P('seq')
- grad_state_gain: float32 [2048], replicated
- grad_out_proj: float32 [2048, 2048], P('seq')
- grad_mlp_gain: float32 [2048], replicated
- grad_mlp_gate: float32 [2048, 5632], P('seq')
- grad_mlp_up: float32 [2048, 5632], P('seq')
- grad_mlp_down: float32 [5632, 2048], P('seq')
Inputs may be any that keep to these rules, and one draw needn't show every extreme that they name: `seq_lengths`: row g holds the lengths of the 4 sequences of group g in the order of its tokens; each row sums to 2048.
All inputs are finite; a program needn't handle non-finite values.
Results may differ from a plain program's by a relative error of at most 0.009.
Values may be sent and summed in bfloat16 or wider, within the bound.
No kernel may reach another device: no remote copies, remote signals or barrier semaphores. Data moves between devices by JAX's collectives and lax.ppermute only.
A program may use at most 512 MiB of HBM per device.

v0:
```python
from functools import partial

import jax
import jax.numpy as jnp
from jax import lax
from jax.sharding import PartitionSpec as P

LOWER = 0.9
EPSILON = 1e-06


def entering(value, axis, join, neutral, backward):
    count, mine = (lax.axis_size(axis), lax.axis_index(axis))
    pieces = jax.tree.map(lambda part: lax.all_gather(part, axis), value)
    if backward:
        pieces = jax.tree.map(lambda part: part[::-1], pieces)
        mine = count - 1 - mine
    running = jax.tree.map(
        lambda part, zero: jnp.full_like(part, 0) + jnp.asarray(zero, part.dtype), value, neutral
    )

    def turn(position, running):
        longer = join(running, jax.tree.map(lambda part: part[position], pieces))
        return jax.tree.map(lambda new, old: jnp.where(position < mine, new, old), longer, running)

    return lax.fori_loop(0, count - 1, turn, running)


def rms_scale(values, weights):
    return values * lax.rsqrt(jnp.mean(values * values, axis=1, keepdims=True) + EPSILON) * weights


def gates(keeping, proj_input, proj_forget, bias_term):
    forget = LOWER + (1.0 - LOWER) * jax.nn.sigmoid(proj_forget + bias_term)
    return (forget * keeping, jax.nn.silu(proj_input) * (1.0 - forget))


def carry_join(earlier, later):
    return (earlier[0] * later[0], later[0] * earlier[1] + later[1])


def output_gate(states, proj_gate, weights):
    return rms_scale(states, weights) * jax.nn.silu(proj_gate)


def glu_hidden(gate_vals, up_vals):
    return jax.nn.silu(gate_vals) * up_vals


def matmul(lhs_arr, rhs_arr):
    return jnp.dot(lhs_arr, rhs_arr, preferred_element_type=jnp.float32)


def matmul_back(lhs_arr, rhs_arr):
    return lax.dot_general(
        lhs_arr, rhs_arr, (((1,), (1,)), ((), ())), preferred_element_type=jnp.float32
    )


def outer_sum(lhs_arr, rhs_arr):
    return lax.dot_general(
        lhs_arr, rhs_arr, (((0,), (0,)), ((), ())), preferred_element_type=jnp.float32
    )


def reduce_rows(pair_list):
    blocks = [outer_sum(left_mat, right_mat) for left_mat, right_mat in pair_list]
    return lax.psum_scatter(jnp.concatenate(blocks, axis=1), "seq", scatter_dimension=0, tiled=True)


def on_device(
    tokens,
    seq_lengths,
    cotangent,
    norm_gain,
    input_proj,
    forget_proj,
    forget_bias,
    gate_proj,
    state_gain,
    out_proj,
    mlp_gain,
    mlp_gate,
    mlp_up,
    mlp_down,
):
    tok_rows = tokens.shape[0]
    width = tokens.shape[1]
    starts = jnp.cumsum(seq_lengths[0]) - seq_lengths[0]
    where_tok = lax.axis_index("seq") * tok_rows + jnp.arange(tok_rows, dtype=jnp.int32)
    keeping = 1.0 - jnp.sum(
        (where_tok[:, None] == starts[None, :]).astype(jnp.float32), axis=1, keepdims=True
    )
    local_weights = (input_proj, forget_proj, gate_proj, out_proj, mlp_gate, mlp_up, mlp_down)
    whole_weights = (
        lax.all_gather(local_weights[0], "seq", axis=0, tiled=True),
        lax.all_gather(local_weights[1], "seq", axis=0, tiled=True),
        lax.all_gather(local_weights[2], "seq", axis=0, tiled=True),
        lax.all_gather(local_weights[3], "seq", axis=0, tiled=True),
        lax.all_gather(local_weights[4], "seq", axis=0, tiled=True),
        lax.all_gather(local_weights[5], "seq", axis=0, tiled=True),
        lax.all_gather(local_weights[6], "seq", axis=0, tiled=True),
    )
    whole_input, whole_forget, whole_gate, whole_output, whole_expand, whole_lift, whole_reduce = (
        whole_weights
    )
    inputs = tokens.astype(jnp.float32)
    normed = rms_scale(inputs, norm_gain).astype(jnp.bfloat16)
    proj_input = matmul(normed, whole_input)
    proj_forget = matmul(normed, whole_forget)
    proj_gate = matmul(normed, whole_gate)
    decay, income = gates(keeping, proj_input, proj_forget, forget_bias)
    prod_local, state_local = lax.associative_scan(carry_join, (decay, income), axis=0)
    identity = (jnp.ones((width,), jnp.float32), jnp.zeros((width,), jnp.float32))
    carry_prod, carry_state = entering(
        (prod_local[-1], state_local[-1]), "seq", carry_join, identity, False
    )
    states = state_local + prod_local * carry_state[None, :]
    gated = output_gate(states, proj_gate, state_gain).astype(jnp.bfloat16)
    middle = inputs + matmul(gated, whole_output)
    normed_mid = rms_scale(middle, mlp_gain).astype(jnp.bfloat16)
    gate_vals = matmul(normed_mid, whole_expand)
    up_vals = matmul(normed_mid, whole_lift)
    hidden = glu_hidden(gate_vals, up_vals).astype(jnp.bfloat16)
    block_out = (middle + matmul(hidden, whole_reduce)).astype(jnp.bfloat16)
    whole_input, whole_forget, whole_gate, whole_output, whole_expand, whole_lift, whole_reduce = (
        lax.all_gather(local_weights[0], "seq", axis=0, tiled=True),
        lax.all_gather(local_weights[1], "seq", axis=0, tiled=True),
        lax.all_gather(local_weights[2], "seq", axis=0, tiled=True),
        lax.all_gather(local_weights[3], "seq", axis=0, tiled=True),
        lax.all_gather(local_weights[4], "seq", axis=0, tiled=True),
        lax.all_gather(local_weights[5], "seq", axis=0, tiled=True),
        lax.all_gather(local_weights[6], "seq", axis=0, tiled=True),
    )
    grad_hidden = matmul_back(cotangent, whole_reduce)
    unused_hidden, pull_glu = jax.vjp(glu_hidden, gate_vals, up_vals)
    grad_gate, grad_up = pull_glu(grad_hidden)
    grad_gate = grad_gate.astype(jnp.bfloat16)
    grad_up = grad_up.astype(jnp.bfloat16)
    grad_normed_mid = matmul_back(grad_gate, whole_expand) + matmul_back(grad_up, whole_lift)
    unused_mid, pull_mid = jax.vjp(rms_scale, middle, mlp_gain)
    back_mid, grad_mlp_gain = pull_mid(grad_normed_mid)
    grad_middle = cotangent.astype(jnp.float32) + back_mid
    grad_mix = grad_middle.astype(jnp.bfloat16)
    grad_gated = matmul_back(grad_mix, whole_output)
    unused_gated, pull_gated = jax.vjp(output_gate, states, proj_gate, state_gain)
    grad_direct, grad_proj_gate, grad_state_gain = pull_gated(grad_gated)
    decay_next = jnp.concatenate([decay[1:], jnp.ones((1, width), jnp.float32)], axis=0)
    after_prod, grad_local = lax.associative_scan(
        carry_join, (decay_next, grad_direct), reverse=True, axis=0
    )
    summary = (decay[0] * after_prod[0], decay[0] * grad_local[0])
    carry_back, incoming = entering(summary, "seq", carry_join, identity, True)
    grad_state = grad_local + after_prod * incoming[None, :]
    state_prev = jnp.concatenate([carry_state[None, :], states[:-1]], axis=0)
    unused_gates, pull_gates = jax.vjp(
        partial(gates, keeping), proj_input, proj_forget, forget_bias
    )
    grad_proj_input, grad_proj_forget, grad_forget_bias = pull_gates(
        (grad_state * state_prev, grad_state)
    )
    grad_proj_cat = jnp.concatenate(
        [
            grad_proj_input.astype(jnp.bfloat16),
            grad_proj_forget.astype(jnp.bfloat16),
            grad_proj_gate.astype(jnp.bfloat16),
        ],
        axis=1,
    )
    grad_normed = (
        matmul_back(grad_proj_cat[:, :width], whole_input)
        + matmul_back(grad_proj_cat[:, width : 2 * width], whole_forget)
        + matmul_back(grad_proj_cat[:, 2 * width :], whole_gate)
    )
    unused_norm, pull_norm = jax.vjp(rms_scale, inputs, norm_gain)
    back_inputs, grad_norm_gain = pull_norm(grad_normed)
    grad_tokens = grad_middle + back_inputs
    grad_ff_cat = jnp.concatenate([grad_gate, grad_up], axis=1)
    mixer_sum = reduce_rows([(normed, grad_proj_cat), (gated, grad_mix)])
    expand_sum = reduce_rows([(normed_mid, grad_ff_cat)])
    reduce_sum = reduce_rows([(hidden, cotangent)])
    mixer_sum, expand_sum, reduce_sum = lax.psum((mixer_sum, expand_sum, reduce_sum), "grp")
    ff_width = hidden.shape[1]
    grad_norm_gain, grad_forget_bias, grad_state_gain, grad_mlp_gain = lax.psum(
        (grad_norm_gain, grad_forget_bias, grad_state_gain, grad_mlp_gain), ("grp", "seq")
    )
    return (
        block_out,
        grad_tokens,
        grad_norm_gain,
        mixer_sum[:, :width],
        mixer_sum[:, width : 2 * width],
        grad_forget_bias,
        mixer_sum[:, 2 * width : 3 * width],
        grad_state_gain,
        mixer_sum[:, 3 * width :],
        grad_mlp_gain,
        expand_sum[:, :ff_width],
        expand_sum[:, ff_width:],
        reduce_sum,
    )


def solution(mesh):
    return jax.shard_map(
        on_device,
        mesh=mesh,
        in_specs=(
            P(("grp", "seq"), None),
            P("grp", None),
            P(("grp", "seq"), None),
            P(),
            P("seq", None),
            P("seq", None),
            P(),
            P("seq", None),
            P(),
            P("seq", None),
            P(),
            P("seq", None),
            P("seq", None),
            P("seq", None),
        ),
        out_specs=(
            P(("grp", "seq"), None),
            P(("grp", "seq"), None),
            P(),
            P("seq", None),
            P("seq", None),
            P(),
            P("seq", None),
            P(),
            P("seq", None),
            P(),
            P("seq", None),
            P("seq", None),
            P("seq", None),
        ),
        check_vma=False,
    )
```

profile of v0, /device:TPU:0, one launch (start us, length us, event | category | flops | bytes accessed | tf_op | source)
XLA Modules:
  0.0 3437.8 jit_solution(5058741044298978133)
XLA Ops:
  12.7 81.7 %all-gather.12.cloned.1.call-done = bf16[2048,2048]{1,0:T(8,128)(2,1)} async-done(((bf16[256,2048]{1,0:T(8,128)(2,1)}), bf16[2048,2048]{1,0:T(8,128)(2,1)}) %all-gather.12.cloned.1.call-update) | async-done | bytes 8388624 | tf_op jit(solution)/shard_map/all_gather | solution.py:96
  101.5 75.1 %all-gather.14.cloned.1.call-done = bf16[2048,2048]{1,0:T(8,128)(2,1)} async-done(((bf16[256,2048]{1,0:T(8,128)(2,1)}), bf16[2048,2048]{1,0:T(8,128)(2,1)}) %all-gather.14.cloned.1.call-update) | async-done | bytes 8388624 | tf_op jit(solution)/shard_map/all_gather | solution.py:97
  341.2 14.3 all-gather
  375.9 18.5 all-gather.1
  415.4 128.7 %all-gather.20.cloned.1.call-done = bf16[2048,5632]{1,0:T(8,128)(2,1)} async-done(((bf16[256,5632]{1,0:T(8,128)(2,1)}), bf16[2048,5632]{1,0:T(8,128)(2,1)}) %all-gather.20.cloned.1.call-update) | async-done | bytes 23068688 | tf_op jit(solution)/shard_map/all_gather | solution.py:100
  544.2 15.0 fusion.92
  559.1 187.4 %all-gather.22.cloned.1.call-done = bf16[2048,5632]{1,0:T(8,128)(2,1)} async-done(((bf16[256,5632]{1,0:T(8,128)(2,1)}), bf16[2048,5632]{1,0:T(8,128)(2,1)}) %all-gather.22.cloned.1.call-update) | async-done | bytes 23068688 | tf_op jit(solution)/shard_map/all_gather | solution.py:101
  746.6 14.9 fusion.93
  761.4 187.7 %all-gather.24.cloned.1.call-done = bf16[5632,2048]{1,0:T(8,128)(2,1)} async-done(((bf16[704,2048]{1,0:T(8,128)(2,1)}), bf16[5632,2048]{1,0:T(8,128)(2,1)}) %all-gather.24.cloned.1.call-update) | async-done | bytes 23068688 | tf_op jit(solution)/shard_map/all_gather | solution.py:102
  949.1 25.0 multiply_convert_fusion
  975.7 17.8 fusion.96
  1021.4 12.9 fusion.94
  1034.4 14.1 multiply_reduce_fusion
  1242.3 16.7 rev.14
  1277.6 16.8 rev.15
  1295.4 14.6 all-gather.2
  1310.2 14.6 all-gather.3
  1339.8 21.2 fusion.8
  1361.1 43.8 %pad_maximum_fusion = f32[2048,8192]{1,0:T(8,128)} fusion(f32[2048,2048]{1,0:T(8,128)} %fusion.44, f32[2048,6144]{1,0:T(8,128)} %fusion.8), kind=kLoop, calls=%fused_computation.6 | loop fusion | flops 16777216 | bytes 134217728 | tf_op jit(solution)/shard_map/concatenate | solution.py:68
  1404.9 35.5 %fusion.3 = f32[2048,11264]{1,0:T(8,128)} fusion(bf16[256,2048]{1,0:T(8,128)(2,1)} %copy-done.21, bf16[256,5632]{1,0:T(8,128)(2,1)} %get-tuple-element.282, bf16[256,5632]{1,0:T(8,128)(2,1)} %get-tuple-element.283), kind=kOutput, calls=%fused_computation.11 | convolution fusion | flops 11822694400 | bytes 99090432 | tf_op jit(solution)/shard_map/dot_general | solution.py:61
  1440.7 637.0 %reduce-scatter.6.cloned.1.call-done = f32[256,8192]{1,0:T(8,128)} async-done(((f32[2048,8192]{1,0:T(8,128)}), f32[256,8192]{1,0:T(8,128)}) %reduce-scatter.6.cloned.1.call-update) | async-done | bytes 8388624 | tf_op jit(solution)/shard_map/reduce_scatter | solution.py:68
  2077.7 876.9 %reduce-scatter.10.cloned.1.call-done = f32[256,11264]{1,0:T(8,128)} async-done(((f32[2048,11264]{1,0:T(8,128)}), f32[256,11264]{1,0:T(8,128)}) %reduce-scatter.10.cloned.1.call-update) | async-done | bytes 11534352
  2972.0 39.1 %all-reduce.67 = (f32[2048]{0:T(1024)}, f32[2048]{0:T(1024)}, f32[2048]{0:T(1024)}, f32[2048]{0:T(1024)}) all-reduce(f32[2048]{0:T(1024)S(1)} %get-tuple-element.243, f32[2048]{0:T(1024)S(1)} %get-tuple-element.272, f32[2048]{0:T(1024)S(1)} %copy-done.85, f32[2048]{0:T(1024)S(1)} %copy-done.84), channel_id=1, replica_groups=mesh['grp'=4,'seq'=8] {'grp','seq'}, use_global_device_ids=true, to_apply=%region_13.14 | all-reduce | flops 8192 | bytes 65536 | tf_op jit(solution)/shard_map/psum | solution.py:184
  3028.1 383.6 %all-reduce.71.cloned.1.call-done = (f32[256,8192]{1,0:T(8,128)}, f32[256,11264]{1,0:T(8,128)}, f32[704,2048]{1,0:T(8,128)}) async-done(((f32[256,8192]{1,0:T(8,128)}, f32[256,11264]{1,0:T(8,128)}, f32[704,2048]{1,0:T(8,128)}), (f32[256,8192]{1,0:T(8,128)}, f32[256,11264]{1,0:T(8,128)}, f32[704,2048]{1,0:T(8,128)})) %all-reduce.71.cloned.1.call-update) | async-done | bytes 25690128 | tf_op jit(solution)/shard_map/psum | solution.py:182
  (542 shorter events, 529.4 us)
Async XLA Ops:
  7.2 87.2 %all-gather.12.cloned.1.call-start = ((), (), s32[]{:S(2)}) async-start(), calls=%async_computation.3 | async-start | bytes 9437184 | tf_op jit(solution)/shard_map/all_gather | solution.py:96
  7.9 168.7 %all-gather.14.cloned.1.call-start = ((), (), s32[]{:S(2)}) async-start(), calls=%async_computation.4 | async-start | bytes 9437184 | tf_op jit(solution)/shard_map/all_gather | solution.py:97
  8.7 390.4 %all-gather.16.cloned.1.call-start = ((), (), s32[]{:S(2)}) async-start(), calls=%async_computation.5 | async-start | bytes 9437184 | tf_op jit(solution)/shard_map/all_gather | solution.py:98
  9.4 398.1 %all-gather.18.cloned.1.call-start = ((), (), s32[]{:S(2)}) async-start(), calls=%async_computation.6 | async-start | bytes 9437184 | tf_op jit(solution)/shard_map/all_gather | solution.py:99
  10.0 534.2 %all-gather.20.cloned.1.call-start = ((), (), s32[]{:S(2)}) async-start(), calls=%async_computation.7 | async-start | bytes 25952256 | tf_op jit(solution)/shard_map/all_gather | solution.py:100
  10.6 736.0 %all-gather.22.cloned.1.call-start = ((), (), s32[]{:S(2)}) async-start(), calls=%async_computation.8 | async-start | bytes 25952256 | tf_op jit(solution)/shard_map/all_gather | solution.py:101
  11.2 83.2 %copy-start.41 = (f32[2048]{0:T(1024)S(1)}, f32[2048]{0:T(1024)}, u32[]{:S(2)}) copy-start(f32[2048]{0:T(1024)} %param.21) | copy-start | bytes 24580
  11.2 937.9 %all-gather.24.cloned.1.call-start = ((), (), s32[]{:S(2)}) async-start(), calls=%async_computation.9 | async-start | bytes 25952256 | tf_op jit(solution)/shard_map/all_gather | solution.py:102
  11.9 1428.7 %reduce-scatter.8.cloned.1.call-start = ((), (), s32[]{:S(2)}) async-start(), calls=%async_computation.11 | async-start | bytes 51904512 | tf_op jit(solution)/shard_map/reduce_scatter | solution.py:68
  12.7 88.8 %copy-start.82 = (f32[256]{0:T(256)}, f32[256]{0:T(256)S(1)}, u32[]{:S(2)}) copy-start(f32[256]{0:T(256)S(1)} %fusion.32) | copy-start | bytes 3076
  12.7 163.9 %copy-start.53 = (f32[256]{0:T(256)}, f32[256]{0:T(256)S(1)}, u32[]{:S(2)}) copy-start(f32[256]{0:T(256)S(1)} %fusion.67) | copy-start | bytes 3076
  12.7 163.9 %copy-start.87 = (f32[256]{0:T(256)}, f32[256]{0:T(256)S(1)}, u32[]{:S(2)}) copy-start(f32[256]{0:T(256)S(1)} %broadcast_subtract_fusion) | copy-start | bytes 3076
  12.7 163.9 %copy-start.89 = (f32[2048]{0:T(1024)S(1)}, f32[2048]{0:T(1024)}, u32[]{:S(2)}) copy-start(f32[2048]{0:T(1024)} %param.24) | copy-start | bytes 24580
  185.8 108.6 %copy-start.4 = (f32[256,2048]{1,0:T(8,128)}, f32[256,2048]{1,0:T(8,128)S(1)}, u32[]{:S(2)}) copy-start(f32[256,2048]{1,0:T(8,128)S(1)} %get-tuple-element.294) | copy-start | bytes 6291460
  340.2 26.2 copy-start.13
  415.4 331.2 %copy-start.21 = (bf16[256,2048]{1,0:T(8,128)(2,1)}, bf16[256,2048]{1,0:T(8,128)(2,1)S(1)}, u32[]{:S(2)}) copy-start(bf16[256,2048]{1,0:T(8,128)(2,1)S(1)} %multiply_convert_fusion.2) | copy-start | bytes 3145732
  559.1 390.0 %copy-start.29 = (bf16[256,2048]{1,0:T(8,128)(2,1)S(1)}, bf16[256,2048]{1,0:T(8,128)(2,1)}, u32[]{:S(2)}) copy-start(bf16[256,2048]{1,0:T(8,128)(2,1)} %param.20) | copy-start | bytes 3145732
  993.5 1084.1 %reduce-scatter.6.cloned.1.call-start = ((), (), s32[]{:S(2)}) async-start(), calls=%async_computation.10 | async-start | bytes 75497472 | tf_op jit(solution)/shard_map/reduce_scatter | solution.py:68
  1051.6 273.9 %copy-start = (f32[256,2048]{1,0:T(8,128)}, f32[256,2048]{1,0:T(8,128)S(1)}, u32[]{:S(2)}) copy-start(f32[256,2048]{1,0:T(8,128)S(1)} %fusion.23) | copy-start | bytes 6291460
  1277.6 47.9 %copy-start.35 = (bf16[256,2048]{1,0:T(8,128)(2,1)S(1)}, bf16[256,2048]{1,0:T(8,128)(2,1)}, u32[]{:S(2)}) copy-start(bf16[256,2048]{1,0:T(8,128)(2,1)} %get-tuple-element.364) | copy-start | bytes 3145732
  1404.9 1549.7 %reduce-scatter.10.cloned.1.call-start = ((), (), s32[]{:S(2)}) async-start(), calls=%async_computation.12 | async-start | bytes 103809024
  1440.4 1971.3 %all-reduce.71.cloned.1.call-start = ((), (), s32[]{:S(2)}) async-start(), calls=%async_computation.13 | async-start | bytes 51380224 | tf_op jit(solution)/shard_map/psum | solution.py:182
  2967.7 43.4 %copy-start.83 = (f32[256]{0:T(256)S(1)}, f32[256]{0:T(256)}, u32[]{:S(2)}) copy-start(f32[256]{0:T(256)} %copy-done.82) | copy-start | bytes 3076
  2967.8 43.4 %copy-start.1 = (f32[256,2048]{1,0:T(8,128)S(1)}, f32[256,2048]{1,0:T(8,128)}, u32[]{:S(2)}) copy-start(f32[256,2048]{1,0:T(8,128)} %copy-done) | copy-start | bytes 6291460
  (82 other events, 547.2 us)
Sparse Core Ops, SparseCore 0:
  9.6 84.7 all-gather.11
  96.0 80.5 all-gather.13
  178.2 80.6 all-gather.15
  260.3 80.5 all-gather.17
  342.4 201.6 all-gather.19
  545.7 200.8 all-gather.21
  748.2 200.8 all-gather.23
  993.7 442.9 reduce-scatter.7
  1439.2 638.4 reduce-scatter.5
  2079.9 874.6 reduce-scatter.9
  2959.0 452.6 all-reduce.70
where the time goes:
time: 3460 us; the launch traced here: 3440 us
  waiting for transfers between devices  2560 us (74%)
  local copies, waits for them, and re-layouts  381 us (11%)
  matrix products  235 us (7%)
  other arithmetic  142 us (4%)
  blocking collectives  101 us (3%)
    unnamed x12, waiting for transfers between devices  881 us
    reduce_scatter x2, waiting for transfers between devices, reduce_rows(): lax.psum_scatter(jnp.concatenate(blocks, axis=1), 'seq', scatter_dimensio...  637 us
    psum x1, waiting for transfers between devices, on_device(): lax.psum((mixer_sum, expand_sum, reduce_sum), 'grp')  384 us
    all_gather x1, waiting for transfers between devices, on_device(): lax.all_gather(local_weights[6], 'seq', axis=0, tiled=True)  188 us
    all_gather x1, waiting for transfers between devices, on_device(): lax.all_gather(local_weights[5], 'seq', axis=0, tiled=True)  187 us
    slice x57, local copies, waits for them, and re-layouts, on_device(): lax.associative_scan(carry_join, (decay_next, grad_direct), reverse=True,...  129 us
    all_gather x1, waiting for transfers between devices, on_device(): lax.all_gather(local_weights[4], 'seq', axis=0, tiled=True)  129 us
    slice x52, local copies, waits for them, and re-layouts, on_device(): lax.associative_scan(carry_join, (decay, income), axis=0)  97.2 us
  transfers between devices with their start and end apart: 11, of which 8 were waited for; matrix products, arithmetic and copies ran while one was open for 20% of the time, Pallas kernels for 0%

commit v1 on v0

v1 whole, which is shorter than its diff:
```python
from functools import partial

import jax
import jax.numpy as jnp
from jax import lax
from jax.experimental import pallas as pl
from jax.experimental.pallas import tpu as pltpu
from jax.sharding import PartitionSpec as P

LOWER = 0.9
EPSILON = 1e-06
GRP = 4
LANE = 128
ROWS = 8
F32 = jnp.float32
BF16 = jnp.bfloat16
SWAP_X = [(0, 1), (1, 0), (2, 3), (3, 2)]
SWAP_Y = [(0, 2), (2, 0), (1, 3), (3, 1)]
SLOT = ((0, 1), (4, 3), (2, 6), (5, 7))
VMEM_LIMIT = 56 * 1024 * 1024


def matmul(lhs_arr, rhs_arr, out=F32):
    return jnp.dot(lhs_arr, rhs_arr, preferred_element_type=F32).astype(out)


def matmul_back(lhs_arr, rhs_arr, out=F32):
    return lax.dot_general(
        lhs_arr, rhs_arr, (((1,), (1,)), ((), ())), preferred_element_type=F32
    ).astype(out)


def outer_sum(lhs_arr, rhs_arr, out=BF16):
    return lax.dot_general(
        lhs_arr, rhs_arr, (((0,), (0,)), ((), ())), preferred_element_type=F32
    ).astype(out)


def rms_parts(values):
    return lax.rsqrt(jnp.mean(values * values, axis=1, keepdims=True) + EPSILON)


def rms_back(values, scale, weights, grad):
    weighted = values * grad
    inner = jnp.mean(weighted * weights, axis=1, keepdims=True)
    return scale * weights * grad - values * (scale * scale * scale * inner), jnp.sum(
        weighted * scale, axis=0
    )


def exchange(own):
    half = own.shape[0] // 2
    top, low = own[:half], own[half:]
    from_x = lax.ppermute(top, "grp", SWAP_X)
    from_y = lax.ppermute(low, "grp", SWAP_Y)
    tops = lax.ppermute(jnp.concatenate([top, from_x]), "grp", SWAP_Y)
    lows = lax.ppermute(jnp.concatenate([low, from_y]), "grp", SWAP_X)
    return top, low, from_x, from_y, tops[:half], tops[half:], lows[:half], lows[half:]


def gather_rows(own):
    top, low, from_x, from_y, y_top, across_top, x_low, across_low = exchange(own)
    return jnp.concatenate([top, low, y_top, x_low, from_x, across_top, from_y, across_low])


def gather_blocks(own):
    top, low, from_x, from_y, y_top, across_top, x_low, across_low = exchange(own)
    return jnp.concatenate(
        [top, low, from_x, x_low, y_top, from_y, across_top, across_low]
    ).reshape((GRP,) + own.shape)


def scatter_rows(multiply, rows):
    quarter = rows.shape[0] // 8
    to_x = multiply(rows[4 * quarter : 6 * quarter])
    to_y = multiply(rows[6 * quarter :])
    by_x = lax.ppermute(to_x.astype(BF16), "grp", SWAP_X)
    by_y = lax.ppermute(to_y.astype(BF16), "grp", SWAP_Y)
    kept = multiply(rows[: 4 * quarter])
    for_y = (kept[2 * quarter : 3 * quarter] + by_x[quarter:].astype(F32)).astype(BF16)
    for_x = (kept[3 * quarter :] + by_y[quarter:].astype(F32)).astype(BF16)
    last_y = lax.ppermute(for_y, "grp", SWAP_Y)
    last_x = lax.ppermute(for_x, "grp", SWAP_X)
    top = kept[:quarter] + by_x[:quarter].astype(F32) + last_y.astype(F32)
    low = kept[quarter : 2 * quarter] + by_y[:quarter].astype(F32) + last_x.astype(F32)
    return jnp.concatenate([top, low])


def by_relation(values, mine):
    values = jnp.where(mine % 2 == 1, values[jnp.array([1, 0, 3, 2])], values)
    return jnp.where(mine // 2 == 1, values[jnp.array([2, 3, 0, 1])], values)


def pick_columns(mine, matrices, parts, spread):
    rows, wide = matrices[0].shape
    piece = wide // (GRP * parts)
    own = wide // GRP
    count = len(matrices)
    step = min(rows, 64)

    def body(mine_ref, *refs):
        out_ref = refs[-1]
        for index, ref in enumerate(refs[:-1]):
            for which in range(GRP):

                @pl.when(mine_ref[0] == which)
                def _(index=index, ref=ref, which=which):
                    whole = ref[...].astype(F32)
                    picked = jnp.concatenate(
                        [
                            whole[:, (part * GRP + which) * piece : (part * GRP + which + 1) * piece]
                            for part in range(parts)
                        ],
                        axis=1,
                    ).astype(BF16)
                    if not spread:
                        out_ref[:, index * own : (index + 1) * own] = picked
                    else:
                        for turn in range(own // LANE):
                            at = (turn * count + index) * LANE
                            out_ref[:, at : at + LANE] = picked[:, turn * LANE : (turn + 1) * LANE]

    return pl.pallas_call(
        body,
        grid=(rows // step,),
        in_specs=[pl.BlockSpec(memory_space=pltpu.SMEM)]
        + [pl.BlockSpec((step, wide), lambda i: (i, 0))] * count,
        out_specs=pl.BlockSpec((step, own * count), lambda i: (i, 0)),
        out_shape=jax.ShapeDtypeStruct((rows, own * count), BF16),
        compiler_params=pltpu.CompilerParams(vmem_limit_bytes=VMEM_LIMIT),
        name="pick_columns",
    )(mine.reshape(1), *matrices)


def place_columns(mine, blocks, parts, count, spread):
    _, rows, wide = blocks.shape
    own = wide // count
    piece = own // parts
    step = min(rows, 32)

    def body(mine_ref, blocks_ref, *out_refs):
        for which in range(GRP):
            block = blocks_ref[mine_ref[0] ^ which].astype(F32)
            for index, out_ref in enumerate(out_refs):
                if spread:
                    turns = [
                        block[:, (turn * count + index) * LANE : (turn * count + index + 1) * LANE]
                        for turn in range(own // LANE)
                    ]
                    mat = jnp.concatenate(turns, axis=1)
                else:
                    mat = block[:, index * own : (index + 1) * own]
                for part in range(parts):
                    at = (part * GRP + which) * piece
                    out_ref[:, at : at + piece] = mat[:, part * piece : (part + 1) * piece]

    return pl.pallas_call(
        body,
        grid=(rows // step,),
        in_specs=[
            pl.BlockSpec(memory_space=pltpu.SMEM),
            pl.BlockSpec((GRP, step, wide), lambda i: (0, i, 0)),
        ],
        out_specs=[pl.BlockSpec((step, own * GRP), lambda i: (i, 0))] * count,
        out_shape=[jax.ShapeDtypeStruct((rows, own * GRP), F32)] * count,
        compiler_params=pltpu.CompilerParams(vmem_limit_bytes=VMEM_LIMIT),
        name="place_columns",
    )(mine.reshape(1), blocks)


def keep_rows(info_ref, owner, first, count):
    place = info_ref[0] + first + lax.broadcasted_iota(jnp.int32, (count, LANE), 0)
    keep = jnp.ones((count, LANE), F32)
    for one in range(GRP):
        keep = jnp.where(place == info_ref[2 + owner * GRP + one], 0.0, keep)
    return keep


def scan_forward(info, proj, bias):
    _, half, wide = proj.shape
    own = wide // 3
    tiles = half // ROWS

    def body(info_ref, proj_ref, bias_ref, prod_ref, state_ref, ends_ref):
        row = lax.broadcasted_iota(jnp.int32, (ROWS, LANE), 0)
        bias_row = bias_ref[...]

        def tile(part, step, carry):
            out = []
            for owner in range(GRP):
                slot = SLOT[owner][part]
                at = pl.ds(pl.multiple_of(step * ROWS, ROWS), ROWS)
                both = proj_ref[slot, at, : 2 * LANE]
                enter = both[:, :LANE]
                forget = LOWER + (1.0 - LOWER) * jax.nn.sigmoid(both[:, LANE:] + bias_row)
                decay = forget * keep_rows(info_ref, owner, part * half + step * ROWS, ROWS)
                income = enter * jax.nn.sigmoid(enter) * (1.0 - forget)
                for shift in (1, 2, 4):
                    fits = row >= shift
                    before = jnp.where(fits, pltpu.roll(income, shift, 0), 0.0)
                    factor = jnp.where(fits, pltpu.roll(decay, shift, 0), 1.0)
                    income = income + decay * before
                    decay = decay * factor
                prod, state = carry[owner]
                state_now = income + decay * state
                prod_now = decay * prod
                prod_ref[slot, at, :] = prod_now
                state_ref[slot, at, :] = state_now
                out.append((prod_now[ROWS - 1 :], state_now[ROWS - 1 :]))
            return tuple(out)

        carry = tuple(
            (jnp.ones((1, LANE), F32), jnp.zeros((1, LANE), F32)) for owner in range(GRP)
        )
        for part in range(2):
            carry = lax.fori_loop(0, tiles, partial(tile, part), carry)
        for owner in range(GRP):
            ends_ref[owner : owner + 1, :] = carry[owner][0]
            ends_ref[GRP + owner : GRP + owner + 1, :] = carry[owner][1]

    block = pl.BlockSpec((8, half, LANE), lambda j: (0, 0, j))
    return pl.pallas_call(
        body,
        grid=(own // LANE,),
        in_specs=[
            pl.BlockSpec(memory_space=pltpu.SMEM),
            pl.BlockSpec((8, half, 3 * LANE), lambda j: (0, 0, j)),
            pl.BlockSpec((1, LANE), lambda j: (0, j)),
        ],
        out_specs=[block, block, pl.BlockSpec((2 * GRP, LANE), lambda j: (0, j))],
        out_shape=[
            jax.ShapeDtypeStruct((8, half, own), F32),
            jax.ShapeDtypeStruct((8, half, own), F32),
            jax.ShapeDtypeStruct((2 * GRP, own), F32),
        ],
        compiler_params=pltpu.CompilerParams(vmem_limit_bytes=VMEM_LIMIT),
        name="scan_forward",
    )(info, proj, bias)


def entering_state(info_ref, ends_ref, count, backward):
    state = jnp.zeros((GRP, LANE), F32)
    order = range(count - 1, 0, -1) if backward else range(count - 1)
    for place in order:
        longer = ends_ref[place, GRP:, :] + ends_ref[place, :GRP, :] * state
        reached = place > info_ref[1] if backward else place < info_ref[1]
        state = jnp.where(reached, longer, state)
    return state


def finish_forward(info, ends, prod, state, proj, gain):
    _, half, own = prod.shape
    count = ends.shape[0]

    def body(info_ref, ends_ref, prod_ref, state_ref, proj_ref, gain_ref, states_ref, mix_ref, squares_ref, enter_ref):
        entering = entering_state(info_ref, ends_ref, count, False)
        enter_ref[...] = entering

        @pl.when(pl.program_id(0) == 0)
        def _():
            squares_ref[...] = jnp.zeros_like(squares_ref)

        for owner in range(GRP):
            for part in range(2):
                slot = SLOT[owner][part]
                states = state_ref[slot] + prod_ref[slot] * entering[owner : owner + 1]
                states_ref[slot] = states
                gate = proj_ref[slot]
                mix_ref[slot] = (states * gain_ref[...] * (gate * jax.nn.sigmoid(gate))).astype(BF16)
                squares_ref[slot] += jnp.sum(states * states, axis=1, keepdims=True)

    block = pl.BlockSpec((8, half, LANE), lambda j: (0, 0, j))
    return pl.pallas_call(
        body,
        grid=(own // LANE,),
        in_specs=[
            pl.BlockSpec(memory_space=pltpu.SMEM),
            pl.BlockSpec((count, 2 * GRP, LANE), lambda j: (0, 0, j)),
            block,
            block,
            pl.BlockSpec((8, half, LANE), lambda j: (0, 0, 3 * j + 2)),
            pl.BlockSpec((1, LANE), lambda j: (0, j)),
        ],
        out_specs=[
            block,
            block,
            pl.BlockSpec((8, half, 1), lambda j: (0, 0, 0)),
            pl.BlockSpec((GRP, LANE), lambda j: (0, j)),
        ],
        out_shape=[
            jax.ShapeDtypeStruct((8, half, own), F32),
            jax.ShapeDtypeStruct((8, half, own), BF16),
            jax.ShapeDtypeStruct((8, half, 1), F32),
            jax.ShapeDtypeStruct((GRP, own), F32),
        ],
        compiler_params=pltpu.CompilerParams(vmem_limit_bytes=VMEM_LIMIT),
        name="finish_forward",
    )(info, ends, prod, state, proj, gain)


def scan_backward(info, proj, bias, gain, states, back, coupling):
    _, half, wide = proj.shape
    own = wide // 3
    tiles = half // ROWS

    def body(info_ref, proj_ref, bias_ref, gain_ref, states_ref, back_ref, coupling_ref, prod_ref, grad_ref, ends_ref):
        row = lax.broadcasted_iota(jnp.int32, (ROWS, LANE), 0)
        bias_row = bias_ref[...]
        gain_row = gain_ref[...]

        def tile(part, turn, carry):
            step = tiles - 1 - turn
            out = []
            for owner in range(GRP):
                slot = SLOT[owner][part]
                at = pl.ds(pl.multiple_of(step * ROWS, ROWS), ROWS)
                both = proj_ref[slot, at, LANE:]
                gate = both[:, LANE:]
                forget = LOWER + (1.0 - LOWER) * jax.nn.sigmoid(both[:, :LANE] + bias_row)
                decay = forget * keep_rows(info_ref, owner, part * half + step * ROWS, ROWS)
                direct = (
                    gain_row * (gate * jax.nn.sigmoid(gate)) * back_ref[slot, at, :]
                    - states_ref[slot, at, :] * coupling_ref[slot, at, :]
                )
                flow = decay * direct
                for shift in (1, 2, 4):
                    fits = row < ROWS - shift
                    after = jnp.where(fits, pltpu.roll(flow, ROWS - shift, 0), 0.0)
                    factor = jnp.where(fits, pltpu.roll(decay, ROWS - shift, 0), 1.0)
                    flow = flow + decay * after
                    decay = decay * factor
                prod, grad = carry[owner]
                flow = flow + decay * grad
                decay = decay * prod
                last = row == ROWS - 1
                grad_ref[slot, at, :] = direct + jnp.where(last, grad, pltpu.roll(flow, ROWS - 1, 0))
                prod_ref[slot, at, :] = jnp.where(last, prod, pltpu.roll(decay, ROWS - 1, 0))
                out.append((decay[:1], flow[:1]))
            return tuple(out)

        carry = tuple(
            (jnp.ones((1, LANE), F32), jnp.zeros((1, LANE), F32)) for owner in range(GRP)
        )
        for part in (1, 0):
            carry = lax.fori_loop(0, tiles, partial(tile, part), carry)
        for owner in range(GRP):
            ends_ref[owner : owner + 1, :] = carry[owner][0]
            ends_ref[GRP + owner : GRP + owner + 1, :] = carry[owner][1]

    block = pl.BlockSpec((8, half, LANE), lambda j: (0, 0, j))
    vector = pl.BlockSpec((1, LANE), lambda j: (0, j))
    return pl.pallas_call(
        body,
        grid=(own // LANE,),
        in_specs=[
            pl.BlockSpec(memory_space=pltpu.SMEM),
            pl.BlockSpec((8, half, 3 * LANE), lambda j: (0, 0, j)),
            vector,
            vector,
            block,
            block,
            pl.BlockSpec((8, half, 1), lambda j: (0, 0, 0)),
        ],
        out_specs=[block, block, pl.BlockSpec((2 * GRP, LANE), lambda j: (0, j))],
        out_shape=[
            jax.ShapeDtypeStruct((8, half, own), F32),
            jax.ShapeDtypeStruct((8, half, own), F32),
            jax.ShapeDtypeStruct((2 * GRP, own), F32),
        ],
        compiler_params=pltpu.CompilerParams(vmem_limit_bytes=VMEM_LIMIT),
        name="scan_backward",
    )(info, proj, bias, gain, states, back, coupling)


def finish_backward(info, ends, prod, grad, proj, bias, gain, states, enter, back):
    _, half, own = prod.shape
    count = ends.shape[0]

    def body(info_ref, ends_ref, prod_ref, grad_ref, proj_ref, bias_ref, gain_ref, states_ref, enter_ref, back_ref, out_ref, sums_ref):
        entering = entering_state(info_ref, ends_ref, count, True)
        first = lax.broadcasted_iota(jnp.int32, (half, LANE), 0) == 0
        bias_sum = jnp.zeros((1, LANE), F32)
        gain_sum = jnp.zeros((1, LANE), F32)
        for owner in range(GRP):
            before = enter_ref[owner : owner + 1, :]
            for part in range(2):
                slot = SLOT[owner][part]
                states = states_ref[slot]
                previous = jnp.where(first, before, pltpu.roll(states, 1, 0))
                before = states[half - 1 :]
                total = grad_ref[slot] + prod_ref[slot] * entering[owner : owner + 1]
                enter = proj_ref[slot, :, :LANE]
                gate = proj_ref[slot, :, 2 * LANE :]
                sig = jax.nn.sigmoid(proj_ref[slot, :, LANE : 2 * LANE] + bias_ref[...])
                enter_sig = jax.nn.sigmoid(enter)
                gate_sig = jax.nn.sigmoid(gate)
                keep = keep_rows(info_ref, owner, part * half, half)
                grad_forget = total * (previous * keep - enter * enter_sig)
                grad_proj = grad_forget * ((1.0 - LOWER) * sig * (1.0 - sig))
                forget = LOWER + (1.0 - LOWER) * sig
                pull = back_ref[slot] * states
                out_ref[slot, :, :LANE] = (
                    total * (1.0 - forget) * (enter_sig * (1.0 + enter * (1.0 - enter_sig)))
                ).astype(BF16)
                out_ref[slot, :, LANE : 2 * LANE] = grad_proj.astype(BF16)
                out_ref[slot, :, 2 * LANE :] = (
                    pull * gain_ref[...] * (gate_sig * (1.0 + gate * (1.0 - gate_sig)))
                ).astype(BF16)
                bias_sum = bias_sum + jnp.sum(grad_proj, axis=0, keepdims=True)
                gain_sum = gain_sum + jnp.sum(pull * (gate * gate_sig), axis=0, keepdims=True)
        sums_ref[0:1, :] = bias_sum
        sums_ref[1:2, :] = gain_sum

    block = pl.BlockSpec((8, half, LANE), lambda j: (0, 0, j))
    wide = pl.BlockSpec((8, half, 3 * LANE), lambda j: (0, 0, j))
    vector = pl.BlockSpec((1, LANE), lambda j: (0, j))
    return pl.pallas_call(
        body,
        grid=(own // LANE,),
        in_specs=[
            pl.BlockSpec(memory_space=pltpu.SMEM),
            pl.BlockSpec((count, 2 * GRP, LANE), lambda j: (0, 0, j)),
            block,
            block,
            wide,
            vector,
            vector,
            block,
            pl.BlockSpec((GRP, LANE), lambda j: (0, j)),
            block,
        ],
        out_specs=[wide, pl.BlockSpec((2, LANE), lambda j: (0, j))],
        out_shape=[
            jax.ShapeDtypeStruct((8, half, 3 * own), BF16),
            jax.ShapeDtypeStruct((2, own), F32),
        ],
        compiler_params=pltpu.CompilerParams(vmem_limit_bytes=VMEM_LIMIT),
        name="finish_backward",
    )(info, ends, prod, grad, proj, bias, gain, states, enter, back)


def on_device(
    tokens,
    seq_lengths,
    cotangent,
    norm_gain,
    input_proj,
    forget_proj,
    forget_bias,
    gate_proj,
    state_gain,
    out_proj,
    mlp_gain,
    mlp_gate,
    mlp_up,
    mlp_down,
):
    tok_rows, width = tokens.shape
    half = tok_rows // 2
    parts = lax.axis_size("seq")
    mine, place = lax.axis_index("grp"), lax.axis_index("seq")
    own = width // GRP
    ff_own = mlp_gate.shape[1] // GRP

    def own_rows(matrix):
        count = matrix.shape[0] // GRP
        return lax.dynamic_slice_in_dim(matrix, mine * count, count, 0)

    def own_features(vector):
        cut = vector.reshape(parts, GRP, -1)
        return lax.dynamic_index_in_dim(cut, mine, 1, False).reshape(1, -1)

    def all_features(vector):
        cut = vector.reshape(parts, 1, -1)
        spread = jnp.where(jnp.arange(GRP)[None, :, None] == mine, cut, 0.0)
        return spread.reshape(-1)

    def whole(rows):
        return lax.all_gather(rows, "seq", axis=0, tiled=True)

    def reduced(grads):
        return lax.psum_scatter(grads, "seq", scatter_dimension=0, tiled=True)

    w_proj = whole(pick_columns(mine, (input_proj, forget_proj, gate_proj), parts, True))
    w_out = whole(own_rows(out_proj))
    w_ff = whole(pick_columns(mine, (mlp_gate, mlp_up), parts, False))
    w_down = whole(own_rows(mlp_down))

    lengths = lax.all_gather(seq_lengths, "grp", axis=0, tiled=True)
    starts = by_relation(jnp.cumsum(lengths, axis=1) - lengths, mine)
    info = jnp.concatenate([jnp.stack([place * tok_rows, place]), starts.reshape(-1)]).astype(jnp.int32)
    bias = own_features(forget_bias)
    gain = own_features(state_gain)

    inputs = tokens.astype(F32)
    scale_in = rms_parts(inputs)
    normed = gather_rows((inputs * scale_in * norm_gain).astype(BF16))
    cot = gather_rows(cotangent)

    proj = matmul(normed, w_proj).reshape(8, half, 3 * own)
    prod, state, ends = scan_forward(info, proj, bias)
    ends = lax.all_gather(ends, "seq")
    states, mix, squares, enter = finish_forward(info, ends, prod, state, proj, gain)
    mix = mix.reshape(GRP * tok_rows, own)
    squares = jnp.stack(
        [jnp.concatenate([squares[SLOT[k][0], :, 0], squares[SLOT[k][1], :, 0]]) for k in range(GRP)]
    )
    squares = lax.psum(by_relation(squares, mine), "grp")
    squares = lax.dynamic_index_in_dim(squares, mine, 0, False)
    scale_state = lax.rsqrt(squares / width + EPSILON)[:, None]

    raw = scatter_rows(partial(matmul, rhs_arr=w_out), mix)
    middle = inputs + raw * scale_state
    scale_mid = rms_parts(middle)
    normed_mid = gather_rows((middle * scale_mid * mlp_gain).astype(BF16))

    gate_vals = matmul(normed_mid, w_ff[:, :ff_own])
    up_vals = matmul(normed_mid, w_ff[:, ff_own:])
    gate_sig = jax.nn.sigmoid(gate_vals)
    gate_act = gate_vals * gate_sig
    hidden = (gate_act * up_vals).astype(BF16)
    block_out = (middle + scatter_rows(partial(matmul, rhs_arr=w_down), hidden)).astype(BF16)
    sum_down = reduced(outer_sum(hidden, cot))

    grad_hidden = matmul_back(cot, w_down)
    grad_gate = grad_hidden * up_vals * (gate_sig * (1.0 + gate_vals * (1.0 - gate_sig)))
    grad_up = grad_hidden * gate_act
    grad_ff = jnp.concatenate([grad_gate.astype(BF16), grad_up.astype(BF16)], axis=1)
    grad_normed_mid = scatter_rows(partial(matmul_back, rhs_arr=w_ff), grad_ff)
    sum_ff = reduced(outer_sum(normed_mid, grad_ff))

    back_mid, grad_mlp_gain = rms_back(middle, scale_mid, mlp_gain, grad_normed_mid)
    grad_middle = cotangent.astype(F32) + back_mid
    scaled_mix = (grad_middle * scale_state).astype(BF16)
    coupling = (
        scale_state[:, 0] * scale_state[:, 0] * scale_state[:, 0] * jnp.mean(raw * grad_middle, axis=1)
    )
    grad_mix = gather_rows(scaled_mix)
    coupling = by_relation(lax.all_gather(coupling, "grp"), mine).reshape(GRP, 2, half)
    order = [(k, h) for slot in range(8) for k in range(GRP) for h in range(2) if SLOT[k][h] == slot]
    coupling = jnp.stack([coupling[k, h] for k, h in order])[:, :, None]

    back = matmul_back(grad_mix, w_out).reshape(8, half, own)
    sum_out = reduced(outer_sum(mix, grad_mix))
    after, local, ends_back = scan_backward(info, proj, bias, gain, states, back, coupling)
    ends_back = lax.all_gather(ends_back, "seq")
    grad_proj, sums = finish_backward(
        info, ends_back, after, local, proj, bias, gain, states, enter, back
    )
    grad_proj = grad_proj.reshape(GRP * tok_rows, 3 * own)
    grad_normed = scatter_rows(partial(matmul_back, rhs_arr=w_proj), grad_proj)
    sum_proj = reduced(outer_sum(normed, grad_proj))
    back_in, grad_norm_gain = rms_back(inputs, scale_in, norm_gain, grad_normed)
    grad_tokens = grad_middle + back_in

    vectors = jnp.stack([grad_norm_gain, all_features(sums[0]), all_features(sums[1]), grad_mlp_gain])
    vectors = lax.psum(vectors, ("grp", "seq"))

    def whole_rows(summed):
        blocks = by_relation(gather_blocks(summed), mine)
        return blocks.reshape(-1, summed.shape[1]).astype(F32)

    grad_down = whole_rows(sum_down)
    grad_out = whole_rows(sum_out)
    grad_mlp_gate, grad_mlp_up = place_columns(mine, gather_blocks(sum_ff), parts, 2, False)
    grad_input, grad_forget, grad_gate_proj = place_columns(
        mine, gather_blocks(sum_proj), parts, 3, True
    )
    return (
        block_out,
        grad_tokens,
        vectors[0],
        grad_input,
        grad_forget,
        vectors[1],
        grad_gate_proj,
        vectors[2],
        grad_out,
        vectors[3],
        grad_mlp_gate,
        grad_mlp_up,
        grad_down,
    )


def solution(mesh):
    rows = P("seq", None)
    tokens = P(("grp", "seq"), None)
    return jax.shard_map(
        on_device,
        mesh=mesh,
        in_specs=(
            tokens,
            P("grp", None),
            tokens,
            P(),
            rows,
            rows,
            P(),
            rows,
            P(),
            rows,
            P(),
            rows,
            rows,
            rows,
        ),
        out_specs=(
            tokens,
            tokens,
            P(),
            rows,
            rows,
            P(),
            rows,
            P(),
            rows,
            P(),
            rows,
            rows,
            rows,
        ),
        check_vma=False,
    )
```

time: 3460 us -> 827 us (0.24)
  waiting for transfers between devices: 2560 us -> 285 us
  local copies, waits for them, and re-layouts: 381 us -> 76.4 us
  other arithmetic: 142 us -> 45.2 us
  matrix products: 235 us -> 156 us
  Pallas kernels: 0 us -> 63.8 us
  starting transfers between devices: 0.6 us -> 54 us
    unnamed x12 -> x8, waiting for transfers between devices: 881 us -> 0.13 us
    all_gather x7 -> x4, waiting for transfers between devices: 661 us -> 4.1 us  [whole(): return lax.all_gather(rows, 'seq', axis=0, tiled=True)]
    reduce_scatter x2 -> x4, waiting for transfers between devices: 637 us -> 3.68 us  [reduced(): return lax.psum_scatter(grads, 'seq', scatter_dimension=0, tiled=True)]
    psum x1 -> x0, waiting for transfers between devices: 384 us -> none  [on_device(): lax.psum((mixer_sum, expand_sum, reduce_sum), 'grp')]
    ppermute x0 -> x48, waiting for transfers between devices: none -> 277 us  [the longest x8 53.4 us: exchange(): tops = lax.ppermute(jnp.concatenate([top, from_x]), 'grp', SWAP_Y)]
    slice x112 -> x15, local copies, waits for them, and re-layouts: 244 us -> 11.5 us  [the longest x8 7.91 us: exchange(): top, low = (own[:half], own[half:])]
    pad x56 -> x0, local copies, waits for them, and re-layouts: 89.9 us -> none  [the longest x28 47.9 us: on_device(): lax.associative_scan(carry_join, (decay_next, grad_direct), reverse=True,...]
    pallas_call x0 -> x8, Pallas kernels: none -> 63.8 us  [the longest x2 17 us: place_columns(): pl.pallas_call(body, grid=(rows // step,), in_specs=[pl.BlockSpec(memory_...]
  transfers between devices with their start and end apart: 11 -> 56, of which waited for: 8 -> 34; matrix products, arithmetic and copies ran while one was open for 20% -> 29% of each run, Pallas kernels for 0% -> 6%
where the time goes in v1:
time: 827 us; the launch traced here: 814 us
  waiting for transfers between devices  285 us (34%)
  matrix products  156 us (19%)
  blocking collectives  119 us (14%)
  local copies, waits for them, and re-layouts  76.4 us (9%)
  Pallas kernels  63.8 us (8%)
  starting transfers between devices  54 us (7%)
  other arithmetic  45.2 us (5%)
  between operations  15.5 us (2%)
    dot_general x8, matrix products, matmul_back(): lax.dot_general(lhs_arr, rhs_arr, (((1,), (1,)), ((), ())), preferred_ele...  63.6 us
    ppermute x8, waiting for transfers between devices, exchange(): tops = lax.ppermute(jnp.concatenate([top, from_x]), 'grp', SWAP_Y)  53.4 us
    ppermute x4, waiting for transfers between devices, scatter_rows(): last_y = lax.ppermute(for_y, 'grp', SWAP_Y)  50.1 us
    ppermute x8, waiting for transfers between devices, exchange(): lows = lax.ppermute(jnp.concatenate([low, from_y]), 'grp', SWAP_X)  49.9 us
    ppermute x4, waiting for transfers between devices, scatter_rows(): by_x = lax.ppermute(to_x.astype(BF16), 'grp', SWAP_X)  48 us
    dot_general x9, matrix products, matmul(): return jnp.dot(lhs_arr, rhs_arr, preferred_element_type=F32).astype(out)  47.9 us
    dot_general x4, matrix products, outer_sum(): lax.dot_general(lhs_arr, rhs_arr, (((0,), (0,)), ((), ())), preferred_ele...  44.4 us
    unnamed x142, local copies, waits for them, and re-layouts  40.7 us
  transfers between devices with their start and end apart: 56, of which 34 were waited for; matrix products, arithmetic and copies ran while one was open for 29% of the time, Pallas kernels for 6%

profile of v1, /device:TPU:0, one launch (start us, length us, event | category | flops | bytes accessed | tf_op | source)
XLA Modules:
  0.0 814.2 jit_solution(9493744345565133872)
XLA Ops:
  31.5 22.6 %all-gather.2 = s32[4,1,4]{2,1,0:T(1,128)S(1)} all-gather(s32[1,1,4]{2,1,0:T(1,128)S(1)} %bitcast.151), channel_id=1, replica_groups=mesh['grp'=4,'seq'=8] {'grp'}, dimensions={0}, use_global_device_ids=true | all-gather | bytes 80 | tf_op jit(solution)/shard_map/all_gather | solution.py:489
  70.0 14.6 %collective-permute-done.1 = bf16[256,2048]{1,0:T(8,128)(2,1)S(1)} collective-permute-done((bf16[256,2048]{1,0:T(8,128)(2,1)S(1)}, bf16[256,2048]{1,0:T(8,128)(2,1)S(1)}, u32[]{:S(2)}, u32[]{:S(2)}) %collective-permute-start.1) | collective-permute-done | bytes 1048608 | tf_op jit(solution)/shard_map/ppermute | solution.py:56
  95.0 11.8 %fusion.66 = f32[1024,1536]{1,0:T(8,128)} fusion(bf16[1024,2048]{1,0:T(8,128)(2,1)} %slice_dynamic-update-slice_fusion.16, bf16[2048,1536]{1,0:T(8,128)(2,1)} %all-gather.9.cloned.1.call-done), kind=kOutput, calls=%fused_computation.253 | convolution fusion | flops 6442450944 | bytes 16777216 | tf_op jit(solution)/shard_map/dot_general | solution.py:24
  114.9 18.3 %all-gather = f32[64,512]{1,0:T(8,128)} all-gather(f32[8,512]{1,0:T(8,128)} %get-tuple-element.30), channel_id=2, replica_groups=mesh['grp'=4,'seq'=8] {'seq'}, dimensions={0}, use_global_device_ids=true | all-gather | bytes 147456 | tf_op jit(solution)/shard_map/all_gather | solution.py:502
  149.0 18.8 %collective-permute-done.4 = bf16[256,2048]{1,0:T(8,128)(2,1)S(1)} collective-permute-done((bf16[256,2048]{1,0:T(8,128)(2,1)S(1)}, bf16[256,2048]{1,0:T(8,128)(2,1)S(1)}, u32[]{:S(2)}, u32[]{:S(2)}) %collective-permute-start.4) | collective-permute-done | bytes 1048608 | tf_op jit(solution)/shard_map/ppermute | solution.py:77
  173.9 10.2 %collective-permute-done.5 = bf16[128,2048]{1,0:T(8,128)(2,1)S(1)} collective-permute-done((bf16[128,2048]{1,0:T(8,128)(2,1)S(1)}, bf16[128,2048]{1,0:T(8,128)(2,1)S(1)}, u32[]{:S(2)}, u32[]{:S(2)}) %collective-permute-start.5) | collective-permute-done | bytes 524320 | tf_op jit(solution)/shard_map/ppermute | solution.py:82
  188.4 15.7 %psum.14 = f32[4,256]{1,0:T(4,128)S(1)} all-reduce(f32[4,256]{1,0:T(4,128)S(1)} %broadcast_select_fusion.7), channel_id=1, replica_groups=mesh['grp'=4,'seq'=8] {'grp'}, use_global_device_ids=true, to_apply=%region_2.3 | all-reduce | flops 1024 | bytes 8192 | tf_op jit(solution)/shard_map/psum | solution.py:508
  233.2 14.9 %collective-permute-done.9 = bf16[256,2048]{1,0:T(8,128)(2,1)S(1)} collective-permute-done((bf16[256,2048]{1,0:T(8,128)(2,1)S(1)}, bf16[256,2048]{1,0:T(8,128)(2,1)S(1)}, u32[]{:S(2)}, u32[]{:S(2)}) %collective-permute-start.9) | collective-permute-done | bytes 1048608 | tf_op jit(solution)/shard_map/ppermute | solution.py:56
  253.3 11.9 %fusion.2 = f32[1024,1408]{1,0:T(8,128)} fusion(bf16[1024,2048]{1,0:T(8,128)(2,1)} %slice_dynamic-update-slice_fusion.12, bf16[2048,2816]{1,0:T(8,128)(2,1)} %all-gather.13.cloned.1.call-done), kind=kOutput, calls=%fused_computation.22 | convolution fusion | flops 5905580032 | bytes 15728640 | tf_op jit(solution)/shard_map/dot_general | solution.py:24
  279.3 16.6 %multiply_convert_fusion = (bf16[1024,1408]{1,0:T(8,128)(2,1)}, bf16[1024,1408]{1,0:T(8,128)(2,1)}, bf16[1024,1408]{1,0:T(8,128)(2,1)}) fusion(f32[1024,1408]{1,0:T(8,128)} %fusion.2, f32[1024,1408]{1,0:T(8,128)} %fusion, bf16[1024,2048]{1,0:T(8,128)(2,1)} %slice_dynamic-update-slice_fusion.8, bf16[1408,2048]{1,0:T(8,128)(2,1)} %all-gather.15.cloned.1.call-done), kind=kOutput, calls=%fused_computation.24 | convolution fusion | flops 5927206912 | bytes 30146560 | tf_op jit(solution)/shard_map/dot_general | solution.py:28
  338.6 14.3 %collective-permute-done.12 = bf16[256,2048]{1,0:T(8,128)(2,1)S(1)} collective-permute-done((bf16[256,2048]{1,0:T(8,128)(2,1)S(1)}, bf16[256,2048]{1,0:T(8,128)(2,1)S(1)}, u32[]{:S(2)}, u32[]{:S(2)}) %collective-permute-start.12) | collective-permute-done | bytes 1048608 | tf_op jit(solution)/shard_map/ppermute | solution.py:77
  354.6 20.6 %collective-permute-done.21 = bf16[128,2048]{1,0:T(8,128)(2,1)S(1)} collective-permute-done((bf16[128,2048]{1,0:T(8,128)(2,1)S(1)}, bf16[128,2048]{1,0:T(8,128)(2,1)S(1)}, u32[]{:S(2)}, u32[]{:S(2)}) %collective-permute-start.21) | collective-permute-done | bytes 524320 | tf_op jit(solution)/shard_map/ppermute | solution.py:82
  388.6 10.4 %collective-permute-done.15 = bf16[128,2048]{1,0:T(8,128)(2,1)S(1)} collective-permute-done((bf16[128,2048]{1,0:T(8,128)(2,1)S(1)}, bf16[128,2048]{1,0:T(8,128)(2,1)S(1)}, u32[]{:S(2)}, u32[]{:S(2)}) %collective-permute-start.15) | collective-permute-done | bytes 524320 | tf_op jit(solution)/shard_map/ppermute | solution.py:83
  404.2 10.3 %collective-permute-done.24 = bf16[128,2048]{1,0:T(8,128)(2,1)S(1)} collective-permute-done((bf16[128,2048]{1,0:T(8,128)(2,1)S(1)}, bf16[128,2048]{1,0:T(8,128)(2,1)S(1)}, u32[]{:S(2)}, u32[]{:S(2)}) %collective-permute-start.24) | collective-permute-done | bytes 524320 | tf_op jit(solution)/shard_map/ppermute | solution.py:54
  417.7 19.4 %collective-permute-done.25 = bf16[256,2048]{1,0:T(8,128)(2,1)S(1)} collective-permute-done((bf16[256,2048]{1,0:T(8,128)(2,1)S(1)}, bf16[256,2048]{1,0:T(8,128)(2,1)S(1)}, u32[]{:S(2)}, u32[]{:S(2)}) %collective-permute-start.25) | collective-permute-done | bytes 1048608 | tf_op jit(solution)/shard_map/ppermute | solution.py:56
  444.7 10.4 %convolution_convert_fusion.1 = bf16[1408,2048]{1,0:T(8,128)(2,1)} fusion(bf16[1024,1408]{1,0:T(8,128)(2,1)} %get-tuple-element.73, bf16[1024,2048]{1,0:T(8,128)(2,1)} %slice_dynamic-update-slice_fusion.8), kind=kOutput, calls=%fused_computation.18 | convolution fusion | flops 5908463616 | bytes 12845056 | tf_op jit(solution)/shard_map/dot_general | solution.py:34
  470.9 14.9 %scan_backward.1 = (f32[8,128,512]{2,1,0:T(8,128)}, f32[8,128,512]{2,1,0:T(8,128)}, f32[8,512]{1,0:T(8,128)}) custom-call(s32[18]{0:T(128)} %pad_add_fusion.info_ref, f32[8,128,1536]{2,1,0:T(8,128)} %bitcast.108, f32[1,512]{1,0:T(1,128)} %reshape.208.bias_ref, f32[1,512]{1,0:T(1,128)} %reshape.210.gain_ref, f32[8,128,512]{2,1,0:T(8,128)} %get-tuple-element.35.states_ref, ...), custom_call_target="tpu_custom_call" | custom-call | tf_op jit(solution)/shard_map/scan_backward/pallas_call | solution.py:352
  485.7 15.8 %all-gather.1 = f32[64,512]{1,0:T(8,128)} all-gather(f32[8,512]{1,0:T(8,128)} %get-tuple-element.36), channel_id=3, replica_groups=mesh['grp'=4,'seq'=8] {'seq'}, dimensions={0}, use_global_device_ids=true | all-gather | bytes 147456 | tf_op jit(solution)/shard_map/all_gather | solution.py:546
  510.6 11.6 %convolution_convert_fusion.2 = bf16[2048,1536]{1,0:T(8,128)(2,1)} fusion(bf16[1024,2048]{1,0:T(8,128)(2,1)} %slice_dynamic-update-slice_fusion.16, bf16[1024,1536]{1,0:T(8,128)(2,1)} %bitcast.116), kind=kOutput, calls=%fused_computation.19 | convolution fusion | flops 6445596672 | bytes 13631488 | tf_op jit(solution)/shard_map/dot_general | solution.py:34
  522.7 18.5 %convolution_convert_fusion = bf16[2048,2816]{1,0:T(8,128)(2,1)} fusion(bf16[1024,2048]{1,0:T(8,128)(2,1)} %slice_dynamic-update-slice_fusion.12, bf16[1024,1408]{1,0:T(8,128)(2,1)} %get-tuple-element.71, bf16[1024,1408]{1,0:T(8,128)(2,1)} %get-tuple-element.72), kind=kOutput, calls=%fused_computation.10 | convolution fusion | flops 11828461568 | bytes 21495808 | tf_op jit(solution)/shard_map/dot_general | solution.py:34
  558.1 14.9 %collective-permute-done.28 = bf16[256,2048]{1,0:T(8,128)(2,1)S(1)} collective-permute-done((bf16[256,2048]{1,0:T(8,128)(2,1)S(1)}, bf16[256,2048]{1,0:T(8,128)(2,1)S(1)}, u32[]{:S(2)}, u32[]{:S(2)}) %collective-permute-start.28) | collective-permute-done | bytes 1048608 | tf_op jit(solution)/shard_map/ppermute | solution.py:77
  591.8 12.0 %collective-permute-done.31 = bf16[128,2048]{1,0:T(8,128)(2,1)S(1)} collective-permute-done((bf16[128,2048]{1,0:T(8,128)(2,1)S(1)}, bf16[128,2048]{1,0:T(8,128)(2,1)S(1)}, u32[]{:S(2)}, u32[]{:S(2)}) %collective-permute-start.31) | collective-permute-done | bytes 524320 | tf_op jit(solution)/shard_map/ppermute | solution.py:83
  606.9 39.1 %psum.15 = f32[4,2048]{1,0:T(4,128)S(1)} all-reduce(f32[4,2048]{1,0:T(4,128)S(1)} %pad_maximum_fusion.21), channel_id=1, replica_groups=mesh['grp'=4,'seq'=8] {'grp','seq'}, use_global_device_ids=true, to_apply=%region_9.10 | all-reduce | flops 8192 | bytes 65536 | tf_op jit(solution)/shard_map/psum | solution.py:557
  767.5 22.7 %collective-permute-done.42 = bf16[256,2816]{1,0:T(8,128)(2,1)S(1)} collective-permute-done((bf16[256,2816]{1,0:T(8,128)(2,1)S(1)}, bf16[256,2816]{1,0:T(8,128)(2,1)S(1)}, u32[]{:S(2)}, u32[]{:S(2)}) %collective-permute-start.42) | collective-permute-done | bytes 1441824 | tf_op jit(solution)/shard_map/ppermute | solution.py:57
  (391 shorter events, 408.2 us)
Async XLA Ops:
  7.2 87.8 %all-gather.9.cloned.1.call-start = ((), (), s32[]{:S(2)}) async-start(), calls=%async_computation.4 | async-start | bytes 7077888 | tf_op jit(solution)/shard_map/all_gather | solution.py:479
  11.7 128.1 %all-gather.11.cloned.1.call-start = ((), (), s32[]{:S(2)}) async-start(), calls=%async_computation.5 | async-start | bytes 2359296 | tf_op jit(solution)/shard_map/all_gather | solution.py:479
  13.5 239.8 %all-gather.13.cloned.1.call-start = ((), (), s32[]{:S(2)}) async-start(), calls=%async_computation.6 | async-start | bytes 12976128 | tf_op jit(solution)/shard_map/all_gather | solution.py:479
  18.4 260.9 %all-gather.15.cloned.1.call-start = ((), (), s32[]{:S(2)}) async-start(), calls=%async_computation.7 | async-start | bytes 6488064 | tf_op jit(solution)/shard_map/all_gather | solution.py:479
  24.3 32.7 %collective-permute-start = (bf16[128,2048]{1,0:T(8,128)(2,1)}, bf16[128,2048]{1,0:T(8,128)(2,1)}, u32[]{:S(2)}, u32[]{:S(2)}) collective-permute-start(bf16[128,2048]{1,0:T(8,128)(2,1)} %get-tuple-element.96), channel_id=1, source_target_pairs={{0,8},{8,0},{16,24},{24,16},{1,9},{9,1},{17,25},{25,17},{2,10},{10... | collective-permute-start | bytes 1572872 | tf_op jit(solution)/shard_map/ppermute | solution.py:54
  27.3 33.9 %collective-permute-start.2 = (bf16[128,2048]{1,0:T(8,128)(2,1)}, bf16[128,2048]{1,0:T(8,128)(2,1)}, u32[]{:S(2)}, u32[]{:S(2)}) collective-permute-start(bf16[128,2048]{1,0:T(8,128)(2,1)} %get-tuple-element.95), channel_id=1, source_target_pairs={{0,16},{16,0},{8,24},{24,8},{1,17},{17,1},{9,25},{25,9},{2,18},{18... | collective-permute-start | bytes 1572872 | tf_op jit(solution)/shard_map/ppermute | solution.py:55
  29.8 34.9 %collective-permute-start.16 = (bf16[128,2048]{1,0:T(8,128)(2,1)}, bf16[128,2048]{1,0:T(8,128)(2,1)}, u32[]{:S(2)}, u32[]{:S(2)}) collective-permute-start(bf16[128,2048]{1,0:T(8,128)(2,1)} %get-tuple-element.90), channel_id=1, source_target_pairs={{0,8},{8,0},{16,24},{24,16},{1,9},{9,1},{17,25},{25,17},{2,10},{10... | collective-permute-start | bytes 1572872 | tf_op jit(solution)/shard_map/ppermute | solution.py:54
  30.4 37.1 %collective-permute-start.18 = (bf16[128,2048]{1,0:T(8,128)(2,1)}, bf16[128,2048]{1,0:T(8,128)(2,1)S(1)}, u32[]{:S(2)}, u32[]{:S(2)}) collective-permute-start(bf16[128,2048]{1,0:T(8,128)(2,1)} %get-tuple-element.89), channel_id=1, source_target_pairs={{0,16},{16,0},{8,24},{24,8},{1,17},{17,1},{9,25},{25,9},{2,18},{18... | collective-permute-start | bytes 1572872 | tf_op jit(solution)/shard_map/ppermute | solution.py:55
  31.4 619.1 %reduce-scatter.7.cloned.1.call-start = ((), (), s32[]{:S(2)}) async-start(), calls=%async_computation.9 | async-start | bytes 2359296 | tf_op jit(solution)/shard_map/reduce_scatter | solution.py:482
  66.9 77.0 %collective-permute-start.17 = (bf16[256,2048]{1,0:T(8,128)(2,1)}, bf16[256,2048]{1,0:T(8,128)(2,1)}, u32[]{:S(2)}, u32[]{:S(2)}) collective-permute-start(bf16[256,2048]{1,0:T(8,128)(2,1)} %pad_maximum_fusion.11), channel_id=1, source_target_pairs={{0,16},{16,0},{8,24},{24,8},{1,17},{17,1},{9,25},{25,9},{2,18},{18... | collective-permute-start | bytes 3145736 | tf_op jit(solution)/shard_map/ppermute | solution.py:56
  69.6 140.4 %collective-permute-start.19 = (bf16[256,2048]{1,0:T(8,128)(2,1)}, bf16[256,2048]{1,0:T(8,128)(2,1)}, u32[]{:S(2)}, u32[]{:S(2)}) collective-permute-start(bf16[256,2048]{1,0:T(8,128)(2,1)} %pad_maximum_fusion.12), channel_id=1, source_target_pairs={{0,8},{8,0},{16,24},{24,16},{1,9},{9,1},{17,25},{25,17},{2,10},{10... | collective-permute-start | bytes 3145736 | tf_op jit(solution)/shard_map/ppermute | solution.py:57
  147.5 26.3 %collective-permute-start.6 = (bf16[256,2048]{1,0:T(8,128)(2,1)}, bf16[256,2048]{1,0:T(8,128)(2,1)}, u32[]{:S(2)}, u32[]{:S(2)}) collective-permute-start(bf16[256,2048]{1,0:T(8,128)(2,1)} %convolution_convert_fusion.6), channel_id=1, source_target_pairs={{0,16},{16,0},{8,24},{24,8},{1,17},{17,1},{9,25},{25,9},{2,18},{18... | collective-permute-start | bytes 3145736 | tf_op jit(solution)/shard_map/ppermute | solution.py:78
  221.5 26.7 %collective-permute-start.9 = (bf16[256,2048]{1,0:T(8,128)(2,1)S(1)}, bf16[256,2048]{1,0:T(8,128)(2,1)S(1)}, u32[]{:S(2)}, u32[]{:S(2)}) collective-permute-start(bf16[256,2048]{1,0:T(8,128)(2,1)S(1)} %pad_maximum_fusion.9), channel_id=1, source_target_pairs={{0,16},{16,0},{8,24},{24,8},{1,17},{17,1},{9,25},{25,9},{2,18},{18... | collective-permute-start | bytes 3145736 | tf_op jit(solution)/shard_map/ppermute | solution.py:56
  304.9 27.1 %collective-permute-start.20 = (bf16[256,2048]{1,0:T(8,128)(2,1)}, bf16[256,2048]{1,0:T(8,128)(2,1)S(1)}, u32[]{:S(2)}, u32[]{:S(2)}) collective-permute-start(bf16[256,2048]{1,0:T(8,128)(2,1)} %convolution_convert_fusion.5), channel_id=1, source_target_pairs={{0,8},{8,0},{16,24},{24,16},{1,9},{9,1},{17,25},{25,17},{2,10},{10... | collective-permute-start | bytes 3145736 | tf_op jit(solution)/shard_map/ppermute | solution.py:77
  315.3 39.3 %collective-permute-start.22 = (bf16[256,2048]{1,0:T(8,128)(2,1)}, bf16[256,2048]{1,0:T(8,128)(2,1)S(1)}, u32[]{:S(2)}, u32[]{:S(2)}) collective-permute-start(bf16[256,2048]{1,0:T(8,128)(2,1)} %convolution_convert_fusion.4), channel_id=1, source_target_pairs={{0,16},{16,0},{8,24},{24,8},{1,17},{17,1},{9,25},{25,9},{2,18},{18... | collective-permute-start | bytes 3145736 | tf_op jit(solution)/shard_map/ppermute | solution.py:78
  318.7 34.3 %collective-permute-start.12 = (bf16[256,2048]{1,0:T(8,128)(2,1)S(1)}, bf16[256,2048]{1,0:T(8,128)(2,1)S(1)}, u32[]{:S(2)}, u32[]{:S(2)}) collective-permute-start(bf16[256,2048]{1,0:T(8,128)(2,1)S(1)} %convolution_convert_fusion.11), channel_id=1, source_target_pairs={{0,8},{8,0},{16,24},{24,16},{1,9},{9,1},{17,25},{25,17},{2,10},{10... | collective-permute-start | bytes 3145736 | tf_op jit(solution)/shard_map/ppermute | solution.py:77
  321.4 55.1 %collective-permute-start.14 = (bf16[256,2048]{1,0:T(8,128)(2,1)S(1)}, bf16[256,2048]{1,0:T(8,128)(2,1)S(1)}, u32[]{:S(2)}, u32[]{:S(2)}) collective-permute-start(bf16[256,2048]{1,0:T(8,128)(2,1)S(1)} %convolution_convert_fusion.10), channel_id=1, source_target_pairs={{0,16},{16,0},{8,24},{24,8},{1,17},{17,1},{9,25},{25,9},{2,18},{18... | collective-permute-start | bytes 3145736 | tf_op jit(solution)/shard_map/ppermute | solution.py:78
  332.2 43.0 %collective-permute-start.21 = (bf16[128,2048]{1,0:T(8,128)(2,1)S(1)}, bf16[128,2048]{1,0:T(8,128)(2,1)S(1)}, u32[]{:S(2)}, u32[]{:S(2)}) collective-permute-start(bf16[128,2048]{1,0:T(8,128)(2,1)S(1)} %fusion.29), channel_id=1, source_target_pairs={{0,16},{16,0},{8,24},{24,8},{1,17},{17,1},{9,25},{25,9},{2,18},{18... | collective-permute-start | bytes 1572872 | tf_op jit(solution)/shard_map/ppermute | solution.py:82
  353.1 32.5 %collective-permute-start.13 = (bf16[128,2048]{1,0:T(8,128)(2,1)S(1)}, bf16[128,2048]{1,0:T(8,128)(2,1)S(1)}, u32[]{:S(2)}, u32[]{:S(2)}) collective-permute-start(bf16[128,2048]{1,0:T(8,128)(2,1)S(1)} %fusion.33), channel_id=1, source_target_pairs={{0,16},{16,0},{8,24},{24,8},{1,17},{17,1},{9,25},{25,9},{2,18},{18... | collective-permute-start | bytes 1572872 | tf_op jit(solution)/shard_map/ppermute | solution.py:82
  444.7 221.6 %reduce-scatter.11.cloned.1.call-start = ((), (), s32[]{:S(2)}) async-start(), calls=%async_computation.11 | async-start | bytes 6488064 | tf_op jit(solution)/shard_map/reduce_scatter | solution.py:482
  455.2 243.2 %reduce-scatter.5.cloned.1.call-start = ((), (), s32[]{:S(2)}) async-start(), calls=%async_computation.8 | async-start | bytes 7077888 | tf_op jit(solution)/shard_map/reduce_scatter | solution.py:482
  522.2 214.4 %reduce-scatter.9.cloned.1.call-start = ((), (), s32[]{:S(2)}) async-start(), calls=%async_computation.10 | async-start | bytes 12976128 | tf_op jit(solution)/shard_map/reduce_scatter | solution.py:482
  753.9 36.3 %collective-permute-start.42 = (bf16[256,2816]{1,0:T(8,128)(2,1)S(1)}, bf16[256,2816]{1,0:T(8,128)(2,1)S(1)}, u32[]{:S(2)}, u32[]{:S(2)}) collective-permute-start(bf16[256,2816]{1,0:T(8,128)(2,1)S(1)} %pad_maximum_fusion.5), channel_id=1, source_target_pairs={{0,8},{8,0},{16,24},{24,16},{1,9},{9,1},{17,25},{25,17},{2,10},{10... | collective-permute-start | bytes 4325384 | tf_op jit(solution)/shard_map/ppermute | solution.py:57
  763.8 30.2 %collective-permute-start.43 = (bf16[256,2816]{1,0:T(8,128)(2,1)S(1)}, bf16[256,2816]{1,0:T(8,128)(2,1)S(1)}, u32[]{:S(2)}, u32[]{:S(2)}) collective-permute-start(bf16[256,2816]{1,0:T(8,128)(2,1)S(1)} %pad_maximum_fusion.6), channel_id=1, source_target_pairs={{0,16},{16,0},{8,24},{24,8},{1,17},{17,1},{9,25},{25,9},{2,18},{18... | collective-permute-start | bytes 4325384 | tf_op jit(solution)/shard_map/ppermute | solution.py:56
  (80 other events, 1173.8 us)
Sparse Core Ops, SparseCore 0:
  11.9 67.4 all-gather.8
  80.9 27.7 all-gather.10
  110.9 108.0 all-gather.12
  220.5 58.7 all-gather.14
  444.8 33.3 reduce-scatter.6
  481.0 64.4 reduce-scatter.10
  547.8 67.9 reduce-scatter.4
  618.1 118.4 reduce-scatter.8

commit v2 on v1

v2 whole, which is shorter than its diff:
```python
from functools import partial

import jax
import jax.numpy as jnp
from jax import lax
from jax.experimental import pallas as pl
from jax.experimental.pallas import tpu as pltpu
from jax.sharding import PartitionSpec as P

LOWER = 0.9
EPSILON = 1e-06
GRP = 4
LANE = 128
ROWS = 8
F32 = jnp.float32
BF16 = jnp.bfloat16
SWAP_X = [(0, 1), (1, 0), (2, 3), (3, 2)]
SWAP_Y = [(0, 2), (2, 0), (1, 3), (3, 1)]
TO_X, TO_Y, KEPT = (2, 6), (5, 7), (0, 1, 3, 4)
VMEM_LIMIT = 56 * 1024 * 1024
NN = (((1,), (0,)), ((), ()))
NT = (((1,), (1,)), ((), ()))
TN = (((0,), (0,)), ((), ()))
COSTS = {"finish_mid": 200}
SMALL = pl.CostEstimate(flops=1024, bytes_accessed=1024, transcendentals=0)
ANY = pl.BlockSpec(memory_space=pl.ANY)
SMEM = pl.BlockSpec(memory_space=pltpu.SMEM)


def dot(lhs_arr, rhs_arr, dims):
    return lax.dot_general(lhs_arr, rhs_arr, dims, preferred_element_type=F32)


def call(body, name, grid, in_specs, out_specs, out_shape, args, deps=(), scratch=(), aliases=None):
    n_in, n_deps = len(in_specs), len(deps)

    def wrapped(*refs):
        body(*refs[:n_in], *refs[n_in + n_deps :])

    return pl.pallas_call(
        wrapped,
        grid=grid,
        in_specs=list(in_specs) + [ANY] * n_deps,
        out_specs=out_specs,
        out_shape=out_shape,
        scratch_shapes=list(scratch),
        compiler_params=pltpu.CompilerParams(vmem_limit_bytes=VMEM_LIMIT),
        input_output_aliases=aliases or {},
        cost_estimate=pl.CostEstimate(
            flops=COSTS.get(name, 1) * 1_000_000_000, bytes_accessed=1024, transcendentals=0
        ),
        name=name,
    )(*args, *deps)


def shape(dims, dtype):
    return jax.ShapeDtypeStruct(tuple(dims), dtype)


def whole_block(array):
    return pl.BlockSpec(array.shape, lambda *i: (0,) * len(array.shape))


def product(name, lhs_arr, rhs_arr, depth, first, wide, step, deps=()):
    rows = lhs_arr.shape[0]

    def body(lhs_ref, rhs_ref, out_ref):
        out_ref[...] = dot(lhs_ref[...], rhs_ref[...], NN)

    return call(
        body,
        name,
        (wide // step,),
        [
            pl.BlockSpec((rows, depth), lambda j: (0, 0)),
            pl.BlockSpec((depth, step), lambda j: (0, first // step + j)),
        ],
        pl.BlockSpec((rows, step), lambda j: (0, j)),
        shape((rows, wide), F32),
        (lhs_arr, rhs_arr),
        deps,
    )


def product_back(name, lhs_arr, rhs_arr, step, deps=()):
    rows = lhs_arr.shape[0]
    wide, depth = rhs_arr.shape

    def body(lhs_ref, rest_ref, rhs_ref, out_ref, sum_ref):
        out_ref[...] = dot(lhs_ref[...], rhs_ref[...], NT)

        @pl.when(pl.program_id(0) == 0)
        def _():
            sum_ref[...] = jnp.broadcast_to(join(rest_ref[...]), (rows, LANE))

    return call(
        body,
        name,
        (wide // step,),
        [
            pl.BlockSpec((rows, depth), lambda j: (0, 0)),
            pl.BlockSpec((rows, LANE), lambda j: (0, depth // LANE)),
            pl.BlockSpec((step, depth), lambda j: (j, 0)),
        ],
        [pl.BlockSpec((rows, step), lambda j: (0, j)), pl.BlockSpec((rows, LANE), lambda j: (0, 0))],
        [shape((rows, wide), F32), shape((rows, LANE), F32)],
        (lhs_arr, lhs_arr, rhs_arr),
        deps,
    )


def outer_sum(name, lhs_arr, rhs_arr, rows, wide, step, deps=()):
    depth = lhs_arr.shape[0]
    by_rows = step > 0
    step = abs(step)

    def body(lhs_ref, rhs_ref, out_ref):
        out_ref[...] = dot(lhs_ref[...], rhs_ref[...], TN).astype(BF16)

    if by_rows:
        grid = (rows // step,)
        specs = [
            pl.BlockSpec((depth, step), lambda j: (0, j)),
            pl.BlockSpec((depth, wide), lambda j: (0, 0)),
        ]
        out_spec = pl.BlockSpec((step, wide), lambda j: (j, 0))
    else:
        grid = (wide // step,)
        specs = [
            pl.BlockSpec((depth, rows), lambda j: (0, 0)),
            pl.BlockSpec((depth, step), lambda j: (0, j)),
        ]
        out_spec = pl.BlockSpec((rows, step), lambda j: (0, j))
    return call(body, name, grid, specs, out_spec, shape((rows, wide), BF16), (lhs_arr, rhs_arr), deps)


def outer_gate_out(normed, grad_gate, mix, grad_mix, parts, wide, deps=()):
    depth, own = mix.shape
    count = own // parts
    turns = wide // own

    def right(lhs_ref, rhs_ref, out_ref):
        out_ref[...] = dot(lhs_ref[...], rhs_ref[...], TN).astype(BF16).reshape(parts, count, own)

    half_done = call(
        right,
        "part_out",
        (turns,),
        [
            pl.BlockSpec((depth, own), lambda j: (0, 0)),
            pl.BlockSpec((depth, own), lambda j: (0, j)),
        ],
        pl.BlockSpec((parts, count, own), lambda j: (0, j, 1)),
        shape((parts, turns * count, 2 * own), BF16),
        (mix, grad_mix),
        deps,
    ).reshape(wide, 2 * own)

    def left(lhs_ref, rhs_ref, _, out_ref):
        out_ref[...] = dot(lhs_ref[...], rhs_ref[...], TN).astype(BF16)

    return call(
        left,
        "part_gate",
        (turns,),
        [
            pl.BlockSpec((depth, own), lambda j: (0, j)),
            pl.BlockSpec((depth, own), lambda j: (0, 0)),
            ANY,
        ],
        pl.BlockSpec((own, own), lambda j: (j, 0)),
        shape((wide, 2 * own), BF16),
        (normed, grad_gate, half_done),
        aliases={2: 0},
    )


def after(value, *events):
    return lax.optimization_barrier((value, events))[0]


def send_x(value):
    return lax.ppermute(value, "grp", SWAP_X)


def send_y(value):
    return lax.ppermute(value, "grp", SWAP_Y)


def lay(pieces, deps=()):
    if any(piece.shape[0] % 16 for piece in pieces):
        return jnp.concatenate(pieces)
    wide = pieces[0].shape[1]
    at = [0]
    for piece in pieces:
        at.append(at[-1] + piece.shape[0])
    deps = tuple(deps)

    def body(*refs):
        out_ref, sems = refs[-2], refs[-1]
        copies = [
            pltpu.make_async_copy(
                ref, out_ref.at[pl.ds(at[index], pieces[index].shape[0])], sems.at[index]
            )
            for index, ref in enumerate(refs[: len(pieces)])
        ]
        for copy in copies:
            copy.start()
        for copy in copies:
            copy.wait()

    return call(
        body,
        "lay",
        (),
        [pl.BlockSpec(memory_space=pltpu.VMEM)] * len(pieces),
        ANY,
        shape((at[-1], wide), pieces[0].dtype),
        tuple(pieces),
        deps,
        [pltpu.SemaphoreType.DMA((len(pieces),))],
    )


def start_gather(own):
    half = own.shape[0] // 2 if own.shape[0] % 16 else (own.shape[0] + 16) // 32 * 16
    top, low = own[:half], own[half:]
    x_top, y_low = send_x(top), send_y(low)
    x_low, y_top = send_x(low), send_y(top)
    return (top, low, x_top, x_low, y_top, y_low), x_top


def end_gather(held, deps=(), hold=()):
    top, low, x_top, x_low, y_top, y_low = held
    x_on, y_on = (x_top, y_low) if not hold else after((x_top, y_low), hold)
    across_top, across_low = send_y(x_on), send_x(y_on)
    return lay((top, low, x_top, x_low, y_top, y_low, across_top, across_low), deps)


def gather_rows(own, deps=(), hold=()):
    return end_gather(start_gather(own)[0], deps, hold)


def sum_everywhere(value):
    value = value + send_x(value)
    value = value + send_y(value)
    count = lax.axis_size("seq")
    step = 1
    while step < count:
        value = value + lax.ppermute(value, "seq", [(one, one ^ step) for one in range(count)])
        step *= 2
    return value


def gather_blocks(own, deps=(), hold=()):
    held, came = start_gather(own)
    return end_gather(held, deps, hold).reshape((GRP,) + own.shape), came


def split(column):
    high = column.astype(BF16).astype(F32)
    rest = column - high
    middle = rest.astype(BF16).astype(F32)
    lane = lax.broadcasted_iota(jnp.int32, column.shape, 1)
    zero = jnp.zeros_like(column)
    picked = jnp.where(lane == 0, high, jnp.where(lane == 1, middle, jnp.where(lane == 2, rest - middle, zero)))
    return picked.astype(BF16)


def join(block):
    return jnp.sum(block.astype(F32), axis=1, keepdims=True)


def partial_sums(name, dims, rows, weights, step, column=None, deps=(), stacked=None, firsts=(0, 0)):
    half = rows[0].shape[0] // 8
    pairs = len(rows)
    if stacked is not None:
        wide, parts, first = stacked
        own = rows[0].shape[1]
        specs = [pl.BlockSpec((parts, own // parts, step), lambda j: (0, j, first // step))]
    elif dims is NN:
        wide = weights[0].shape[1]
        specs = [pl.BlockSpec((one.shape[1], step), lambda j: (0, j)) for one in rows]
    else:
        wide = weights[0].shape[0]
        specs = [
            pl.BlockSpec((step, one.shape[1]), lambda j, at=at // one.shape[1]: (j, at))
            for one, at in zip(rows, firsts)
        ]
    extra = 0 if column is None else LANE
    columns = () if column is None else (column,)

    def pick(value, slots):
        return jnp.concatenate([value[slot * half : (slot + 1) * half] for slot in slots])

    def body(*refs):
        x_ref, y_ref, kept_ref = refs[-3:]
        at = pl.ds(pl.multiple_of(pl.program_id(0) * step, LANE), step)
        sums = None
        for rows_ref, weights_ref in zip(refs[:pairs], refs[pairs : 2 * pairs]):
            block = weights_ref[...]
            if stacked is not None:
                block = block.reshape(own, step)
            term = dot(rows_ref[...], block, dims)
            sums = term if sums is None else sums + term
        x_ref[:, at] = pick(sums, TO_X).astype(BF16)
        y_ref[:, at] = pick(sums, TO_Y).astype(BF16)
        kept_ref[...] = pick(sums, KEPT)
        if column is not None:

            @pl.when(pl.program_id(0) == 0)
            def _():
                x_ref[:, wide:] = split(pick(refs[-4], TO_X))
                y_ref[:, wide:] = split(pick(refs[-4], TO_Y))

    sent = shape((2 * half, wide + extra), BF16)
    return call(
        body,
        name,
        (wide // step,),
        [whole_block(one) for one in rows] + specs + [whole_block(one) for one in columns],
        [whole_block(sent), whole_block(sent), pl.BlockSpec((4 * half, step), lambda j: (0, j))],
        [sent, sent, shape((4 * half, wide), F32)],
        tuple(rows) + tuple(weights) + columns,
        deps,
    )


def merge(name, kept, by_x, by_y, column=None, deps=()):
    half = kept.shape[0] // 4
    wide = kept.shape[1]
    extra = 0 if column is None else LANE
    columns = () if column is None else (column,)

    def body(kept_ref, by_x_ref, by_y_ref, *refs):
        for_y_ref, for_x_ref = refs[-2:]
        for_y_ref[:, :wide] = (kept_ref[half:, :] + by_x_ref[:, :wide].astype(F32)).astype(BF16)
        for_x_ref[:, :wide] = (kept_ref[:half, :] + by_y_ref[:, :wide].astype(F32)).astype(BF16)
        if column is not None:
            for_y_ref[:, wide:] = split(refs[0][4 * half : 5 * half] + join(by_x_ref[:, wide:]))
            for_x_ref[:, wide:] = split(refs[0][3 * half : 4 * half] + join(by_y_ref[:, wide:]))

    again = shape((half, wide + extra), BF16)
    return call(
        body,
        name,
        (1,),
        [
            pl.BlockSpec((2 * half, wide), lambda j: (1, 0)),
            pl.BlockSpec((half, wide + extra), lambda j: (1, 0)),
            pl.BlockSpec((half, wide + extra), lambda j: (1, 0)),
        ]
        + [whole_block(one) for one in columns],
        [whole_block(again), whole_block(again)],
        [again, again],
        (kept, by_x, by_y) + columns,
        deps,
    )


def scattered_specs(pieces, step, turn=None):
    kept, by_x, by_y, last_y, last_x = pieces[:5]
    half = last_y.shape[0]
    count = half // step
    wide = by_x.shape[1]
    received = pl.BlockSpec((step, wide), lambda h, i: (i, 0))
    specs = [
        pl.BlockSpec((step, kept.shape[1]), lambda h, i: (h * count + i, 0)),
        received,
        received,
        received,
        received,
    ]
    if len(pieces) > 5:
        specs.append(pl.BlockSpec((step, LANE), lambda h, i: (h * count + i, 0)))
    return specs


def scattered_sum(refs, wide):
    top = pl.program_id(0) == 0
    first = jnp.where(top, refs[1][...].astype(F32), refs[2][...].astype(F32))
    second = jnp.where(top, refs[3][...].astype(F32), refs[4][...].astype(F32))
    came = first + second
    total = refs[0][...] + came[:, :wide]
    if len(refs) == 5:
        return total, None
    return total, refs[5][:, :1] + jnp.sum(came[:, wide:], axis=1, keepdims=True)


def own_block(step, count, wide):
    return pl.BlockSpec((step, wide), lambda h, i: (h * count + i, 0))


def finish_mix(pieces, tokens, gain, width):
    rows = tokens.shape[0]
    half = rows // 2
    step = min(half, 64)
    count = half // step

    def body(*refs):
        tokens_ref, gain_ref, middle_ref, normed_ref, raw_ref, scale_ref, scale_mid_ref = refs[-7:]
        raw, squares = scattered_sum(refs[:-7], width)
        scale = lax.rsqrt(squares / width + EPSILON)
        middle = tokens_ref[...].astype(F32) + raw * scale
        scale_mid = lax.rsqrt(jnp.mean(middle * middle, axis=1, keepdims=True) + EPSILON)
        middle_ref[...] = middle
        raw_ref[...] = raw
        normed_ref[...] = (middle * scale_mid * gain_ref[...]).astype(BF16)
        scale_ref[...] = scale
        scale_mid_ref[...] = scale_mid

    block = own_block(step, count, width)
    thin = own_block(step, count, 1)
    return call(
        body,
        "finish_mix",
        (2, count),
        scattered_specs(pieces, step) + [block, pl.BlockSpec((1, width), lambda h, i: (0, 0))],
        [block, block, block, thin, thin],
        [
            shape((rows, width), F32),
            shape((rows, width), BF16),
            shape((rows, width), F32),
            shape((rows, 1), F32),
            shape((rows, 1), F32),
        ],
        tuple(pieces) + (tokens, gain),
    )


def add_scattered(pieces, middle, out, width, deps=()):
    rows = middle.shape[0]
    half = rows // 2
    step = min(half, 64)
    count = half // step

    def body(*refs):
        middle_ref, out_ref = refs[-2:]
        out_ref[...] = (middle_ref[...] + scattered_sum(refs[:-2], width)[0]).astype(out)

    block = own_block(step, count, width)
    return call(
        body,
        "add_scattered",
        (2, count),
        scattered_specs(pieces, step) + [block],
        block,
        shape((rows, width), out),
        tuple(pieces) + (middle,),
        deps,
    )


def norm_back(values, scale, gain, grad):
    weighted = values * grad
    inner = jnp.mean(weighted * gain, axis=1, keepdims=True)
    back = scale * gain * grad - values * (scale * scale * scale * inner)
    return back, jnp.sum(weighted * scale, axis=0, keepdims=True)


def finish_mid(pieces, middle, cotangent, raw, scale, scale_mid, gain, width):
    rows = middle.shape[0]
    half = rows // 2
    step = min(half, 64)
    count = half // step

    def body(*refs):
        middle_ref, cot_ref, raw_ref, scale_ref, scale_mid_ref, gain_ref, grad_ref, send_ref, sum_ref = refs[-9:]
        grad, _ = scattered_sum(refs[:-9], width)
        back, gain_part = norm_back(middle_ref[...], scale_mid_ref[...], gain_ref[...], grad)
        grad_middle = cot_ref[...].astype(F32) + back
        scale = scale_ref[...]
        coupling = scale * scale * scale * jnp.mean(raw_ref[...] * grad_middle, axis=1, keepdims=True)
        grad_ref[...] = grad_middle
        send_ref[:, :width] = (grad_middle * scale).astype(BF16)
        send_ref[:, width:] = split(jnp.broadcast_to(coupling, (step, LANE)))

        @pl.when((pl.program_id(0) == 0) & (pl.program_id(1) == 0))
        def _():
            sum_ref[...] = jnp.zeros_like(sum_ref)

        sum_ref[...] += gain_part

    block = own_block(step, count, width)
    thin = own_block(step, count, 1)
    row = pl.BlockSpec((1, width), lambda h, i: (0, 0))
    return call(
        body,
        "finish_mid",
        (2, count),
        scattered_specs(pieces, step) + [block, block, block, thin, thin, row],
        [block, own_block(step, count, width + LANE), row],
        [shape((rows, width), F32), shape((rows, width + LANE), BF16), shape((1, width), F32)],
        tuple(pieces) + (middle, cotangent, raw, scale, scale_mid, gain),
    )


def finish_in(pieces, tokens, grad_middle, gain, width, deps=()):
    rows = tokens.shape[0]
    half = rows // 2
    step = min(half, 64)
    count = half // step

    def body(*refs):
        tokens_ref, middle_ref, gain_ref, out_ref, sum_ref = refs[-5:]
        grad, _ = scattered_sum(refs[:-5], width)
        values = tokens_ref[...].astype(F32)
        scale = lax.rsqrt(jnp.mean(values * values, axis=1, keepdims=True) + EPSILON)
        back, gain_part = norm_back(values, scale, gain_ref[...], grad)
        out_ref[...] = middle_ref[...] + back

        @pl.when((pl.program_id(0) == 0) & (pl.program_id(1) == 0))
        def _():
            sum_ref[...] = jnp.zeros_like(sum_ref)

        sum_ref[...] += gain_part

    block = own_block(step, count, width)
    row = pl.BlockSpec((1, width), lambda h, i: (0, 0))
    return call(
        body,
        "finish_in",
        (2, count),
        scattered_specs(pieces, step) + [block, block, row],
        [block, row],
        [shape((rows, width), F32), shape((1, width), F32)],
        tuple(pieces) + (tokens, grad_middle, gain),
        deps,
    )


def norm_in(tokens, starts, gain, width):
    rows = tokens.shape[0]
    step = min(rows, 64)

    def body(starts_ref, tokens_ref, gain_ref, out_ref):
        values = tokens_ref[...].astype(F32)
        scale = lax.rsqrt(jnp.mean(values * values, axis=1, keepdims=True) + EPSILON)
        out_ref[:, :width] = (values * scale * gain_ref[...]).astype(BF16)
        here = starts_ref[0] + pl.program_id(0) * step
        here = here + lax.broadcasted_iota(jnp.int32, (step, LANE), 0)
        keep = jnp.ones((step, LANE), F32)
        for one in range(1, starts.shape[0]):
            keep = jnp.where(here == starts_ref[one], 0.0, keep)
        out_ref[:, width:] = keep.astype(BF16)

    return call(
        body,
        "norm_in",
        (rows // step,),
        [SMEM, pl.BlockSpec((step, width), lambda i: (i, 0)), pl.BlockSpec((1, width), lambda i: (0, 0))],
        pl.BlockSpec((step, width + LANE), lambda i: (i, 0)),
        shape((rows, width + LANE), BF16),
        (starts, tokens, gain),
    )


def feed_forward(normed, weights, deps=()):
    rows, depth = normed.shape
    own = weights.shape[1] // 2

    def body(normed_ref, weights_ref, hidden_ref, by_gate_ref, by_up_ref):
        both = dot(normed_ref[...], weights_ref[...], NN)
        gate, up = both[:, :LANE], both[:, LANE:]
        sig = jax.nn.sigmoid(gate)
        act = gate * sig
        hidden_ref[...] = (act * up).astype(BF16)
        by_gate_ref[...] = up * (sig * (1.0 + gate * (1.0 - sig)))
        by_up_ref[...] = act

    block = pl.BlockSpec((rows, LANE), lambda j: (0, j))
    return call(
        body,
        "feed_forward",
        (own // LANE,),
        [whole_block(normed), pl.BlockSpec((depth, 2 * LANE), lambda j: (0, j))],
        [block, block, block],
        [shape((rows, own), BF16), shape((rows, own), F32), shape((rows, own), F32)],
        (normed, weights),
        deps,
    )


def feed_back(cot, weights, by_gate, by_up, deps=()):
    rows, depth = cot.shape
    own = weights.shape[0]
    step = min(rows, 256)

    def body(cot_ref, weights_ref, by_gate_ref, by_up_ref, out_ref):
        grad = dot(cot_ref[...], weights_ref[...], NT)
        for turn in range(own // LANE):
            part = slice(turn * LANE, (turn + 1) * LANE)
            out_ref[:, 2 * turn * LANE : (2 * turn + 1) * LANE] = (grad[:, part] * by_gate_ref[:, part]).astype(BF16)
            out_ref[:, (2 * turn + 1) * LANE : (2 * turn + 2) * LANE] = (grad[:, part] * by_up_ref[:, part]).astype(BF16)

    return call(
        body,
        "feed_back",
        (rows // step,),
        [
            pl.BlockSpec((step, depth), lambda j: (j, 0)),
            whole_block(weights),
            pl.BlockSpec((step, own), lambda j: (j, 0)),
            pl.BlockSpec((step, own), lambda j: (j, 0)),
        ],
        pl.BlockSpec((step, 2 * own), lambda j: (j, 0)),
        shape((rows, 2 * own), BF16),
        (cot, weights, by_gate, by_up),
        deps,
    )


def by_relation(values, mine):
    values = jnp.where(mine % 2 == 1, values[jnp.array([1, 0, 3, 2])], values)
    return jnp.where(mine // 2 == 1, values[jnp.array([2, 3, 0, 1])], values)


def pick_columns(mine, matrices, parts, spread, deps=()):
    rows, wide = matrices[0].shape
    piece = wide // (GRP * parts)
    own = wide // GRP
    count = len(matrices)
    step = min(rows, 64)

    def body(mine_ref, *refs):
        out_ref = refs[-1]
        for index, ref in enumerate(refs[:-1]):
            for which in range(GRP):

                @pl.when(mine_ref[0] == which)
                def _(index=index, ref=ref, which=which):
                    whole = ref[...].astype(F32)
                    picked = jnp.concatenate(
                        [
                            whole[:, (part * GRP + which) * piece : (part * GRP + which + 1) * piece]
                            for part in range(parts)
                        ],
                        axis=1,
                    ).astype(BF16)
                    if not spread:
                        out_ref[:, index * own : (index + 1) * own] = picked
                    else:
                        for turn in range(own // LANE):
                            at = (turn * count + index) * LANE
                            out_ref[:, at : at + LANE] = picked[:, turn * LANE : (turn + 1) * LANE]

    return call(
        body,
        "pick_columns",
        (rows // step,),
        [SMEM] + [pl.BlockSpec((step, wide), lambda i: (i, 0))] * count,
        pl.BlockSpec((step, own * count), lambda i: (i, 0)),
        shape((rows, own * count), BF16),
        (mine.reshape(1),) + tuple(matrices),
        deps,
    )


def pick_first(mine, input_proj, forget_proj, gate_proj, out_proj, parts):
    rows, wide = input_proj.shape
    piece = wide // (GRP * parts)
    own = wide // GRP
    count = rows // GRP

    def body(mine_ref, input_ref, forget_ref, gate_ref, out_ref, first_ref):
        at = pl.ds(pl.multiple_of(mine_ref[0] * count, count), count)
        first_ref[:, 3 * own :] = out_ref[at, :]
        for which in range(GRP):

            @pl.when(mine_ref[0] == which)
            def _(which=which):
                for index, ref in enumerate((input_ref, forget_ref, gate_ref)):
                    picked = jnp.concatenate(
                        [
                            ref[:, (part * GRP + which) * piece : (part * GRP + which + 1) * piece].astype(F32)
                            for part in range(parts)
                        ],
                        axis=1,
                    ).astype(BF16)
                    if index == 2:
                        first_ref[:, 2 * own : 3 * own] = picked
                        continue
                    for turn in range(own // LANE):
                        to = (2 * turn + index) * LANE
                        first_ref[:, to : to + LANE] = picked[:, turn * LANE : (turn + 1) * LANE]

    block = pl.BlockSpec((count, wide), lambda i: (i, 0))
    return call(
        body,
        "pick_first",
        (GRP,),
        [SMEM, block, block, block, pl.BlockSpec((rows, own), lambda i: (0, i))],
        pl.BlockSpec((count, 4 * own), lambda i: (i, 0)),
        shape((rows, 4 * own), BF16),
        (mine.reshape(1), input_proj, forget_proj, gate_proj, out_proj),
    )


def place_columns(mine, blocks, parts, count, own, spread):
    _, rows, _ = blocks.shape
    piece = own // parts
    step = min(rows, 32)

    def body(mine_ref, blocks_ref, *out_refs):
        for which in range(GRP):
            block = blocks_ref[mine_ref[0] ^ which].astype(F32)
            for index, out_ref in enumerate(out_refs):
                if spread:
                    turns = [
                        block[:, (turn * count + index) * LANE : (turn * count + index + 1) * LANE]
                        for turn in range(own // LANE)
                    ]
                    mat = jnp.concatenate(turns, axis=1)
                else:
                    mat = block[:, index * own : (index + 1) * own]
                for part in range(parts):
                    at = (part * GRP + which) * piece
                    out_ref[:, at : at + piece] = mat[:, part * piece : (part + 1) * piece]

    return pl.pallas_call(
        body,
        grid=(rows // step,),
        in_specs=[
            pl.BlockSpec(memory_space=pltpu.SMEM),
            pl.BlockSpec((GRP, step, own * count), lambda i: (0, i, 0)),
        ],
        out_specs=[pl.BlockSpec((step, own * GRP), lambda i: (i, 0))] * count,
        out_shape=[jax.ShapeDtypeStruct((rows, own * GRP), F32)] * count,
        compiler_params=pltpu.CompilerParams(vmem_limit_bytes=VMEM_LIMIT),
        cost_estimate=SMALL,
        name="place_columns",
    )(mine.reshape(1), blocks)


def scan_forward(keep, proj, bias):
    _, half, wide = proj.shape
    own = wide // 2
    tiles = half // ROWS

    def body(keep_ref, proj_ref, bias_ref, prod_ref, state_ref, ends_ref):
        row = lax.broadcasted_iota(jnp.int32, (ROWS, LANE), 0)
        bias_row = bias_ref[...]

        def tile(part, step, carry):
            out = []
            for owner in range(GRP):
                slot = 2 * owner + part
                at = pl.ds(pl.multiple_of(step * ROWS, ROWS), ROWS)
                both = proj_ref[slot, at, :]
                enter = both[:, :LANE]
                forget = LOWER + (1.0 - LOWER) * jax.nn.sigmoid(both[:, LANE:] + bias_row)
                decay = forget * keep_ref[slot, at, :]
                income = enter * jax.nn.sigmoid(enter) * (1.0 - forget)
                for shift in (1, 2, 4):
                    fits = row >= shift
                    before = jnp.where(fits, pltpu.roll(income, shift, 0), 0.0)
                    factor = jnp.where(fits, pltpu.roll(decay, shift, 0), 1.0)
                    income = income + decay * before
                    decay = decay * factor
                prod, state = carry[owner]
                state_now = income + decay * state
                prod_now = decay * prod
                prod_ref[slot, at, :] = prod_now
                state_ref[slot, at, :] = state_now
                out.append((prod_now[ROWS - 1 :], state_now[ROWS - 1 :]))
            return tuple(out)

        carry = tuple(
            (jnp.ones((1, LANE), F32), jnp.zeros((1, LANE), F32)) for owner in range(GRP)
        )
        for part in range(2):
            carry = lax.fori_loop(0, tiles, partial(tile, part), carry)
        for owner in range(GRP):
            ends_ref[owner : owner + 1, :] = carry[owner][0]
            ends_ref[GRP + owner : GRP + owner + 1, :] = carry[owner][1]

    block = pl.BlockSpec((8, half, LANE), lambda j: (0, 0, j))
    return pl.pallas_call(
        body,
        grid=(own // LANE,),
        in_specs=[
            pl.BlockSpec((8, half, LANE), lambda j: (0, 0, 0)),
            pl.BlockSpec((8, half, 2 * LANE), lambda j: (0, 0, j)),
            pl.BlockSpec((1, LANE), lambda j: (0, j)),
        ],
        out_specs=[block, block, pl.BlockSpec((2 * GRP, LANE), lambda j: (0, j))],
        out_shape=[
            jax.ShapeDtypeStruct((8, half, own), F32),
            jax.ShapeDtypeStruct((8, half, own), F32),
            jax.ShapeDtypeStruct((2 * GRP, own), F32),
        ],
        compiler_params=pltpu.CompilerParams(vmem_limit_bytes=VMEM_LIMIT),
        cost_estimate=SMALL,
        name="scan_forward",
    )(keep, proj, bias)


def entering_state(info_ref, ends_ref, parts, backward):
    here = info_ref[0]
    state = jnp.zeros((GRP, LANE), F32)
    for place in range(parts - 1, 0, -1) if backward else range(parts - 1):
        longer = ends_ref[place, GRP:, :] + ends_ref[place, :GRP, :] * state
        state = jnp.where(place > here if backward else place < here, longer, state)
    return state


def finish_forward(info, ends, prod, state, proj, gain, deps=()):
    _, half, own = prod.shape
    count = ends.shape[0]

    def body(info_ref, ends_ref, prod_ref, state_ref, proj_ref, gain_ref, states_ref, mix_ref, squares_ref, enter_ref):
        entering = entering_state(info_ref, ends_ref, count, False)
        enter_ref[...] = entering

        @pl.when(pl.program_id(0) == 0)
        def _():
            squares_ref[...] = jnp.zeros_like(squares_ref)

        for owner in range(GRP):
            for part in range(2):
                slot = 2 * owner + part
                states = state_ref[slot] + prod_ref[slot] * entering[owner : owner + 1]
                states_ref[slot] = states
                gate = proj_ref[slot]
                mix_ref[slot] = (states * gain_ref[...] * (gate * jax.nn.sigmoid(gate))).astype(BF16)
                squares_ref[slot] += states * states

        @pl.when(pl.program_id(0) == own // LANE - 1)
        def _():
            for slot in range(8):
                total = jnp.sum(squares_ref[slot], axis=1, keepdims=True)
                squares_ref[slot] = jnp.broadcast_to(total, (half, LANE))

    block = pl.BlockSpec((8, half, LANE), lambda j: (0, 0, j))
    return call(
        body,
        "finish_forward",
        (own // LANE,),
        [
            SMEM,
            pl.BlockSpec((count, 2 * GRP, LANE), lambda j: (0, 0, j)),
            block,
            block,
            block,
            pl.BlockSpec((1, LANE), lambda j: (0, j)),
        ],
        [
            block,
            block,
            pl.BlockSpec((8, half, LANE), lambda j: (0, 0, 0)),
            pl.BlockSpec((GRP, LANE), lambda j: (0, j)),
        ],
        [
            shape((8, half, own), F32),
            shape((8, half, own), BF16),
            shape((8, half, LANE), F32),
            shape((GRP, own), F32),
        ],
        (info, ends, prod, state, proj, gain),
        deps,
    )


def scan_backward(keep, proj, proj_gate, bias, gain, states, back, coupling):
    _, half, own = proj_gate.shape
    tiles = half // ROWS

    def body(
        keep_ref, proj_ref, gate_ref, bias_ref, gain_ref, states_ref, back_ref, coupling_ref,
        prod_ref, grad_ref, ends_ref, out_ref, sum_ref,
    ):
        row = lax.broadcasted_iota(jnp.int32, (ROWS, LANE), 0)
        bias_row = bias_ref[...]
        gain_row = gain_ref[...]

        def tile(part, turn, carry):
            step = tiles - 1 - turn
            out = []
            for owner in range(GRP):
                slot = 2 * owner + part
                at = pl.ds(pl.multiple_of(step * ROWS, ROWS), ROWS)
                gate = gate_ref[slot, at, :]
                forget = LOWER + (1.0 - LOWER) * jax.nn.sigmoid(proj_ref[slot, at, :] + bias_row)
                decay = forget * keep_ref[slot, at, :]
                direct = (
                    gain_row * (gate * jax.nn.sigmoid(gate)) * back_ref[slot, at, :]
                    - states_ref[slot, at, :] * coupling_ref[slot, at, :]
                )
                flow = decay * direct
                for shift in (1, 2, 4):
                    fits = row < ROWS - shift
                    later = jnp.where(fits, pltpu.roll(flow, ROWS - shift, 0), 0.0)
                    factor = jnp.where(fits, pltpu.roll(decay, ROWS - shift, 0), 1.0)
                    flow = flow + decay * later
                    decay = decay * factor
                prod, grad = carry[owner]
                flow = flow + decay * grad
                decay = decay * prod
                last = row == ROWS - 1
                grad_ref[slot, at, :] = direct + jnp.where(last, grad, pltpu.roll(flow, ROWS - 1, 0))
                prod_ref[slot, at, :] = jnp.where(last, prod, pltpu.roll(decay, ROWS - 1, 0))
                out.append((decay[:1], flow[:1]))
            return tuple(out)

        carry = tuple(
            (jnp.ones((1, LANE), F32), jnp.zeros((1, LANE), F32)) for owner in range(GRP)
        )
        for part in (1, 0):
            carry = lax.fori_loop(0, tiles, partial(tile, part), carry)
        for owner in range(GRP):
            ends_ref[owner : owner + 1, :] = carry[owner][0]
            ends_ref[GRP + owner : GRP + owner + 1, :] = carry[owner][1]
        gain_sum = jnp.zeros((1, LANE), F32)
        for slot in range(8):
            gate = gate_ref[slot]
            gate_sig = jax.nn.sigmoid(gate)
            pull = back_ref[slot] * states_ref[slot]
            out_ref[slot] = (pull * gain_row * (gate_sig * (1.0 + gate * (1.0 - gate_sig)))).astype(BF16)
            gain_sum = gain_sum + jnp.sum(pull * (gate * gate_sig), axis=0, keepdims=True)
        sum_ref[...] = gain_sum

    block = pl.BlockSpec((8, half, LANE), lambda j: (0, 0, j))
    vector = pl.BlockSpec((1, LANE), lambda j: (0, j))
    rows = pl.BlockSpec((8, half, LANE), lambda j: (0, 0, 0))
    return call(
        body,
        "scan_backward",
        (own // LANE,),
        [rows, pl.BlockSpec((8, half, LANE), lambda j: (0, 0, 2 * j + 1)), block, vector, vector, block, block, rows],
        [block, block, pl.BlockSpec((2 * GRP, LANE), lambda j: (0, j)), block, vector],
        [
            shape((8, half, own), F32),
            shape((8, half, own), F32),
            shape((2 * GRP, own), F32),
            shape((8, half, own), BF16),
            shape((1, own), F32),
        ],
        (keep, proj, proj_gate, bias, gain, states, back, coupling),
    )


def finish_backward(info, keep, ends, prod, grad, proj, bias, states, enter, deps=()):
    _, half, own = prod.shape
    parts = ends.shape[0]

    def body(info_ref, keep_ref, ends_ref, prod_ref, grad_ref, proj_ref, bias_ref, states_ref, enter_ref, out_ref, sum_ref):
        entering = entering_state(info_ref, ends_ref, parts, True)
        first = lax.broadcasted_iota(jnp.int32, (half, LANE), 0) == 0
        bias_sum = jnp.zeros((1, LANE), F32)
        for owner in range(GRP):
            before = enter_ref[owner : owner + 1, :]
            for part in range(2):
                slot = 2 * owner + part
                states = states_ref[slot]
                previous = jnp.where(first, before, pltpu.roll(states, 1, 0))
                before = states[half - 1 :]
                total = grad_ref[slot] + prod_ref[slot] * entering[owner : owner + 1]
                enter = proj_ref[slot, :, :LANE]
                sig = jax.nn.sigmoid(proj_ref[slot, :, LANE:] + bias_ref[...])
                enter_sig = jax.nn.sigmoid(enter)
                grad_forget = total * (previous * keep_ref[slot] - enter * enter_sig)
                grad_proj = grad_forget * ((1.0 - LOWER) * sig * (1.0 - sig))
                forget = LOWER + (1.0 - LOWER) * sig
                out_ref[slot, :, :LANE] = (
                    total * (1.0 - forget) * (enter_sig * (1.0 + enter * (1.0 - enter_sig)))
                ).astype(BF16)
                out_ref[slot, :, LANE:] = grad_proj.astype(BF16)
                bias_sum = bias_sum + jnp.sum(grad_proj, axis=0, keepdims=True)
        sum_ref[...] = bias_sum

    block = pl.BlockSpec((8, half, LANE), lambda j: (0, 0, j))
    pair = pl.BlockSpec((8, half, 2 * LANE), lambda j: (0, 0, j))
    vector = pl.BlockSpec((1, LANE), lambda j: (0, j))
    return call(
        body,
        "finish_backward",
        (own // LANE,),
        [
            SMEM,
            pl.BlockSpec((8, half, LANE), lambda j: (0, 0, 0)),
            pl.BlockSpec((parts, 2 * GRP, LANE), lambda j: (0, 0, j)),
            block,
            block,
            pair,
            vector,
            block,
            pl.BlockSpec((GRP, LANE), lambda j: (0, j)),
        ],
        [pair, vector],
        [shape((8, half, 2 * own), BF16), shape((1, own), F32)],
        (info, keep, ends, prod, grad, proj, bias, states, enter),
        deps,
    )


def place_rows(mine, blocks, deps=()):
    _, rows, wide = blocks.shape

    def body(mine_ref, blocks_ref, out_ref):
        out_ref[0] = blocks_ref[mine_ref[0] ^ pl.program_id(0)].astype(F32)

    return call(
        body,
        "place_rows",
        (GRP,),
        [SMEM, whole_block(blocks)],
        pl.BlockSpec((1, rows, wide), lambda j: (j, 0, 0)),
        shape((GRP, rows, wide), F32),
        (mine.reshape(1), blocks),
        deps,
    ).reshape(GRP * rows, wide)


def place_stacked(mine, blocks, first, own):
    _, rows, wide = blocks.shape
    count = rows // GRP

    def body(mine_ref, blocks_ref, out_ref):
        for which in range(GRP):
            out_ref[which * count : (which + 1) * count, :] = blocks_ref[mine_ref[0] ^ which].astype(F32)

    return call(
        body,
        "place_stacked",
        (GRP,),
        [SMEM, pl.BlockSpec((GRP, count, own), lambda j: (0, j, first // own))],
        pl.BlockSpec((rows, own), lambda j: (0, j)),
        shape((rows, GRP * own), F32),
        (mine.reshape(1), blocks),
    )


def on_device(
    tokens,
    seq_lengths,
    cotangent,
    norm_gain,
    input_proj,
    forget_proj,
    forget_bias,
    gate_proj,
    state_gain,
    out_proj,
    mlp_gain,
    mlp_gate,
    mlp_up,
    mlp_down,
):
    tok_rows, width = tokens.shape
    half = tok_rows // 2
    plane = GRP * tok_rows
    parts = lax.axis_size("seq")
    mine, place = lax.axis_index("grp"), lax.axis_index("seq")
    own = width // GRP

    def own_rows(matrix):
        count = matrix.shape[0] // GRP
        return lax.dynamic_slice_in_dim(matrix, mine * count, count, 0)

    def own_features(vector):
        cut = vector.reshape(parts, GRP, -1)
        return lax.dynamic_index_in_dim(cut, mine, 1, False).reshape(1, -1)

    def all_features(vector):
        cut = vector.reshape(parts, 1, -1)
        spread = jnp.where(jnp.arange(GRP)[None, :, None] == mine, cut, 0.0)
        return spread.reshape(-1)

    def whole(rows):
        return lax.all_gather(rows, "seq", axis=0, tiled=True)

    def reduced(grads):
        return lax.psum_scatter(grads, "seq", scatter_dimension=0, tiled=True)

    starts = (jnp.cumsum(seq_lengths[0]) - seq_lengths[0]).astype(jnp.int32)
    starts = jnp.concatenate([(place * tok_rows).reshape(1).astype(jnp.int32), starts])
    info = place.reshape(1).astype(jnp.int32)
    bias = own_features(forget_bias)
    gain = own_features(state_gain)
    in_gain, mid_gain = norm_gain.reshape(1, -1), mlp_gain.reshape(1, -1)

    w_first = whole(pick_first(mine, input_proj, forget_proj, gate_proj, out_proj, parts))
    normed = norm_in(tokens, starts, in_gain, width)
    normed = gather_rows(normed)
    ff_cols = pick_columns(mine, (mlp_gate, mlp_up), parts, True, (normed,))
    w_ff = whole(ff_cols)
    w_down = whole(own_rows(mlp_down))
    cot = gather_rows(after(cotangent, normed), deps=(ff_cols,))
    keep = normed[:, width:].astype(F32).reshape(8, half, LANE)

    proj = product("proj_pair", normed, w_first, width, 0, 2 * own, 256, (cot,)).reshape(8, half, 2 * own)
    prod, state, ends = scan_forward(keep, proj, bias)
    ends = lax.all_gather(ends, "seq")
    proj_gate = product("proj_gate", normed, w_first, width, 2 * own, own, 256, (prod,))
    proj_gate = proj_gate.reshape(8, half, own)
    states, mix, squares, enter = finish_forward(info, ends, prod, state, proj_gate, gain)
    mix, squares = mix.reshape(plane, own), squares.reshape(plane, LANE)
    w_stacked = w_first.reshape(parts, -1, 4 * own)
    to_x, to_y, kept = partial_sums(
        "mix", NN, (mix,), (w_stacked,), own, squares, stacked=(width, parts, 3 * own)
    )
    by_x, by_y = send_x(to_x), send_y(to_y)
    for_y, for_x = merge("mix_merge", kept, by_x, by_y, squares)
    pieces = (kept, by_x, by_y, send_y(for_y), send_x(for_x), squares)
    middle, normed_mid, raw, scale_state, scale_mid = finish_mix(pieces, tokens, mid_gain, width)
    normed_mid = gather_rows(normed_mid)
    w_out = w_stacked[:, :, 3 * own :].reshape(parts, GRP, -1, own).transpose(0, 2, 1, 3)
    w_out = w_out.reshape(own, width)

    hidden, by_gate, by_up = feed_forward(normed_mid, w_ff)
    part_down = outer_sum("part_down", hidden, cot, hidden.shape[1], width, -512)
    sum_down = reduced(part_down)

    to_x, to_y, kept_out = partial_sums("down", NN, (hidden,), (w_down,), 256, deps=(part_down,))
    by_x_out, by_y_out = send_x(to_x), send_y(to_y)
    grad_ff = feed_back(cot, w_down, by_gate, by_up, (to_x,))
    to_x, to_y, kept = partial_sums("grad_mid", NT, (grad_ff,), (w_ff,), 256)
    by_x, by_y = send_x(to_x), send_y(to_y)
    out_for_y, out_for_x = merge("down_merge", kept_out, by_x_out, by_y_out, deps=(to_x,))
    out_last_y, out_last_x = send_y(out_for_y), send_x(out_for_x)
    part_ff = outer_sum("part_ff", normed_mid, grad_ff, width, grad_ff.shape[1], 256, (out_for_y,))
    sum_ff = reduced(part_ff)
    for_y, for_x = merge("grad_mid_merge", kept, by_x, by_y, deps=(part_ff,))
    pieces = (kept, by_x, by_y, send_y(for_y), send_x(for_x))
    grad_middle, scaled_mix, grad_mlp_gain = finish_mid(
        pieces, middle, cotangent, raw, scale_state, scale_mid, mid_gain, width
    )
    pieces_out = (kept_out, by_x_out, by_y_out, out_last_y, out_last_x)
    grad_mix = gather_rows(scaled_mix)

    back, coupling = product_back("back", grad_mix, w_out, 256)
    after_prod, local, ends_back, grad_gate, gain_sum = scan_backward(
        keep,
        proj,
        proj_gate,
        bias,
        gain,
        states,
        back.reshape(8, half, own),
        coupling.reshape(8, half, LANE),
    )
    ends_back = lax.all_gather(ends_back, "seq")
    blocks_down, _ = gather_blocks(after(sum_down, grad_mix), (ends_back,), (after_prod,))
    block_out = add_scattered(pieces_out, middle, BF16, width, (blocks_down,))
    grad_gate = grad_gate.reshape(plane, own)
    part_gate_out = outer_gate_out(normed, grad_gate, mix, grad_mix, parts, width, (block_out,))
    sum_gate_out = reduced(part_gate_out)
    grad_pair, bias_sum = finish_backward(
        info, keep, ends_back, after_prod, local, proj, bias, states, enter, (part_gate_out,)
    )
    grad_pair = grad_pair.reshape(plane, 2 * own)
    held, came_ff = start_gather(after(sum_ff, blocks_down))
    part_pair = outer_sum("part_pair", normed, grad_pair, width, 2 * own, 256, (came_ff,))
    sum_pair = reduced(part_pair)
    to_x, to_y, kept = partial_sums(
        "grad_in",
        NT,
        (grad_pair, grad_gate),
        (w_first, w_first),
        256,
        deps=(part_pair,),
        firsts=(0, 2 * own),
    )
    by_x, by_y = send_x(to_x), send_y(to_y)
    blocks_ff = end_gather(held, (to_x,), (grad_pair,)).reshape((GRP,) + sum_ff.shape)
    grad_down = place_rows(mine, blocks_down, (to_x,))
    for_y, for_x = merge("grad_in_merge", kept, by_x, by_y, deps=(grad_down, blocks_ff))
    last_y, last_x = send_y(for_y), send_x(for_x)
    pieces = (kept, by_x, by_y, last_y, last_x)
    grad_tokens, grad_norm_gain = finish_in(pieces, tokens, grad_middle, in_gain, width)
    vectors = sum_everywhere(
        jnp.stack(
            [grad_norm_gain[0], all_features(bias_sum), all_features(gain_sum), grad_mlp_gain[0]]
        )
    )
    blocks_gate_out, came = gather_blocks(after(sum_gate_out, by_y))
    grad_mlp_gate, grad_mlp_up = place_columns(mine, blocks_ff, parts, 2, w_ff.shape[1] // 2, True)
    (grad_gate_proj,) = place_columns(mine, blocks_gate_out, parts, 1, own, True)
    grad_out = place_stacked(mine, blocks_gate_out, own, own)
    blocks_pair, _ = gather_blocks(after(sum_pair, came), (grad_mlp_gate, grad_gate_proj, grad_out))
    grad_input, grad_forget = place_columns(mine, blocks_pair, parts, 2, own, True)
    return (
        block_out,
        grad_tokens,
        vectors[0],
        grad_input,
        grad_forget,
        vectors[1],
        grad_gate_proj,
        vectors[2],
        grad_out,
        vectors[3],
        grad_mlp_gate,
        grad_mlp_up,
        grad_down,
    )


def solution(mesh):
    rows = P("seq", None)
    tokens = P(("grp", "seq"), None)
    return jax.shard_map(
        on_device,
        mesh=mesh,
        in_specs=(
            tokens,
            P("grp", None),
            tokens,
            P(),
            rows,
            rows,
            P(),
            rows,
            P(),
            rows,
            P(),
            rows,
            rows,
            rows,
        ),
        out_specs=(
            tokens,
            tokens,
            P(),
            rows,
            rows,
            P(),
            rows,
            P(),
            rows,
            P(),
            rows,
            rows,
            rows,
        ),
        check_vma=False,
    )
```

time: 827 us -> 713 us (0.86); the launches traced: 814 us -> 710 us
  Pallas kernels: 63.8 us -> 300 us
  matrix products: 156 us -> 0 us
  blocking collectives: 119 us -> 34.2 us
  waiting for transfers between devices: 285 us -> 242 us
  other arithmetic: 45.2 us -> 5.26 us
  local copies, waits for them, and re-layouts: 76.4 us -> 36.7 us
  starting transfers between devices: 54 us -> 77.4 us
    pallas_call x6 -> x39, Pallas kernels: 46.8 us -> 278 us  [the longest x38 270 us: call(): pl.pallas_call(wrapped, grid=grid, in_specs=list(in_specs) + [ANY] * n_de...]
    dot_general x21 -> x0, matrix products: 156 us -> none  [the longest x8 63.6 us: matmul_back(): lax.dot_general(lhs_arr, rhs_arr, (((1,), (1,)), ((), ())), preferred_ele...]
    psum x2 -> x0, blocking collectives: 54.9 us -> none  [the longest x1 39.1 us: on_device(): vectors = lax.psum(vectors, ('grp', 'seq'))]
    ppermute x48 -> x69, waiting for transfers between devices: 277 us -> 242 us  [the longest x33 124 us: send_y(): return lax.ppermute(value, 'grp', SWAP_Y)]
    all_gather x2 -> x0, blocking collectives: 30 us -> none  [the longest x1 22.6 us: on_device(): lengths = lax.all_gather(seq_lengths, 'grp', axis=0, tiled=True)]
    ppermute x48 -> x69, starting transfers between devices: 53.2 us -> 77 us  [the longest x33 36.5 us: send_y(): return lax.ppermute(value, 'grp', SWAP_Y)]
    unnamed x142 -> x177, local copies, waits for them, and re-layouts: 40.7 us -> 19.5 us
    gather x10 -> x0, local copies, waits for them, and re-layouts: 13.3 us -> none  [the longest x5 8.66 us: by_relation(): return jnp.where(mine // 2 == 1, values[jnp.array([2, 3, 0, 1])], values)]
  transfers between devices with their start and end apart: 56 -> 76, of which waited for: 34 -> 32; matrix products, arithmetic and copies ran while one was open for 29% -> 3% of each run, Pallas kernels for 6% -> 40%
where the time goes in v2:
time: 713 us; the launch traced here: 710 us
  Pallas kernels  300 us (42%)
  waiting for transfers between devices  242 us (34%)
  starting transfers between devices  77.4 us (11%)
  local copies, waits for them, and re-layouts  36.7 us (5%)
  blocking collectives  34.2 us (5%)
  between operations  15.1 us (2%)
    pallas_call x38, Pallas kernels, call(): pl.pallas_call(wrapped, grid=grid, in_specs=list(in_specs) + [ANY] * n_de...  270 us
    ppermute x33, waiting for transfers between devices, send_y(): return lax.ppermute(value, 'grp', SWAP_Y)  124 us
    ppermute x33, waiting for transfers between devices, send_x(): return lax.ppermute(value, 'grp', SWAP_X)  118 us
    ppermute x33, starting transfers between devices, send_y(): return lax.ppermute(value, 'grp', SWAP_Y)  36.5 us
    ppermute x33, starting transfers between devices, send_x(): return lax.ppermute(value, 'grp', SWAP_X)  35.9 us
    pallas_call x3, Pallas kernels, place_columns(): pl.pallas_call(body, grid=(rows // step,), in_specs=[pl.BlockSpec(memory_...  21.6 us
    unnamed x177, local copies, waits for them, and re-layouts  19.5 us
    all_gather x1, blocking collectives, on_device(): ends = lax.all_gather(ends, 'seq')  17.3 us
  transfers between devices with their start and end apart: 76, of which 32 were waited for; matrix products, arithmetic and copies ran while one was open for 3% of the time, Pallas kernels for 40%

profile of v2, /device:TPU:0, one launch (start us, length us, event | category | flops | bytes accessed | tf_op | source)
XLA Modules:
  0.0 710.3 jit_solution(3527829403101756545)
XLA Ops:
  22.6 11.3 %collective-permute-done.3.refs_5_ = bf16[128,2176]{1,0:T(8,128)(2,1)S(1)} collective-permute-done((bf16[128,2176]{1,0:T(8,128)(2,1)S(1)}, bf16[128,2176]{1,0:T(8,128)(2,1)S(1)}, u32[]{:S(2)}, u32[]{:S(2)}) %collective-permute-start.3) | collective-permute-done | bytes 557088 | tf_op jit(solution)/shard_map/ppermute | solution.py:187
  37.5 10.5 %collective-permute-done.1.refs_3_ = bf16[128,2176]{1,0:T(8,128)(2,1)S(1)} collective-permute-done((bf16[128,2176]{1,0:T(8,128)(2,1)S(1)}, bf16[128,2176]{1,0:T(8,128)(2,1)S(1)}, u32[]{:S(2)}, u32[]{:S(2)}) %collective-permute-start.1) | collective-permute-done | bytes 557088 | tf_op jit(solution)/shard_map/ppermute | solution.py:183
  47.9 10.5 %collective-permute-done.5.refs_7_ = bf16[128,2176]{1,0:T(8,128)(2,1)S(1)} collective-permute-done((bf16[128,2176]{1,0:T(8,128)(2,1)S(1)}, bf16[128,2176]{1,0:T(8,128)(2,1)S(1)}, u32[]{:S(2)}, u32[]{:S(2)}) %collective-permute-start.5) | collective-permute-done | bytes 557088 | tf_op jit(solution)/shard_map/ppermute | solution.py:183
  75.9 10.8 %collective-permute-done.9.refs_5_ = bf16[128,2048]{1,0:T(8,128)(2,1)S(1)} collective-permute-done((bf16[128,2048]{1,0:T(8,128)(2,1)S(1)}, bf16[128,2048]{1,0:T(8,128)(2,1)S(1)}, u32[]{:S(2)}, u32[]{:S(2)}) %collective-permute-start.9) | collective-permute-done | bytes 524320 | tf_op jit(solution)/shard_map/ppermute | solution.py:187
  129.0 17.3 %all-gather = f32[64,512]{1,0:T(8,128)} all-gather(f32[8,512]{1,0:T(8,128)} %get-tuple-element.76), channel_id=2, replica_groups=mesh['grp'=4,'seq'=8] {'seq'}, dimensions={0}, use_global_device_ids=true | all-gather | bytes 147456 | tf_op jit(solution)/shard_map/all_gather | solution.py:1093
  168.1 24.0 %collective-permute-done.12.refs_1_ = bf16[256,2176]{1,0:T(8,128)(2,1)S(1)} collective-permute-done((bf16[256,2176]{1,0:T(8,128)(2,1)}, bf16[256,2176]{1,0:T(8,128)(2,1)S(1)}, u32[]{:S(2)}, u32[]{:S(2)}) %collective-permute-start.12) | collective-permute-done | bytes 1114144 | tf_op jit(solution)/shard_map/ppermute | solution.py:183
  199.8 11.9 %collective-permute-done.14.refs_3_ = bf16[128,2176]{1,0:T(8,128)(2,1)S(1)} collective-permute-done((bf16[128,2176]{1,0:T(8,128)(2,1)}, bf16[128,2176]{1,0:T(8,128)(2,1)S(1)}, u32[]{:S(2)}, u32[]{:S(2)}) %collective-permute-start.14) | collective-permute-done | bytes 557088 | tf_op jit(solution)/shard_map/ppermute | solution.py:187
  226.0 10.8 %collective-permute-done.19.refs_5_ = bf16[128,2048]{1,0:T(8,128)(2,1)S(1)} collective-permute-done((bf16[128,2048]{1,0:T(8,128)(2,1)S(1)}, bf16[128,2048]{1,0:T(8,128)(2,1)S(1)}, u32[]{:S(2)}, u32[]{:S(2)}) %collective-permute-start.19) | collective-permute-done | bytes 524320 | tf_op jit(solution)/shard_map/ppermute | solution.py:187
  238.9 9.7 %collective-permute-done.17.refs_3_ = bf16[128,2048]{1,0:T(8,128)(2,1)S(1)} collective-permute-done((bf16[128,2048]{1,0:T(8,128)(2,1)S(1)}, bf16[128,2048]{1,0:T(8,128)(2,1)S(1)}, u32[]{:S(2)}, u32[]{:S(2)}) %collective-permute-start.17) | collective-permute-done | bytes 524320 | tf_op jit(solution)/shard_map/ppermute | solution.py:183
  263.1 19.9 %feed_forward.1 = (bf16[1024,1408]{1,0:T(8,128)(2,1)}, f32[1024,1408]{1,0:T(8,128)}, f32[1024,1408]{1,0:T(8,128)}) custom-call(bf16[1024,2048]{1,0:T(8,128)(2,1)} %lay.10.refs_0_, bf16[2048,2816]{1,0:T(8,128)(2,1)} %all-gather.8.cloned.1.call-done.refs_1_), custom_call_target="tpu_custom_call" | custom-call | flops 1000000000 | bytes 1024 | tf_op jit(solution)/shard_map/feed_forward/pallas_call | solution.py:40
  283.0 10.1 %part_down.1.refs_2_ = bf16[1408,2048]{1,0:T(8,128)(2,1)} custom-call(bf16[1024,1408]{1,0:T(8,128)(2,1)} %get-tuple-element.87.refs_0_, bf16[1024,2048]{1,0:T(8,128)(2,1)} %lay.9.refs_2_.refs_1_.refs_0_), custom_call_target="tpu_custom_call" | custom-call | flops 1000000000 | bytes 1024 | tf_op jit(solution)/shard_map/part_down/pallas_call | solution.py:40
  293.4 12.3 %down.1 = (bf16[256,2048]{1,0:T(8,128)(2,1)}, bf16[256,2048]{1,0:T(8,128)(2,1)}, f32[512,2048]{1,0:T(8,128)}) custom-call(bf16[1024,1408]{1,0:T(8,128)(2,1)} %get-tuple-element.87.refs_0_, bf16[1408,2048]{1,0:T(8,128)(2,1)} %all-gather.10.cloned.1.call-done.refs_1_, bf16[1408,2048]{1,0:T(8,128)(2,1)} %part_down.1.refs_2_), custom_call_target="tpu_custom_call" | custom-call | flops 1000000000 | bytes 1024 | tf_op jit(solution)/shard_map/down/pallas_call | solution.py:40
  308.1 14.0 %feed_back.1.refs_0_.refs_1_ = bf16[1024,2816]{1,0:T(8,128)(2,1)} custom-call(bf16[1024,2048]{1,0:T(8,128)(2,1)} %lay.9.refs_2_.refs_1_.refs_0_, bf16[1408,2048]{1,0:T(8,128)(2,1)} %all-gather.10.cloned.1.call-done.refs_1_, f32[1024,1408]{1,0:T(8,128)} %get-tuple-element.91.refs_2_, f32[1024,1408]{1,0:T(8,128)} %get-tuple-element.92.refs_3_, ...), custom_call_target="tpu_custom_call" | custom-call | flops 1000000000 | bytes 1024 | tf_op jit(solution)/shard_map/feed_back/pallas_call | solution.py:40
  322.1 18.1 %grad_mid.1 = (bf16[256,2048]{1,0:T(8,128)(2,1)}, bf16[256,2048]{1,0:T(8,128)(2,1)}, f32[512,2048]{1,0:T(8,128)}) custom-call(bf16[1024,2816]{1,0:T(8,128)(2,1)} %feed_back.1.refs_0_.refs_1_, bf16[2048,2816]{1,0:T(8,128)(2,1)} %all-gather.8.cloned.1.call-done.refs_1_), custom_call_target="tpu_custom_call" | custom-call | flops 1000000000 | bytes 1024 | tf_op jit(solution)/shard_map/grad_mid/pallas_call | solution.py:40
  346.2 17.8 %part_ff.1.refs_3_ = bf16[2048,2816]{1,0:T(8,128)(2,1)} custom-call(bf16[1024,2048]{1,0:T(8,128)(2,1)} %lay.10.refs_0_, bf16[1024,2816]{1,0:T(8,128)(2,1)} %feed_back.1.refs_0_.refs_1_, bf16[128,2048]{1,0:T(8,128)(2,1)} %get-tuple-element.94.refs_2_), custom_call_target="tpu_custom_call" | custom-call | flops 1000000000 | bytes 1024 | tf_op jit(solution)/shard_map/part_ff/pallas_call | solution.py:40
  392.1 11.5 %collective-permute-done.33.refs_5_ = bf16[128,2176]{1,0:T(8,128)(2,1)S(1)} collective-permute-done((bf16[128,2176]{1,0:T(8,128)(2,1)S(1)}, bf16[128,2176]{1,0:T(8,128)(2,1)S(1)}, u32[]{:S(2)}, u32[]{:S(2)}) %collective-permute-start.33) | collective-permute-done | bytes 557088 | tf_op jit(solution)/shard_map/ppermute | solution.py:187
  406.3 10.2 %collective-permute-done.31.refs_3_ = bf16[128,2176]{1,0:T(8,128)(2,1)S(1)} collective-permute-done((bf16[128,2176]{1,0:T(8,128)(2,1)S(1)}, bf16[128,2176]{1,0:T(8,128)(2,1)S(1)}, u32[]{:S(2)}, u32[]{:S(2)}) %collective-permute-start.31) | collective-permute-done | bytes 557088 | tf_op jit(solution)/shard_map/ppermute | solution.py:183
  448.5 9.5 %scan_backward.1 = (f32[8,128,512]{2,1,0:T(8,128)}, f32[8,128,512]{2,1,0:T(8,128)}, f32[8,512]{1,0:T(8,128)}, bf16[8,128,512]{2,1,0:T(8,128)(2,1)}, f32[1,512]{1,0:T(1,128)}) custom-call(f32[8,128,128]{2,1,0:T(8,128)} %convert.1.keep_ref.refs_0_.refs_1_, f32[8,128,1024]{2,1,0:T(8,128)} %bitcast.42, f32[8,128,512]{2,1,0:T(8,128)} %bitcast.54, ...), custom_call_target="tpu_custom_call" | custom-call | flops 1000000000 | bytes 1024 | tf_op jit(solution)/shard_map/scan_backward/pallas_call | solution.py:40
  460.5 16.9 %all-gather.1 = f32[64,512]{1,0:T(8,128)} all-gather(f32[8,512]{1,0:T(8,128)} %get-tuple-element.112), channel_id=3, replica_groups=mesh['grp'=4,'seq'=8] {'seq'}, dimensions={0}, use_global_device_ids=true | all-gather | bytes 147456 | tf_op jit(solution)/shard_map/all_gather | solution.py:1142
  510.5 9.6 %collective-permute-done.42.refs_2_ = bf16[128,2816]{1,0:T(8,128)(2,1)S(1)} collective-permute-done((bf16[128,2816]{1,0:T(8,128)(2,1)S(1)}, bf16[128,2816]{1,0:T(8,128)(2,1)S(1)}, u32[]{:S(2)}, u32[]{:S(2)}) %collective-permute-start.42) | collective-permute-done | bytes 720928 | tf_op jit(solution)/shard_map/ppermute | solution.py:183
  521.0 10.2 %part_pair.1.refs_4_ = bf16[2048,1024]{1,0:T(8,128)(2,1)} custom-call(bf16[1024,2176]{1,0:T(8,128)(2,1)} %lay.8.refs_3_.refs_0_, bf16[1024,1024]{1,0:T(8,128)(2,1)} %bitcast.56, bf16[128,2816]{1,0:T(8,128)(2,1)} %copy-done.11), custom_call_target="tpu_custom_call" | custom-call | flops 1000000000 | bytes 1024 | tf_op jit(solution)/shard_map/part_pair/pallas_call | solution.py:40
  533.1 12.4 %grad_in.1 = (bf16[256,2048]{1,0:T(8,128)(2,1)}, bf16[256,2048]{1,0:T(8,128)(2,1)}, f32[512,2048]{1,0:T(8,128)}) custom-call(bf16[1024,1024]{1,0:T(8,128)(2,1)} %bitcast.57, bf16[1024,512]{1,0:T(8,128)(2,1)} %bitcast.67, bf16[2048,2048]{1,0:T(8,128)(2,1)} %all-gather.6.cloned.1.call-done.refs_1_.refs_2_.refs_3_, ...), custom_call_target="tpu_custom_call" | custom-call | flops 1000000000 | bytes 1024 | tf_op jit(solution)/shard_map/grad_in/pallas_call | solution.py:40
  556.8 31.5 %collective-permute-done.46.refs_4_ = bf16[128,2816]{1,0:T(8,128)(2,1)S(1)} collective-permute-done((bf16[128,2816]{1,0:T(8,128)(2,1)S(1)}, bf16[128,2816]{1,0:T(8,128)(2,1)S(1)}, u32[]{:S(2)}, u32[]{:S(2)}) %collective-permute-start.46) | collective-permute-done | bytes 720928 | tf_op jit(solution)/shard_map/ppermute | solution.py:187
  588.2 14.1 %collective-permute-done.48.refs_6_ = bf16[128,2816]{1,0:T(8,128)(2,1)S(1)} collective-permute-done((bf16[128,2816]{1,0:T(8,128)(2,1)S(1)}, bf16[128,2816]{1,0:T(8,128)(2,1)S(1)}, u32[]{:S(2)}, u32[]{:S(2)}) %collective-permute-start.48) | collective-permute-done | bytes 720928 | tf_op jit(solution)/shard_map/ppermute | solution.py:187
  (396 shorter events, 360.2 us)
Async XLA Ops:
  7.2 104.8 %all-gather.6.cloned.1.call-start = ((), (), s32[]{:S(2)}) async-start(), calls=%async_computation.4 | async-start | bytes 9437184 | tf_op jit(solution)/shard_map/all_gather | solution.py:1070
  11.6 251.5 %all-gather.8.cloned.1.call-start = ((), (), s32[]{:S(2)}) async-start(), calls=%async_computation.5 | async-start | bytes 12976128 | tf_op jit(solution)/shard_map/all_gather | solution.py:1070
  21.9 26.0 %collective-permute-start.1 = (bf16[128,2176]{1,0:T(8,128)(2,1)S(1)}, bf16[128,2176]{1,0:T(8,128)(2,1)S(1)}, u32[]{:S(2)}, u32[]{:S(2)}) collective-permute-start(bf16[128,2176]{1,0:T(8,128)(2,1)S(1)} %get-tuple-element.141.refs_1_), channel_id=1, source_target_pairs={{0,8},{8,0},{16,24},{24,16},{1,9},{9,1},{17,25},{25,17},{2,10},{10... | collective-permute-start | bytes 1671176 | tf_op jit(solution)/shard_map/ppermute | solution.py:183
  69.4 224.0 %all-gather.10.cloned.1.call-start = ((), (), s32[]{:S(2)}) async-start(), calls=%async_computation.6 | async-start | bytes 6488064 | tf_op jit(solution)/shard_map/all_gather | solution.py:1070
  70.4 358.1 %reduce-scatter.5.cloned.1.call-start = ((), (), s32[]{:S(2)}) async-start(), calls=%async_computation.7 | async-start | bytes 6488064 | tf_op jit(solution)/shard_map/reduce_scatter | solution.py:1073
  165.0 27.1 %collective-permute-start.12 = (bf16[256,2176]{1,0:T(8,128)(2,1)}, bf16[256,2176]{1,0:T(8,128)(2,1)S(1)}, u32[]{:S(2)}, u32[]{:S(2)}) collective-permute-start(bf16[256,2176]{1,0:T(8,128)(2,1)} %get-tuple-element.82), channel_id=1, source_target_pairs={{0,8},{8,0},{16,24},{24,16},{1,9},{9,1},{17,25},{25,17},{2,10},{10... | collective-permute-start | bytes 3342344 | tf_op jit(solution)/shard_map/ppermute | solution.py:183
  166.6 26.7 %collective-permute-start.13 = (bf16[256,2176]{1,0:T(8,128)(2,1)}, bf16[256,2176]{1,0:T(8,128)(2,1)S(1)}, u32[]{:S(2)}, u32[]{:S(2)}) collective-permute-start(bf16[256,2176]{1,0:T(8,128)(2,1)} %get-tuple-element.83), channel_id=1, source_target_pairs={{0,16},{16,0},{8,24},{24,8},{1,17},{17,1},{9,25},{25,9},{2,18},{18... | collective-permute-start | bytes 3342344 | tf_op jit(solution)/shard_map/ppermute | solution.py:187
  293.2 207.1 %reduce-scatter.7.cloned.1.call-start = ((), (), s32[]{:S(2)}) async-start(), calls=%async_computation.8 | async-start | bytes 12976128 | tf_op jit(solution)/shard_map/reduce_scatter | solution.py:1073
  305.7 36.2 %collective-permute-start.23 = (bf16[256,2048]{1,0:T(8,128)(2,1)}, bf16[256,2048]{1,0:T(8,128)(2,1)S(1)}, u32[]{:S(2)}, u32[]{:S(2)}) collective-permute-start(bf16[256,2048]{1,0:T(8,128)(2,1)} %get-tuple-element.90), channel_id=1, source_target_pairs={{0,16},{16,0},{8,24},{24,8},{1,17},{17,1},{9,25},{25,9},{2,18},{18... | collective-permute-start | bytes 3145736 | tf_op jit(solution)/shard_map/ppermute | solution.py:187
  306.6 35.3 %collective-permute-start.22 = (bf16[256,2048]{1,0:T(8,128)(2,1)}, bf16[256,2048]{1,0:T(8,128)(2,1)S(1)}, u32[]{:S(2)}, u32[]{:S(2)}) collective-permute-start(bf16[256,2048]{1,0:T(8,128)(2,1)} %get-tuple-element.89.refs_4_), channel_id=1, source_target_pairs={{0,8},{8,0},{16,24},{24,16},{1,9},{9,1},{17,25},{25,17},{2,10},{10... | collective-permute-start | bytes 3145736 | tf_op jit(solution)/shard_map/ppermute | solution.py:183
  364.0 253.7 %reduce-scatter.11.cloned.1.call-start = ((), (), s32[]{:S(2)}) async-start(), calls=%async_computation.10 | async-start | bytes 4718592 | tf_op jit(solution)/shard_map/reduce_scatter | solution.py:1073
  390.7 25.8 %collective-permute-start.31 = (bf16[128,2176]{1,0:T(8,128)(2,1)S(1)}, bf16[128,2176]{1,0:T(8,128)(2,1)S(1)}, u32[]{:S(2)}, u32[]{:S(2)}) collective-permute-start(bf16[128,2176]{1,0:T(8,128)(2,1)S(1)} %get-tuple-element.139.refs_1_), channel_id=1, source_target_pairs={{0,8},{8,0},{16,24},{24,16},{1,9},{9,1},{17,25},{25,17},{2,10},{10... | collective-permute-start | bytes 1671176 | tf_op jit(solution)/shard_map/ppermute | solution.py:183
  429.6 29.4 %collective-permute-start.36 = (bf16[96,2048]{1,0:T(8,128)(2,1)S(1)}, bf16[96,2048]{1,0:T(8,128)(2,1)S(1)}, u32[]{:S(2)}, u32[]{:S(2)}) collective-permute-start(bf16[96,2048]{1,0:T(8,128)(2,1)S(1)} %slice.75.refs_0_), channel_id=1, source_target_pairs={{0,8},{8,0},{16,24},{24,16},{1,9},{9,1},{17,25},{25,17},{2,10},{10... | collective-permute-start | bytes 1179656 | tf_op jit(solution)/shard_map/ppermute | solution.py:183
  433.3 26.8 %collective-permute-start.37 = (bf16[80,2048]{1,0:T(8,128)(2,1)S(1)}, bf16[80,2048]{1,0:T(8,128)(2,1)S(1)}, u32[]{:S(2)}, u32[]{:S(2)}) collective-permute-start(bf16[80,2048]{1,0:T(8,128)(2,1)S(1)} %slice.76.refs_1_), channel_id=1, source_target_pairs={{0,8},{8,0},{16,24},{24,16},{1,9},{9,1},{17,25},{25,17},{2,10},{10... | collective-permute-start | bytes 983048 | tf_op jit(solution)/shard_map/ppermute | solution.py:183
  439.2 42.7 %collective-permute-start.24 = (bf16[128,2048]{1,0:T(8,128)(2,1)S(1)}, bf16[128,2048]{1,0:T(8,128)(2,1)S(1)}, u32[]{:S(2)}, u32[]{:S(2)}) collective-permute-start(bf16[128,2048]{1,0:T(8,128)(2,1)S(1)} %copy-done.46), channel_id=1, source_target_pairs={{0,16},{16,0},{8,24},{24,8},{1,17},{17,1},{9,25},{25,9},{2,18},{18... | collective-permute-start | bytes 1572872 | tf_op jit(solution)/shard_map/ppermute | solution.py:187
  440.3 41.6 %collective-permute-start.25 = (bf16[128,2048]{1,0:T(8,128)(2,1)S(1)}, bf16[128,2048]{1,0:T(8,128)(2,1)S(1)}, u32[]{:S(2)}, u32[]{:S(2)}) collective-permute-start(bf16[128,2048]{1,0:T(8,128)(2,1)S(1)} %copy-done.84), channel_id=1, source_target_pairs={{0,8},{8,0},{16,24},{24,16},{1,9},{9,1},{17,25},{25,17},{2,10},{10... | collective-permute-start | bytes 1572872 | tf_op jit(solution)/shard_map/ppermute | solution.py:183
  500.1 148.3 %reduce-scatter.9.cloned.1.call-start = ((), (), s32[]{:S(2)}) async-start(), calls=%async_computation.9 | async-start | bytes 4718592 | tf_op jit(solution)/shard_map/reduce_scatter | solution.py:1073
  545.6 63.7 %collective-permute-start.44 = (bf16[256,2048]{1,0:T(8,128)(2,1)}, bf16[256,2048]{1,0:T(8,128)(2,1)S(1)}, u32[]{:S(2)}, u32[]{:S(2)}) collective-permute-start(bf16[256,2048]{1,0:T(8,128)(2,1)} %get-tuple-element.120), channel_id=1, source_target_pairs={{0,16},{16,0},{8,24},{24,8},{1,17},{17,1},{9,25},{25,9},{2,18},{18... | collective-permute-start | bytes 3145736 | tf_op jit(solution)/shard_map/ppermute | solution.py:187
  546.9 62.4 %collective-permute-start.43 = (bf16[256,2048]{1,0:T(8,128)(2,1)}, bf16[256,2048]{1,0:T(8,128)(2,1)S(1)}, u32[]{:S(2)}, u32[]{:S(2)}) collective-permute-start(bf16[256,2048]{1,0:T(8,128)(2,1)} %get-tuple-element.119.refs_2_.refs_8_), channel_id=1, source_target_pairs={{0,8},{8,0},{16,24},{24,16},{1,9},{9,1},{17,25},{25,17},{2,10},{10... | collective-permute-start | bytes 3145736 | tf_op jit(solution)/shard_map/ppermute | solution.py:183
  547.7 40.5 %collective-permute-start.46 = (bf16[128,2816]{1,0:T(8,128)(2,1)S(1)}, bf16[128,2816]{1,0:T(8,128)(2,1)S(1)}, u32[]{:S(2)}, u32[]{:S(2)}) collective-permute-start(bf16[128,2816]{1,0:T(8,128)(2,1)S(1)} %copy-done.10), channel_id=1, source_target_pairs={{0,16},{16,0},{8,24},{24,8},{1,17},{17,1},{9,25},{25,9},{2,18},{18... | collective-permute-start | bytes 2162696 | tf_op jit(solution)/shard_map/ppermute | solution.py:187
  550.3 52.0 %collective-permute-start.48 = (bf16[128,2816]{1,0:T(8,128)(2,1)S(1)}, bf16[128,2816]{1,0:T(8,128)(2,1)S(1)}, u32[]{:S(2)}, u32[]{:S(2)}) collective-permute-start(bf16[128,2816]{1,0:T(8,128)(2,1)S(1)} %copy-done.12), channel_id=1, source_target_pairs={{0,16},{16,0},{8,24},{24,8},{1,17},{17,1},{9,25},{25,9},{2,18},{18... | collective-permute-start | bytes 2162696 | tf_op jit(solution)/shard_map/ppermute | solution.py:187
  551.7 50.6 %collective-permute-start.49 = (bf16[128,2816]{1,0:T(8,128)(2,1)S(1)}, bf16[128,2816]{1,0:T(8,128)(2,1)S(1)}, u32[]{:S(2)}, u32[]{:S(2)}) collective-permute-start(bf16[128,2816]{1,0:T(8,128)(2,1)S(1)} %collective-permute-done.47.refs_5_), channel_id=1, source_target_pairs={{0,8},{8,0},{16,24},{24,16},{1,9},{9,1},{17,25},{25,17},{2,10},{10... | collective-permute-start | bytes 2162696 | tf_op jit(solution)/shard_map/ppermute | solution.py:183
  651.7 31.3 %collective-permute-start.61 = (bf16[128,1024]{1,0:T(8,128)(2,1)S(1)}, bf16[128,1024]{1,0:T(8,128)(2,1)S(1)}, u32[]{:S(2)}, u32[]{:S(2)}) collective-permute-start(bf16[128,1024]{1,0:T(8,128)(2,1)S(1)} %get-tuple-element.149.refs_1_), channel_id=1, source_target_pairs={{0,16},{16,0},{8,24},{24,8},{1,17},{17,1},{9,25},{25,9},{2,18},{18... | collective-permute-start | bytes 786440 | tf_op jit(solution)/shard_map/ppermute | solution.py:187
  652.6 31.3 %collective-permute-start.58 = (bf16[128,1024]{1,0:T(8,128)(2,1)S(1)}, bf16[128,1024]{1,0:T(8,128)(2,1)S(1)}, u32[]{:S(2)}, u32[]{:S(2)}) collective-permute-start(bf16[128,1024]{1,0:T(8,128)(2,1)S(1)} %get-tuple-element.150.refs_0_), channel_id=1, source_target_pairs={{0,8},{8,0},{16,24},{24,16},{1,9},{9,1},{17,25},{25,17},{2,10},{10... | collective-permute-start | bytes 786440 | tf_op jit(solution)/shard_map/ppermute | solution.py:183
  (141 other events, 1938.2 us)
Sparse Core Ops, SparseCore 0:
  11.7 84.6 all-gather.5
  98.7 107.5 all-gather.7
  208.0 58.7 all-gather.9
  293.3 65.9 reduce-scatter.4
  364.1 121.5 reduce-scatter.6
  500.3 50.3 reduce-scatter.10
  553.5 48.1 reduce-scatter.8

commit v3 on v2

--- a/solution.py
+++ b/solution.py
@@ -1,3 +1,4 @@
+import math
 from functools import partial
 
 import jax
@@ -18,10 +19,11 @@
 SWAP_Y = [(0, 2), (2, 0), (1, 3), (3, 1)]
 TO_X, TO_Y, KEPT = (2, 6), (5, 7), (0, 1, 3, 4)
 VMEM_LIMIT = 56 * 1024 * 1024
+PLACE_STEP = 32
 NN = (((1,), (0,)), ((), ()))
 NT = (((1,), (1,)), ((), ()))
 TN = (((0,), (0,)), ((), ()))
-COSTS = {"finish_mid": 200}
+COSTS = {"finish_in": 67}
 SMALL = pl.CostEstimate(flops=1024, bytes_accessed=1024, transcendentals=0)
 ANY = pl.BlockSpec(memory_space=pl.ANY)
 SMEM = pl.BlockSpec(memory_space=pltpu.SMEM)
@@ -47,7 +49,7 @@
         compiler_params=pltpu.CompilerParams(vmem_limit_bytes=VMEM_LIMIT),
         input_output_aliases=aliases or {},
         cost_estimate=pl.CostEstimate(
-            flops=COSTS.get(name, 1) * 1_000_000_000, bytes_accessed=1024, transcendentals=0
+            flops=1024 + COSTS.get(name, 0) * 1_000_000_000, bytes_accessed=1024, transcendentals=0
         ),
         name=name,
     )(*args, *deps)
@@ -134,7 +136,7 @@
     return call(body, name, grid, specs, out_spec, shape((rows, wide), BF16), (lhs_arr, rhs_arr), deps)
 
 
-def outer_gate_out(normed, grad_gate, mix, grad_mix, parts, wide, deps=()):
+def outer_gate_out(normed, grad_gate, mix, grad_mix, parts, wide, deps, between):
     depth, own = mix.shape
     count = own // parts
     turns = wide // own
@@ -156,6 +158,8 @@
         deps,
     ).reshape(wide, 2 * own)
 
+    middle = between((half_done,))
+
     def left(lhs_ref, rhs_ref, _, out_ref):
         out_ref[...] = dot(lhs_ref[...], rhs_ref[...], TN).astype(BF16)
 
@@ -171,8 +175,9 @@
         pl.BlockSpec((own, own), lambda j: (j, 0)),
         shape((wide, 2 * own), BF16),
         (normed, grad_gate, half_done),
+        middle,
         aliases={2: 0},
-    )
+    ), middle
 
 
 def after(value, *events):
@@ -223,22 +228,24 @@
 
 
 def start_gather(own):
+    return own, send_x(own), send_y(own)
+
+
+def second_step(held, hold=()):
+    own, by_x, by_y = held
     half = own.shape[0] // 2 if own.shape[0] % 16 else (own.shape[0] + 16) // 32 * 16
-    top, low = own[:half], own[half:]
-    x_top, y_low = send_x(top), send_y(low)
-    x_low, y_top = send_x(low), send_y(top)
-    return (top, low, x_top, x_low, y_top, y_low), x_top
+    x_on, y_on = by_x[:half], by_y[half:]
+    if hold:
+        x_on, y_on = after((x_on, y_on), hold)
+    return own, by_x, by_y, send_y(x_on), send_x(y_on)
 
 
 def end_gather(held, deps=(), hold=()):
-    top, low, x_top, x_low, y_top, y_low = held
-    x_on, y_on = (x_top, y_low) if not hold else after((x_top, y_low), hold)
-    across_top, across_low = send_y(x_on), send_x(y_on)
-    return lay((top, low, x_top, x_low, y_top, y_low, across_top, across_low), deps)
+    return lay(second_step(held, hold), deps)
 
 
 def gather_rows(own, deps=(), hold=()):
-    return end_gather(start_gather(own)[0], deps, hold)
+    return end_gather(start_gather(own), deps, hold)
 
 
 def sum_everywhere(value):
@@ -250,11 +257,6 @@
         value = value + lax.ppermute(value, "seq", [(one, one ^ step) for one in range(count)])
         step *= 2
     return value
-
-
-def gather_blocks(own, deps=(), hold=()):
-    held, came = start_gather(own)
-    return end_gather(held, deps, hold).reshape((GRP,) + own.shape), came
 
 
 def split(column):
@@ -458,7 +460,7 @@
     return back, jnp.sum(weighted * scale, axis=0, keepdims=True)
 
 
-def finish_mid(pieces, middle, cotangent, raw, scale, scale_mid, gain, width):
+def finish_mid(pieces, middle, cotangent, raw, scale, scale_mid, gain, width, deps=()):
     rows = middle.shape[0]
     half = rows // 2
     step = min(half, 64)
@@ -492,6 +494,7 @@
         [block, own_block(step, count, width + LANE), row],
         [shape((rows, width), F32), shape((rows, width + LANE), BF16), shape((1, width), F32)],
         tuple(pieces) + (middle, cotangent, raw, scale, scale_mid, gain),
+        deps,
     )
 
 
@@ -608,11 +611,6 @@
         (cot, weights, by_gate, by_up),
         deps,
     )
-
-
-def by_relation(values, mine):
-    values = jnp.where(mine % 2 == 1, values[jnp.array([1, 0, 3, 2])], values)
-    return jnp.where(mine // 2 == 1, values[jnp.array([2, 3, 0, 1])], values)
 
 
 def pick_columns(mine, matrices, parts, spread, deps=()):
@@ -696,14 +694,62 @@
     )
 
 
-def place_columns(mine, blocks, parts, count, own, spread):
-    _, rows, _ = blocks.shape
+def take_out(first, parts, own, deps=()):
+    wide = GRP * own
+
+    def body(first_ref, out_ref):
+        out_ref[...] = first_ref[...].reshape(own, own)
+
+    return call(
+        body,
+        "take_out",
+        (GRP,),
+        [pl.BlockSpec((parts, own // parts, own), lambda j: (0, j, 3))],
+        pl.BlockSpec((own, own), lambda j: (0, j)),
+        shape((own, wide), BF16),
+        (first,),
+        deps,
+    )
+
+
+def piece_blocks(pieces, step, wide, column=None):
+    own, _, _, top, _ = pieces
+    tops = top.shape[0] // step
+    at = (lambda *i: 0) if column is None else (lambda *i: column(i[0]))
+    block = pl.BlockSpec((step, wide), lambda *i: (i[-1], at(*i)))
+    return [
+        block,
+        block,
+        block,
+        pl.BlockSpec((step, wide), lambda *i: (jnp.minimum(i[-1], tops - 1), at(*i))),
+        pl.BlockSpec((step, wide), lambda *i: (jnp.maximum(i[-1] - tops, 0), at(*i))),
+    ]
+
+
+def collect(refs, held_ref, axis, tops):
+    for index in range(3):
+        held_ref[index] = refs[index][...]
+
+    @pl.when(pl.program_id(axis) < tops)
+    def _():
+        held_ref[3] = refs[3][...]
+
+    @pl.when(pl.program_id(axis) >= tops)
+    def _():
+        held_ref[3] = refs[4][...]
+
+
+def place_columns(mine, pieces, parts, count, own, spread, deps=()):
+    rows = pieces[0].shape[0]
     piece = own // parts
-    step = min(rows, 32)
-
-    def body(mine_ref, blocks_ref, *out_refs):
+    step = min(pieces[3].shape[0], PLACE_STEP)
+    tops = pieces[3].shape[0] // step
+
+    def body(mine_ref, *refs):
+        out_refs, held_ref = refs[5:-1], refs[-1]
+        collect(refs, held_ref, 0, tops)
         for which in range(GRP):
-            block = blocks_ref[mine_ref[0] ^ which].astype(F32)
+            block = held_ref[mine_ref[0] ^ which].astype(F32)
             for index, out_ref in enumerate(out_refs):
                 if spread:
                     turns = [
@@ -717,19 +763,17 @@
                     at = (part * GRP + which) * piece
                     out_ref[:, at : at + piece] = mat[:, part * piece : (part + 1) * piece]
 
-    return pl.pallas_call(
-        body,
-        grid=(rows // step,),
-        in_specs=[
-            pl.BlockSpec(memory_space=pltpu.SMEM),
-            pl.BlockSpec((GRP, step, own * count), lambda i: (0, i, 0)),
-        ],
-        out_specs=[pl.BlockSpec((step, own * GRP), lambda i: (i, 0))] * count,
-        out_shape=[jax.ShapeDtypeStruct((rows, own * GRP), F32)] * count,
-        compiler_params=pltpu.CompilerParams(vmem_limit_bytes=VMEM_LIMIT),
-        cost_estimate=SMALL,
-        name="place_columns",
-    )(mine.reshape(1), blocks)
+    return call(
+        body,
+        "place_columns",
+        (rows // step,),
+        [SMEM] + piece_blocks(pieces, step, own * count),
+        [pl.BlockSpec((step, own * GRP), lambda i: (i, 0))] * count,
+        [shape((rows, own * GRP), F32)] * count,
+        (mine.reshape(1),) + tuple(pieces),
+        deps,
+        [pltpu.VMEM((GRP, step, own * count), BF16)],
+    )
 
 
 def scan_forward(keep, proj, bias):
@@ -795,12 +839,36 @@
     )(keep, proj, bias)
 
 
-def entering_state(info_ref, ends_ref, parts, backward):
+def all_ends(ends, parts):
+    if parts > 8:
+        return lax.all_gather(ends, "seq"), ends
+    even = lax.axis_index("seq") % 2 == 0
+    other = lax.ppermute(ends, "seq", [(one, one ^ 1) for one in range(parts)])
+    chip = jnp.concatenate([jnp.where(even, ends, other), jnp.where(even, other, ends)])
+    chips = [chip] + [
+        lax.ppermute(chip, "seq", [(one, (one + step) % parts) for one in range(parts)])
+        for step in range(2, parts, 2)
+    ]
+    return jnp.concatenate(chips).reshape((parts,) + ends.shape), chip
+
+
+def entering_state(info_ref, ends_ref, parts, backward, ordered):
     here = info_ref[0]
+    steps = []
+    if ordered or parts > 8:
+        for place in range(parts - 1, 0, -1) if backward else range(parts - 1):
+            steps.append((place, place > here if backward else place < here))
+    else:
+        chips, chip, core = parts // 2, here // 2, here % 2
+        for away in range(chips - 1, 0, -1):
+            at = chips - away if backward else away
+            for one in (1, 0) if backward else (0, 1):
+                steps.append((2 * at + one, chip + away < chips if backward else chip >= away))
+        steps.append((1, core == 0) if backward else (0, core == 1))
     state = jnp.zeros((GRP, LANE), F32)
-    for place in range(parts - 1, 0, -1) if backward else range(parts - 1):
-        longer = ends_ref[place, GRP:, :] + ends_ref[place, :GRP, :] * state
-        state = jnp.where(place > here if backward else place < here, longer, state)
+    for at, counts in steps:
+        longer = ends_ref[at, GRP:, :] + ends_ref[at, :GRP, :] * state
+        state = jnp.where(counts, longer, state)
     return state
 
 
@@ -809,7 +877,7 @@
     count = ends.shape[0]
 
     def body(info_ref, ends_ref, prod_ref, state_ref, proj_ref, gain_ref, states_ref, mix_ref, squares_ref, enter_ref):
-        entering = entering_state(info_ref, ends_ref, count, False)
+        entering = entering_state(info_ref, ends_ref, count, False, False)
         enter_ref[...] = entering
 
         @pl.when(pl.program_id(0) == 0)
@@ -944,7 +1012,7 @@
     parts = ends.shape[0]
 
     def body(info_ref, keep_ref, ends_ref, prod_ref, grad_ref, proj_ref, bias_ref, states_ref, enter_ref, out_ref, sum_ref):
-        entering = entering_state(info_ref, ends_ref, parts, True)
+        entering = entering_state(info_ref, ends_ref, parts, True, True)
         first = lax.broadcasted_iota(jnp.int32, (half, LANE), 0) == 0
         bias_sum = jnp.zeros((1, LANE), F32)
         for owner in range(GRP):
@@ -993,40 +1061,67 @@
     )
 
 
-def place_rows(mine, blocks, deps=()):
-    _, rows, wide = blocks.shape
-
-    def body(mine_ref, blocks_ref, out_ref):
-        out_ref[0] = blocks_ref[mine_ref[0] ^ pl.program_id(0)].astype(F32)
+def place_rows(mine, pieces, deps=()):
+    rows, wide = pieces[0].shape
+    if rows % 16:
+        pieces = lay(pieces, deps).reshape(GRP, rows, wide)
+
+        def from_laid(mine_ref, pieces_ref, out_ref):
+            out_ref[0] = pieces_ref[mine_ref[0] ^ pl.program_id(0)].astype(F32)
+
+        return call(
+            from_laid,
+            "place_rows",
+            (GRP,),
+            [SMEM, whole_block(pieces)],
+            pl.BlockSpec((1, rows, wide), lambda j: (j, 0, 0)),
+            shape((GRP, rows, wide), F32),
+            (mine.reshape(1), pieces),
+        ).reshape(GRP * rows, wide)
+
+    step = math.gcd(rows, pieces[3].shape[0])
+    tops = pieces[3].shape[0] // step
+
+    def body(mine_ref, *refs):
+        out_ref, held_ref = refs[5:]
+        collect(refs, held_ref, 0, tops)
+        for which in range(GRP):
+            out_ref[which] = held_ref[mine_ref[0] ^ which].astype(F32)
 
     return call(
         body,
         "place_rows",
-        (GRP,),
-        [SMEM, whole_block(blocks)],
-        pl.BlockSpec((1, rows, wide), lambda j: (j, 0, 0)),
+        (rows // step,),
+        [SMEM] + piece_blocks(pieces, step, wide),
+        pl.BlockSpec((GRP, step, wide), lambda i: (0, i, 0)),
         shape((GRP, rows, wide), F32),
-        (mine.reshape(1), blocks),
-        deps,
+        (mine.reshape(1),) + tuple(pieces),
+        deps,
+        [pltpu.VMEM((GRP, step, wide), BF16)],
     ).reshape(GRP * rows, wide)
 
 
-def place_stacked(mine, blocks, first, own):
-    _, rows, wide = blocks.shape
+def place_stacked(mine, pieces, first, own, deps=()):
+    rows = pieces[0].shape[0]
     count = rows // GRP
-
-    def body(mine_ref, blocks_ref, out_ref):
+    tops = pieces[3].shape[0] // count
+
+    def body(mine_ref, *refs):
+        out_ref, held_ref = refs[5:]
+        collect(refs, held_ref, 0, tops)
         for which in range(GRP):
-            out_ref[which * count : (which + 1) * count, :] = blocks_ref[mine_ref[0] ^ which].astype(F32)
+            out_ref[which * count : (which + 1) * count, :] = held_ref[mine_ref[0] ^ which].astype(F32)
 
     return call(
         body,
         "place_stacked",
         (GRP,),
-        [SMEM, pl.BlockSpec((GRP, count, own), lambda j: (0, j, first // own))],
+        [SMEM] + piece_blocks(pieces, count, own, lambda i: first // own),
         pl.BlockSpec((rows, own), lambda j: (0, j)),
         shape((rows, GRP * own), F32),
-        (mine.reshape(1), blocks),
+        (mine.reshape(1),) + tuple(pieces),
+        deps,
+        [pltpu.VMEM((GRP, count, own), BF16)],
     )
 
 
@@ -1081,16 +1176,20 @@
 
     w_first = whole(pick_first(mine, input_proj, forget_proj, gate_proj, out_proj, parts))
     normed = norm_in(tokens, starts, in_gain, width)
-    normed = gather_rows(normed)
+    cot_held = start_gather(cotangent)
+    held = start_gather(normed)
     ff_cols = pick_columns(mine, (mlp_gate, mlp_up), parts, True, (normed,))
     w_ff = whole(ff_cols)
     w_down = whole(own_rows(mlp_down))
-    cot = gather_rows(after(cotangent, normed), deps=(ff_cols,))
+    normed = end_gather(held, (ff_cols,))
+    cot_pieces = second_step(cot_held)
     keep = normed[:, width:].astype(F32).reshape(8, half, LANE)
 
-    proj = product("proj_pair", normed, w_first, width, 0, 2 * own, 256, (cot,)).reshape(8, half, 2 * own)
+    proj = product("proj_pair", normed, w_first, width, 0, 2 * own, 256, cot_pieces).reshape(
+        8, half, 2 * own
+    )
     prod, state, ends = scan_forward(keep, proj, bias)
-    ends = lax.all_gather(ends, "seq")
+    ends, _ = all_ends(ends, parts)
     proj_gate = product("proj_gate", normed, w_first, width, 2 * own, own, 256, (prod,))
     proj_gate = proj_gate.reshape(8, half, own)
     states, mix, squares, enter = finish_forward(info, ends, prod, state, proj_gate, gain)
@@ -1100,34 +1199,40 @@
         "mix", NN, (mix,), (w_stacked,), own, squares, stacked=(width, parts, 3 * own)
     )
     by_x, by_y = send_x(to_x), send_y(to_y)
-    for_y, for_x = merge("mix_merge", kept, by_x, by_y, squares)
+    w_out = take_out(w_stacked, parts, own, (to_x,))
+    cot = lay(cot_pieces, (w_out,))
+    for_y, for_x = merge("mix_merge", kept, by_x, by_y, squares, (cot,))
     pieces = (kept, by_x, by_y, send_y(for_y), send_x(for_x), squares)
     middle, normed_mid, raw, scale_state, scale_mid = finish_mix(pieces, tokens, mid_gain, width)
     normed_mid = gather_rows(normed_mid)
-    w_out = w_stacked[:, :, 3 * own :].reshape(parts, GRP, -1, own).transpose(0, 2, 1, 3)
-    w_out = w_out.reshape(own, width)
-
     hidden, by_gate, by_up = feed_forward(normed_mid, w_ff)
     part_down = outer_sum("part_down", hidden, cot, hidden.shape[1], width, -512)
     sum_down = reduced(part_down)
 
-    to_x, to_y, kept_out = partial_sums("down", NN, (hidden,), (w_down,), 256, deps=(part_down,))
-    by_x_out, by_y_out = send_x(to_x), send_y(to_y)
-    grad_ff = feed_back(cot, w_down, by_gate, by_up, (to_x,))
-    to_x, to_y, kept = partial_sums("grad_mid", NT, (grad_ff,), (w_ff,), 256)
+    grad_ff = feed_back(cot, w_down, by_gate, by_up, (part_down,))
+    part_ff = outer_sum("part_ff", normed_mid, grad_ff, width, grad_ff.shape[1], 256)
+    sum_ff = reduced(part_ff)
+    to_x, to_y, kept = partial_sums("grad_mid", NT, (grad_ff,), (w_ff,), 256, deps=(part_ff,))
     by_x, by_y = send_x(to_x), send_y(to_y)
-    out_for_y, out_for_x = merge("down_merge", kept_out, by_x_out, by_y_out, deps=(to_x,))
-    out_last_y, out_last_x = send_y(out_for_y), send_x(out_for_x)
-    part_ff = outer_sum("part_ff", normed_mid, grad_ff, width, grad_ff.shape[1], 256, (out_for_y,))
-    sum_ff = reduced(part_ff)
-    for_y, for_x = merge("grad_mid_merge", kept, by_x, by_y, deps=(part_ff,))
+    for_y, for_x = merge("grad_mid_merge", kept, by_x, by_y)
     pieces = (kept, by_x, by_y, send_y(for_y), send_x(for_x))
     grad_middle, scaled_mix, grad_mlp_gain = finish_mid(
-        pieces, middle, cotangent, raw, scale_state, scale_mid, mid_gain, width
-    )
-    pieces_out = (kept_out, by_x_out, by_y_out, out_last_y, out_last_x)
-    grad_mix = gather_rows(scaled_mix)
-
+        pieces,
+        middle,
+        cotangent,
+        raw,
+        scale_state,
+        scale_mid,
+        mid_gain,
+        width,
+    )
+    held = start_gather(scaled_mix)
+    to_x, to_y, kept_out = partial_sums("down", NN, (hidden,), (w_down,), 256, deps=(scaled_mix,))
+    grad_mix = end_gather(held, (to_x,))
+
+    to_x, to_y = after((to_x, to_y), grad_mix)
+    by_x_out, by_y_out = send_x(to_x), send_y(to_y)
+    held_down = start_gather(after(sum_down, grad_mix))
     back, coupling = product_back("back", grad_mix, w_out, 256)
     after_prod, local, ends_back, grad_gate, gain_sum = scan_backward(
         keep,
@@ -1139,46 +1244,57 @@
         back.reshape(8, half, own),
         coupling.reshape(8, half, LANE),
     )
-    ends_back = lax.all_gather(ends_back, "seq")
-    blocks_down, _ = gather_blocks(after(sum_down, grad_mix), (ends_back,), (after_prod,))
-    block_out = add_scattered(pieces_out, middle, BF16, width, (blocks_down,))
     grad_gate = grad_gate.reshape(plane, own)
-    part_gate_out = outer_gate_out(normed, grad_gate, mix, grad_mix, parts, width, (block_out,))
+    out_sends = []
+
+    def between(deps):
+        out_sends.extend(merge("down_merge", kept_out, by_x_out, by_y_out, None, deps))
+        return out_sends[0], held_down[1], held_down[2]
+
+    part_gate_out, _ = outer_gate_out(
+        normed, grad_gate, mix, grad_mix, parts, width, (after_prod,), between
+    )
     sum_gate_out = reduced(part_gate_out)
+    out_last_y, out_last_x = send_y(out_sends[0]), send_x(out_sends[1])
+    pieces_out = (kept_out, by_x_out, by_y_out, out_last_y, out_last_x)
+    ends_back = lax.all_gather(after(ends_back, part_gate_out), "seq")
     grad_pair, bias_sum = finish_backward(
         info, keep, ends_back, after_prod, local, proj, bias, states, enter, (part_gate_out,)
     )
     grad_pair = grad_pair.reshape(plane, 2 * own)
-    held, came_ff = start_gather(after(sum_ff, blocks_down))
-    part_pair = outer_sum("part_pair", normed, grad_pair, width, 2 * own, 256, (came_ff,))
+    held_ff = start_gather(after(sum_ff, part_gate_out))
+    to_x, to_y, kept = partial_sums(
+        "grad_in", NT, (grad_pair, grad_gate), (w_first, w_first), 256, firsts=(0, 2 * own)
+    )
+    by_x, by_y = send_x(to_x), send_y(to_y)
+    part_pair = outer_sum("part_pair", normed, grad_pair, width, 2 * own, 256, (to_x,))
     sum_pair = reduced(part_pair)
-    to_x, to_y, kept = partial_sums(
-        "grad_in",
-        NT,
-        (grad_pair, grad_gate),
-        (w_first, w_first),
-        256,
-        deps=(part_pair,),
-        firsts=(0, 2 * own),
-    )
-    by_x, by_y = send_x(to_x), send_y(to_y)
-    blocks_ff = end_gather(held, (to_x,), (grad_pair,)).reshape((GRP,) + sum_ff.shape)
-    grad_down = place_rows(mine, blocks_down, (to_x,))
-    for_y, for_x = merge("grad_in_merge", kept, by_x, by_y, deps=(grad_down, blocks_ff))
+    block_out = add_scattered(
+        pieces_out, middle, BF16, width, (part_pair, held_ff[1], held_ff[2])
+    )
+    grad_down = place_rows(mine, second_step(held_down), (block_out,))
+    for_y, for_x = merge("grad_in_merge", kept, by_x, by_y, deps=(grad_down,))
     last_y, last_x = send_y(for_y), send_x(for_x)
     pieces = (kept, by_x, by_y, last_y, last_x)
-    grad_tokens, grad_norm_gain = finish_in(pieces, tokens, grad_middle, in_gain, width)
+    held_go = start_gather(after(sum_gate_out, held_ff[1], held_ff[2]))
+    grad_mlp_gate, grad_mlp_up = place_columns(
+        mine, second_step(held_ff), parts, 2, w_ff.shape[1] // 2, True, (for_y,)
+    )
+    grad_tokens, grad_norm_gain = finish_in(
+        pieces, tokens, grad_middle, in_gain, width, (grad_mlp_up, held_go[1], held_go[2])
+    )
     vectors = sum_everywhere(
         jnp.stack(
             [grad_norm_gain[0], all_features(bias_sum), all_features(gain_sum), grad_mlp_gain[0]]
         )
     )
-    blocks_gate_out, came = gather_blocks(after(sum_gate_out, by_y))
-    grad_mlp_gate, grad_mlp_up = place_columns(mine, blocks_ff, parts, 2, w_ff.shape[1] // 2, True)
-    (grad_gate_proj,) = place_columns(mine, blocks_gate_out, parts, 1, own, True)
-    grad_out = place_stacked(mine, blocks_gate_out, own, own)
-    blocks_pair, _ = gather_blocks(after(sum_pair, came), (grad_mlp_gate, grad_gate_proj, grad_out))
-    grad_input, grad_forget = place_columns(mine, blocks_pair, parts, 2, own, True)
+    held_pair = start_gather(after(sum_pair, held_go[1], held_go[2]))
+    gate_out_pieces = second_step(held_go)
+    (grad_gate_proj,) = place_columns(mine, gate_out_pieces, parts, 1, own, True)
+    grad_out = place_stacked(mine, gate_out_pieces, own, own, (grad_gate_proj,))
+    grad_input, grad_forget = place_columns(
+        mine, second_step(held_pair), parts, 2, own, True, (grad_out, vectors)
+    )
     return (
         block_out,
         grad_tokens,

time: 713 us -> 655 us (0.919)
  blocking collectives: 34.2 us -> 15.9 us
  starting transfers between devices: 77.4 us -> 60.5 us
  local copies, waits for them, and re-layouts: 36.7 us -> 25.3 us
  Pallas kernels: 300 us -> 292 us
    ppermute x33 -> x25, waiting for transfers between devices: 124 us -> 57 us  [send_y(): return lax.ppermute(value, 'grp', SWAP_Y)]
    ppermute x33 -> x25, waiting for transfers between devices: 118 us -> 165 us  [send_x(): return lax.ppermute(value, 'grp', SWAP_X)]
    pallas_call x3 -> x0, Pallas kernels: 21.6 us -> none  [place_columns(): pl.pallas_call(body, grid=(rows // step,), in_specs=[pl.BlockSpec(memory_...]
    all_gather x2 -> x1, blocking collectives: 34.2 us -> 15.9 us  [on_device(): ends_back = lax.all_gather(after(ends_back, part_gate_out), 'seq')]
    pallas_call x38, Pallas kernels: 270 us -> 284 us  [call(): pl.pallas_call(wrapped, grid=grid, in_specs=list(in_specs) + [ANY] * n_de...]
    ppermute x33 -> x25, starting transfers between devices: 36.5 us -> 25.8 us  [send_y(): return lax.ppermute(value, 'grp', SWAP_Y)]
    unnamed x177 -> x108, local copies, waits for them, and re-layouts: 19.5 us -> 11 us
    ppermute x33 -> x25, starting transfers between devices: 35.9 us -> 27.6 us  [send_x(): return lax.ppermute(value, 'grp', SWAP_X)]
  transfers between devices with their start and end apart: 76 -> 64, of which waited for: 32 -> 36; matrix products, arithmetic and copies ran while one was open for 3% -> 3% of each run, Pallas kernels for 40% -> 43%
where the time goes in v3:
time: 655 us; the launch traced here: 650 us
  Pallas kernels  292 us (45%)
  waiting for transfers between devices  236 us (36%)
  starting transfers between devices  60.5 us (9%)
  local copies, waits for them, and re-layouts  25.3 us (4%)
  blocking collectives  15.9 us (2%)
  between operations  14.7 us (2%)
    pallas_call x38, Pallas kernels, call(): pl.pallas_call(wrapped, grid=grid, in_specs=list(in_specs) + [ANY] * n_de...  284 us
    ppermute x25, waiting for transfers between devices, send_x(): return lax.ppermute(value, 'grp', SWAP_X)  165 us
    ppermute x25, waiting for transfers between devices, send_y(): return lax.ppermute(value, 'grp', SWAP_Y)  57 us
    ppermute x25, starting transfers between devices, send_x(): return lax.ppermute(value, 'grp', SWAP_X)  27.6 us
    ppermute x25, starting transfers between devices, send_y(): return lax.ppermute(value, 'grp', SWAP_Y)  25.8 us
    all_gather x1, blocking collectives, on_device(): ends_back = lax.all_gather(after(ends_back, part_gate_out), 'seq')  15.9 us
  transfers between devices with their start and end apart: 64, of which 36 were waited for; matrix products, arithmetic and copies ran while one was open for 3% of the time, Pallas kernels for 43%

profile of v3, /device:TPU:0, one launch (start us, length us, event | category | flops | bytes accessed | tf_op | source)
XLA Modules:
  0.0 650.3 jit_solution(8939120186613435036)
XLA Ops:
  27.3 23.5 %collective-permute-done.refs_1_ = bf16[256,2176]{1,0:T(8,128)(2,1)S(1)} collective-permute-done((bf16[256,2176]{1,0:T(8,128)(2,1)}, bf16[256,2176]{1,0:T(8,128)(2,1)S(1)}, u32[]{:S(2)}, u32[]{:S(2)}) %collective-permute-start) | collective-permute-done | bytes 1114144 | tf_op jit(solution)/shard_map/ppermute | solution.py:188
  56.1 17.2 %collective-permute-done.4.refs_3_.refs_1_ = bf16[256,2048]{1,0:T(8,128)(2,1)S(1)} collective-permute-done((bf16[256,2048]{1,0:T(8,128)(2,1)}, bf16[256,2048]{1,0:T(8,128)(2,1)S(1)}, u32[]{:S(2)}, u32[]{:S(2)}) %collective-permute-start.4) | collective-permute-done | bytes 1048608 | tf_op jit(solution)/shard_map/ppermute | solution.py:188
  79.4 8.1 %collective-permute-done.2.refs_3_ = bf16[128,2176]{1,0:T(8,128)(2,1)} collective-permute-done((bf16[128,2176]{1,0:T(8,128)(2,1)}, bf16[128,2176]{1,0:T(8,128)(2,1)}, u32[]{:S(2)}, u32[]{:S(2)}) %collective-permute-start.2) | collective-permute-done | bytes 557088 | tf_op jit(solution)/shard_map/ppermute | solution.py:192
  98.0 9.1 %proj_pair.1 = f32[1024,1024]{1,0:T(8,128)} custom-call(bf16[1024,2176]{1,0:T(8,128)(2,1)} %lay.4.refs_0_, bf16[2048,2048]{1,0:T(8,128)(2,1)} %all-gather.5.cloned.1.call-done.refs_1_.refs_2_.refs_3_, bf16[256,2048]{1,0:T(8,128)(2,1)} %refs_6_.3, bf16[256,2048]{1,0:T(8,128)(2,1)} %copy-done.4, bf16[256,2048]{1,0:T(8,128)(2,1)} %copy-done.5, ...), custom_call_target="tpu_custom_call" | custom-call | flops 1024 | bytes 1024 | tf_op jit(solution)/shard_map/proj_pair/pallas_call | solution.py:42
  107.1 8.1 %scan_forward.1 = (f32[8,128,512]{2,1,0:T(8,128)}, f32[8,128,512]{2,1,0:T(8,128)}, f32[8,512]{1,0:T(8,128)}) custom-call(f32[8,128,128]{2,1,0:T(8,128)} %convert.1.keep_ref.refs_0_.refs_1_, f32[8,128,1024]{2,1,0:T(8,128)} %bitcast.33, f32[1,512]{1,0:T(1,128)} %reshape.194.bias_ref.refs_3_.refs_6_), custom_call_target="tpu_custom_call" | custom-call | flops 1024 | bytes 1024 | tf_op jit(solution)/shard_map/scan_forward/pallas_call | solution.py:822
  159.1 14.6 %collective-permute-done.12.refs_1_ = bf16[256,2176]{1,0:T(8,128)(2,1)S(1)} collective-permute-done((bf16[256,2176]{1,0:T(8,128)(2,1)}, bf16[256,2176]{1,0:T(8,128)(2,1)S(1)}, u32[]{:S(2)}, u32[]{:S(2)}) %collective-permute-start.12) | collective-permute-done | bytes 1114144 | tf_op jit(solution)/shard_map/ppermute | solution.py:188
  181.2 9.2 %collective-permute-done.14.refs_3_ = bf16[128,2176]{1,0:T(8,128)(2,1)S(1)} collective-permute-done((bf16[128,2176]{1,0:T(8,128)(2,1)}, bf16[128,2176]{1,0:T(8,128)(2,1)S(1)}, u32[]{:S(2)}, u32[]{:S(2)}) %collective-permute-start.14) | collective-permute-done | bytes 557088 | tf_op jit(solution)/shard_map/ppermute | solution.py:192
  200.6 21.2 %collective-permute-done.16.refs_1_ = bf16[256,2048]{1,0:T(8,128)(2,1)S(1)} collective-permute-done((bf16[256,2048]{1,0:T(8,128)(2,1)}, bf16[256,2048]{1,0:T(8,128)(2,1)S(1)}, u32[]{:S(2)}, u32[]{:S(2)}) %collective-permute-start.16) | collective-permute-done | bytes 1048608 | tf_op jit(solution)/shard_map/ppermute | solution.py:188
  237.9 19.9 %feed_forward.1 = (bf16[1024,1408]{1,0:T(8,128)(2,1)}, f32[1024,1408]{1,0:T(8,128)}, f32[1024,1408]{1,0:T(8,128)}) custom-call(bf16[1024,2048]{1,0:T(8,128)(2,1)} %lay.6.refs_0_, bf16[2048,2816]{1,0:T(8,128)(2,1)} %all-gather.7.cloned.1.call-done.refs_1_), custom_call_target="tpu_custom_call" | custom-call | flops 1024 | bytes 1024 | tf_op jit(solution)/shard_map/feed_forward/pallas_call | solution.py:42
  257.8 10.1 %part_down.1.refs_4_ = bf16[1408,2048]{1,0:T(8,128)(2,1)} custom-call(bf16[1024,1408]{1,0:T(8,128)(2,1)} %get-tuple-element.84.refs_0_, bf16[1024,2048]{1,0:T(8,128)(2,1)} %lay.5.refs_4_.refs_1_.refs_0_), custom_call_target="tpu_custom_call" | custom-call | flops 1024 | bytes 1024 | tf_op jit(solution)/shard_map/part_down/pallas_call | solution.py:42
  268.3 14.6 %feed_back.1.refs_1_.refs_0_ = bf16[1024,2816]{1,0:T(8,128)(2,1)} custom-call(bf16[1024,2048]{1,0:T(8,128)(2,1)} %lay.5.refs_4_.refs_1_.refs_0_, bf16[1408,2048]{1,0:T(8,128)(2,1)} %all-gather.9.cloned.1.call-done.refs_1_, f32[1024,1408]{1,0:T(8,128)} %get-tuple-element.85.refs_2_, f32[1024,1408]{1,0:T(8,128)} %get-tuple-element.86.refs_3_, ...), custom_call_target="tpu_custom_call" | custom-call | flops 1024 | bytes 1024 | tf_op jit(solution)/shard_map/feed_back/pallas_call | solution.py:42
  283.0 17.8 %part_ff.1.refs_2_ = bf16[2048,2816]{1,0:T(8,128)(2,1)} custom-call(bf16[1024,2048]{1,0:T(8,128)(2,1)} %lay.6.refs_0_, bf16[1024,2816]{1,0:T(8,128)(2,1)} %feed_back.1.refs_1_.refs_0_), custom_call_target="tpu_custom_call" | custom-call | flops 1024 | bytes 1024 | tf_op jit(solution)/shard_map/part_ff/pallas_call | solution.py:42
  300.8 18.2 %grad_mid.1 = (bf16[256,2048]{1,0:T(8,128)(2,1)}, bf16[256,2048]{1,0:T(8,128)(2,1)}, f32[512,2048]{1,0:T(8,128)}) custom-call(bf16[1024,2816]{1,0:T(8,128)(2,1)} %feed_back.1.refs_1_.refs_0_, bf16[2048,2816]{1,0:T(8,128)(2,1)} %all-gather.7.cloned.1.call-done.refs_1_, bf16[2048,2816]{1,0:T(8,128)(2,1)} %part_ff.1.refs_2_), custom_call_target="tpu_custom_call" | custom-call | flops 1024 | bytes 1024 | tf_op jit(solution)/shard_map/grad_mid/pallas_call | solution.py:42
  321.2 23.1 %collective-permute-done.20.refs_1_ = bf16[256,2048]{1,0:T(8,128)(2,1)S(1)} collective-permute-done((bf16[256,2048]{1,0:T(8,128)(2,1)}, bf16[256,2048]{1,0:T(8,128)(2,1)S(1)}, u32[]{:S(2)}, u32[]{:S(2)}) %collective-permute-start.20) | collective-permute-done | bytes 1048608 | tf_op jit(solution)/shard_map/ppermute | solution.py:188
  351.1 10.9 %collective-permute-done.22.refs_3_ = bf16[128,2048]{1,0:T(8,128)(2,1)S(1)} collective-permute-done((bf16[128,2048]{1,0:T(8,128)(2,1)}, bf16[128,2048]{1,0:T(8,128)(2,1)S(1)}, u32[]{:S(2)}, u32[]{:S(2)}) %collective-permute-start.22) | collective-permute-done | bytes 524320 | tf_op jit(solution)/shard_map/ppermute | solution.py:192
  373.7 23.4 %collective-permute-done.24.refs_1_ = bf16[256,2176]{1,0:T(8,128)(2,1)S(1)} collective-permute-done((bf16[256,2176]{1,0:T(8,128)(2,1)}, bf16[256,2176]{1,0:T(8,128)(2,1)S(1)}, u32[]{:S(2)}, u32[]{:S(2)}) %collective-permute-start.24) | collective-permute-done | bytes 1114144 | tf_op jit(solution)/shard_map/ppermute | solution.py:188
  399.4 12.3 %down.1 = (bf16[256,2048]{1,0:T(8,128)(2,1)}, bf16[256,2048]{1,0:T(8,128)(2,1)}, f32[512,2048]{1,0:T(8,128)}) custom-call(bf16[1024,1408]{1,0:T(8,128)(2,1)} %get-tuple-element.84.refs_0_, bf16[1408,2048]{1,0:T(8,128)(2,1)} %all-gather.9.cloned.1.call-done.refs_1_, bf16[256,2176]{1,0:T(8,128)(2,1)} %get-tuple-element.96.refs_2_.refs_0_), custom_call_target="tpu_custom_call" | custom-call | flops 1024 | bytes 1024 | tf_op jit(solution)/shard_map/down/pallas_call | solution.py:42
  427.6 9.4 %scan_backward.1 = (f32[8,128,512]{2,1,0:T(8,128)}, f32[8,128,512]{2,1,0:T(8,128)}, f32[8,512]{1,0:T(8,128)}, bf16[8,128,512]{2,1,0:T(8,128)(2,1)}, f32[1,512]{1,0:T(1,128)}) custom-call(f32[8,128,128]{2,1,0:T(8,128)} %convert.1.keep_ref.refs_0_.refs_1_, f32[8,128,1024]{2,1,0:T(8,128)} %bitcast.34, f32[8,128,512]{2,1,0:T(8,128)} %bitcast.39, ...), custom_call_target="tpu_custom_call" | custom-call | flops 1024 | bytes 1024 | tf_op jit(solution)/shard_map/scan_backward/pallas_call | solution.py:42
  466.0 15.9 %all-gather = f32[64,512]{1,0:T(8,128)} all-gather(f32[8,512]{1,0:T(8,128)S(1)} %copy-done.45), channel_id=2, replica_groups=mesh['grp'=4,'seq'=8] {'seq'}, dimensions={0}, use_global_device_ids=true | all-gather | bytes 147456 | tf_op jit(solution)/shard_map/all_gather | solution.py:1260
  489.5 12.4 %grad_in.1 = (bf16[256,2048]{1,0:T(8,128)(2,1)}, bf16[256,2048]{1,0:T(8,128)(2,1)}, f32[512,2048]{1,0:T(8,128)}) custom-call(bf16[1024,1024]{1,0:T(8,128)(2,1)} %bitcast.40, bf16[1024,512]{1,0:T(8,128)(2,1)} %bitcast.48, bf16[2048,2048]{1,0:T(8,128)(2,1)} %all-gather.5.cloned.1.call-done.refs_1_.refs_2_.refs_3_, ...), custom_call_target="tpu_custom_call" | custom-call | flops 1024 | bytes 1024 | tf_op jit(solution)/shard_map/grad_in/pallas_call | solution.py:42
  504.8 10.2 %part_pair.1.refs_6_ = bf16[2048,1024]{1,0:T(8,128)(2,1)} custom-call(bf16[1024,2176]{1,0:T(8,128)(2,1)} %lay.4.refs_0_, bf16[1024,1024]{1,0:T(8,128)(2,1)} %bitcast.41, bf16[256,2048]{1,0:T(8,128)(2,1)} %get-tuple-element.115.refs_2_), custom_call_target="tpu_custom_call" | custom-call | flops 1024 | bytes 1024 | tf_op jit(solution)/shard_map/part_pair/pallas_call | solution.py:42
  518.2 20.7 %collective-permute-done.31.refs_4_ = bf16[128,2048]{1,0:T(8,128)(2,1)} collective-permute-done((bf16[128,2048]{1,0:T(8,128)(2,1)}, bf16[128,2048]{1,0:T(8,128)(2,1)}, u32[]{:S(2)}, u32[]{:S(2)}) %collective-permute-start.31) | collective-permute-done | bytes 524320 | tf_op jit(solution)/shard_map/ppermute | solution.py:188
  555.4 8.1 %place_rows.1 = f32[4,176,2048]{2,1,0:T(8,128)} custom-call(s32[1]{0:T(128)} %bitcast.6.refs_0_, bf16[176,2048]{1,0:T(8,128)(2,1)} %reduce-scatter.5.cloned.1.call-done.refs_1_, bf16[176,2048]{1,0:T(8,128)(2,1)} %copy-done.6, bf16[176,2048]{1,0:T(8,128)(2,1)} %copy-done.10, bf16[96,2048]{1,0:T(8,128)(2,1)} %copy-done.39, ...), custom_call_target="tpu_custom_call" | custom-call | flops 1024 | bytes 1024 | tf_op jit(solution)/shard_map/place_rows/pallas_call | solution.py:42
  571.4 9.7 %place_columns.3 = (f32[256,5632]{1,0:T(8,128)}, f32[256,5632]{1,0:T(8,128)}) custom-call(s32[1]{0:T(128)} %bitcast.6.refs_0_, bf16[256,2816]{1,0:T(8,128)(2,1)} %reduce-scatter.7.cloned.1.call-done.refs_1_, bf16[256,2816]{1,0:T(8,128)(2,1)} %copy-done.2, bf16[256,2816]{1,0:T(8,128)(2,1)} %copy-done.3, bf16[128,2816]{1,0:T(8,128)(2,1)} %copy-done.29, ...), custom_call_target="tpu_custom_call" | custom-call | flops 1024 | bytes 1024 | tf_op jit(solution)/shard_map/place_columns/pallas_call | solution.py:42
  (307 shorter events, 288.1 us)
Async XLA Ops:
  7.2 89.8 %all-gather.5.cloned.1.call-start = ((), (), s32[]{:S(2)}) async-start(), calls=%async_computation.4 | async-start | bytes 9437184 | tf_op jit(solution)/shard_map/all_gather | solution.py:1165
  11.6 226.3 %all-gather.7.cloned.1.call-start = ((), (), s32[]{:S(2)}) async-start(), calls=%async_computation.5 | async-start | bytes 12976128 | tf_op jit(solution)/shard_map/all_gather | solution.py:1165
  21.0 247.3 %all-gather.9.cloned.1.call-start = ((), (), s32[]{:S(2)}) async-start(), calls=%async_computation.6 | async-start | bytes 6488064 | tf_op jit(solution)/shard_map/all_gather | solution.py:1165
  22.1 397.3 %reduce-scatter.5.cloned.1.call-start = ((), (), s32[]{:S(2)}) async-start(), calls=%async_computation.7 | async-start | bytes 6488064 | tf_op jit(solution)/shard_map/reduce_scatter | solution.py:1168
  22.1 28.7 %collective-permute-start = (bf16[256,2176]{1,0:T(8,128)(2,1)}, bf16[256,2176]{1,0:T(8,128)(2,1)S(1)}, u32[]{:S(2)}, u32[]{:S(2)}) collective-permute-start(bf16[256,2176]{1,0:T(8,128)(2,1)} %norm_in.1.refs_3_.refs_0_), channel_id=1, source_target_pairs={{0,8},{8,0},{16,24},{24,16},{1,9},{9,1},{17,25},{25,17},{2,10},{10... | collective-permute-start | bytes 3342344 | tf_op jit(solution)/shard_map/ppermute | solution.py:188
  25.2 28.6 %collective-permute-start.1 = (bf16[256,2176]{1,0:T(8,128)(2,1)}, bf16[256,2176]{1,0:T(8,128)(2,1)S(1)}, u32[]{:S(2)}, u32[]{:S(2)}) collective-permute-start(bf16[256,2176]{1,0:T(8,128)(2,1)} %norm_in.1.refs_3_.refs_0_), channel_id=1, source_target_pairs={{0,16},{16,0},{8,24},{24,8},{1,17},{17,1},{9,25},{25,9},{2,18},{18... | collective-permute-start | bytes 3342344 | tf_op jit(solution)/shard_map/ppermute | solution.py:192
  26.6 46.7 %collective-permute-start.4 = (bf16[256,2048]{1,0:T(8,128)(2,1)}, bf16[256,2048]{1,0:T(8,128)(2,1)S(1)}, u32[]{:S(2)}, u32[]{:S(2)}) collective-permute-start(bf16[256,2048]{1,0:T(8,128)(2,1)} %refs_6_.3), channel_id=1, source_target_pairs={{0,8},{8,0},{16,24},{24,16},{1,9},{9,1},{17,25},{25,17},{2,10},{10... | collective-permute-start | bytes 3145736 | tf_op jit(solution)/shard_map/ppermute | solution.py:188
  27.2 49.0 %collective-permute-start.5 = (bf16[256,2048]{1,0:T(8,128)(2,1)}, bf16[256,2048]{1,0:T(8,128)(2,1)S(1)}, u32[]{:S(2)}, u32[]{:S(2)}) collective-permute-start(bf16[256,2048]{1,0:T(8,128)(2,1)} %refs_6_.3), channel_id=1, source_target_pairs={{0,16},{16,0},{8,24},{24,8},{1,17},{17,1},{9,25},{25,9},{2,18},{18... | collective-permute-start | bytes 3145736 | tf_op jit(solution)/shard_map/ppermute | solution.py:192
  51.7 35.7 %collective-permute-start.2 = (bf16[128,2176]{1,0:T(8,128)(2,1)}, bf16[128,2176]{1,0:T(8,128)(2,1)}, u32[]{:S(2)}, u32[]{:S(2)}) collective-permute-start(bf16[128,2176]{1,0:T(8,128)(2,1)} %slice.84), channel_id=1, source_target_pairs={{0,16},{16,0},{8,24},{24,8},{1,17},{17,1},{9,25},{25,9},{2,18},{18... | collective-permute-start | bytes 1671176 | tf_op jit(solution)/shard_map/ppermute | solution.py:192
  54.7 32.8 %collective-permute-start.3 = (bf16[128,2176]{1,0:T(8,128)(2,1)}, bf16[128,2176]{1,0:T(8,128)(2,1)}, u32[]{:S(2)}, u32[]{:S(2)}) collective-permute-start(bf16[128,2176]{1,0:T(8,128)(2,1)} %slice.85), channel_id=1, source_target_pairs={{0,8},{8,0},{16,24},{24,16},{1,9},{9,1},{17,25},{25,17},{2,10},{10... | collective-permute-start | bytes 1671176 | tf_op jit(solution)/shard_map/ppermute | solution.py:188
  268.0 194.6 %reduce-scatter.7.cloned.1.call-start = ((), (), s32[]{:S(2)}) async-start(), calls=%async_computation.8 | async-start | bytes 12976128 | tf_op jit(solution)/shard_map/reduce_scatter | solution.py:1168
  300.7 253.1 %reduce-scatter.9.cloned.1.call-start = ((), (), s32[]{:S(2)}) async-start(), calls=%async_computation.9 | async-start | bytes 4718592 | tf_op jit(solution)/shard_map/reduce_scatter | solution.py:1168
  419.3 35.8 %collective-permute-start.32 = (bf16[176,2048]{1,0:T(8,128)(2,1)}, bf16[176,2048]{1,0:T(8,128)(2,1)S(1)}, u32[]{:S(2)}, u32[]{:S(2)}) collective-permute-start(bf16[176,2048]{1,0:T(8,128)(2,1)} %reduce-scatter.5.cloned.1.call-done.refs_1_), channel_id=1, source_target_pairs={{0,8},{8,0},{16,24},{24,16},{1,9},{9,1},{17,25},{25,17},{2,10},{10... | collective-permute-start | bytes 2162696 | tf_op jit(solution)/shard_map/ppermute | solution.py:188
  420.3 35.2 %collective-permute-start.33 = (bf16[176,2048]{1,0:T(8,128)(2,1)}, bf16[176,2048]{1,0:T(8,128)(2,1)S(1)}, u32[]{:S(2)}, u32[]{:S(2)}) collective-permute-start(bf16[176,2048]{1,0:T(8,128)(2,1)} %reduce-scatter.5.cloned.1.call-done.refs_1_), channel_id=1, source_target_pairs={{0,16},{16,0},{8,24},{24,8},{1,17},{17,1},{9,25},{25,9},{2,18},{18... | collective-permute-start | bytes 2162696 | tf_op jit(solution)/shard_map/ppermute | solution.py:192
  462.5 138.6 %reduce-scatter.11.cloned.1.call-start = ((), (), s32[]{:S(2)}) async-start(), calls=%async_computation.10 | async-start | bytes 4718592 | tf_op jit(solution)/shard_map/reduce_scatter | solution.py:1168
  462.5 41.0 %collective-permute-start.34 = (bf16[256,2816]{1,0:T(8,128)(2,1)}, bf16[256,2816]{1,0:T(8,128)(2,1)S(1)}, u32[]{:S(2)}, u32[]{:S(2)}) collective-permute-start(bf16[256,2816]{1,0:T(8,128)(2,1)} %reduce-scatter.7.cloned.1.call-done.refs_1_), channel_id=1, source_target_pairs={{0,8},{8,0},{16,24},{24,16},{1,9},{9,1},{17,25},{25,17},{2,10},{10... | collective-permute-start | bytes 4325384 | tf_op jit(solution)/shard_map/ppermute | solution.py:188
  463.9 76.3 %collective-permute-start.35 = (bf16[256,2816]{1,0:T(8,128)(2,1)}, bf16[256,2816]{1,0:T(8,128)(2,1)S(1)}, u32[]{:S(2)}, u32[]{:S(2)}) collective-permute-start(bf16[256,2816]{1,0:T(8,128)(2,1)} %reduce-scatter.7.cloned.1.call-done.refs_1_), channel_id=1, source_target_pairs={{0,16},{16,0},{8,24},{24,8},{1,17},{17,1},{9,25},{25,9},{2,18},{18... | collective-permute-start | bytes 4325384 | tf_op jit(solution)/shard_map/ppermute | solution.py:192
  464.9 51.1 %collective-permute-start.30 = (bf16[128,2048]{1,0:T(8,128)(2,1)}, bf16[128,2048]{1,0:T(8,128)(2,1)S(1)}, u32[]{:S(2)}, u32[]{:S(2)}) collective-permute-start(bf16[128,2048]{1,0:T(8,128)(2,1)} %get-tuple-element.106.refs_3_), channel_id=1, source_target_pairs={{0,16},{16,0},{8,24},{24,8},{1,17},{17,1},{9,25},{25,9},{2,18},{18... | collective-permute-start | bytes 1572872 | tf_op jit(solution)/shard_map/ppermute | solution.py:192
  501.9 61.5 %collective-permute-start.36 = (bf16[256,2048]{1,0:T(8,128)(2,1)}, bf16[256,2048]{1,0:T(8,128)(2,1)}, u32[]{:S(2)}, u32[]{:S(2)}) collective-permute-start(bf16[256,2048]{1,0:T(8,128)(2,1)} %get-tuple-element.115.refs_2_), channel_id=1, source_target_pairs={{0,8},{8,0},{16,24},{24,16},{1,9},{9,1},{17,25},{25,17},{2,10},{10... | collective-permute-start | bytes 3145736 | tf_op jit(solution)/shard_map/ppermute | solution.py:188
  502.5 61.9 %collective-permute-start.37 = (bf16[256,2048]{1,0:T(8,128)(2,1)}, bf16[256,2048]{1,0:T(8,128)(2,1)}, u32[]{:S(2)}, u32[]{:S(2)}) collective-permute-start(bf16[256,2048]{1,0:T(8,128)(2,1)} %get-tuple-element.118), channel_id=1, source_target_pairs={{0,16},{16,0},{8,24},{24,8},{1,17},{17,1},{9,25},{25,9},{2,18},{18... | collective-permute-start | bytes 3145736 | tf_op jit(solution)/shard_map/ppermute | solution.py:192
  503.6 35.3 %collective-permute-start.31 = (bf16[128,2048]{1,0:T(8,128)(2,1)}, bf16[128,2048]{1,0:T(8,128)(2,1)}, u32[]{:S(2)}, u32[]{:S(2)}) collective-permute-start(bf16[128,2048]{1,0:T(8,128)(2,1)} %get-tuple-element.107), channel_id=1, source_target_pairs={{0,8},{8,0},{16,24},{24,16},{1,9},{9,1},{17,25},{25,17},{2,10},{10... | collective-permute-start | bytes 1572872 | tf_op jit(solution)/shard_map/ppermute | solution.py:188
  516.0 52.5 %collective-permute-start.42 = (bf16[128,2816]{1,0:T(8,128)(2,1)}, bf16[128,2816]{1,0:T(8,128)(2,1)S(1)}, u32[]{:S(2)}, u32[]{:S(2)}) collective-permute-start(bf16[128,2816]{1,0:T(8,128)(2,1)} %slice.95), channel_id=1, source_target_pairs={{0,16},{16,0},{8,24},{24,8},{1,17},{17,1},{9,25},{25,9},{2,18},{18... | collective-permute-start | bytes 2162696 | tf_op jit(solution)/shard_map/ppermute | solution.py:192
  601.1 27.3 %collective-permute-start.51 = (bf16[256,1024]{1,0:T(8,128)(2,1)}, bf16[256,1024]{1,0:T(8,128)(2,1)S(1)}, u32[]{:S(2)}, u32[]{:S(2)}) collective-permute-start(bf16[256,1024]{1,0:T(8,128)(2,1)} %reduce-scatter.11.cloned.1.call-done.refs_1_), channel_id=1, source_target_pairs={{0,8},{8,0},{16,24},{24,16},{1,9},{9,1},{17,25},{25,17},{2,10},{10... | collective-permute-start | bytes 1572872 | tf_op jit(solution)/shard_map/ppermute | solution.py:188
  601.9 27.6 %collective-permute-start.52 = (bf16[256,1024]{1,0:T(8,128)(2,1)}, bf16[256,1024]{1,0:T(8,128)(2,1)S(1)}, u32[]{:S(2)}, u32[]{:S(2)}) collective-permute-start(bf16[256,1024]{1,0:T(8,128)(2,1)} %reduce-scatter.11.cloned.1.call-done.refs_1_), channel_id=1, source_target_pairs={{0,16},{16,0},{8,24},{24,8},{1,17},{17,1},{9,25},{25,9},{2,18},{18... | collective-permute-start | bytes 1572872 | tf_op jit(solution)/shard_map/ppermute | solution.py:192
  (93 other events, 1014.6 us)
Sparse Core Ops, SparseCore 0:
  11.7 84.6 all-gather.4
  98.7 109.3 all-gather.6
  209.7 58.6 all-gather.8
  271.1 64.3 reduce-scatter.4
  337.6 117.6 reduce-scatter.6
  462.6 48.4 reduce-scatter.8
  515.1 47.0 reduce-scatter.10

commit v4 on v3

--- a/solution.py
+++ b/solution.py
@@ -23,7 +23,7 @@
 NN = (((1,), (0,)), ((), ()))
 NT = (((1,), (1,)), ((), ()))
 TN = (((0,), (0,)), ((), ()))
-COSTS = {"finish_in": 67}
+COSTS = {"finish_in": 65, "finish_mid": 210}
 SMALL = pl.CostEstimate(flops=1024, bytes_accessed=1024, transcendentals=0)
 ANY = pl.BlockSpec(memory_space=pl.ANY)
 SMEM = pl.BlockSpec(memory_space=pltpu.SMEM)
@@ -249,14 +249,20 @@
 
 
 def sum_everywhere(value):
-    value = value + send_x(value)
-    value = value + send_y(value)
     count = lax.axis_size("seq")
-    step = 1
-    while step < count:
-        value = value + lax.ppermute(value, "seq", [(one, one ^ step) for one in range(count)])
-        step *= 2
-    return value
+    if count > 8:
+        step = 1
+        while step < count:
+            value = value + lax.ppermute(value, "seq", [(one, one ^ step) for one in range(count)])
+            step *= 2
+    else:
+        value = value + lax.ppermute(value, "seq", [(one, one ^ 1) for one in range(count)])
+        value = value + sum(
+            lax.ppermute(value, "seq", [(one, (one + step) % count) for one in range(count)])
+            for step in range(2, count, 2)
+        )
+    across = lax.ppermute(value, "grp", [(one, 3 - one) for one in range(GRP)])
+    return value + send_x(value) + send_y(value) + across
 
 
 def split(column):
@@ -1209,12 +1215,18 @@
     part_down = outer_sum("part_down", hidden, cot, hidden.shape[1], width, -512)
     sum_down = reduced(part_down)
 
-    grad_ff = feed_back(cot, w_down, by_gate, by_up, (part_down,))
-    part_ff = outer_sum("part_ff", normed_mid, grad_ff, width, grad_ff.shape[1], 256)
+    to_x, to_y, kept_out = partial_sums("down", NN, (hidden,), (w_down,), 256, deps=(part_down,))
+    by_x_out, by_y_out = send_x(to_x), send_y(to_y)
+    grad_ff = feed_back(cot, w_down, by_gate, by_up, (to_x,))
+    to_x, to_y, kept = partial_sums("grad_mid", NT, (grad_ff,), (w_ff,), 256)
+    by_x, by_y = send_x(to_x), send_y(to_y)
+    part_ff = outer_sum("part_ff", normed_mid, grad_ff, width, grad_ff.shape[1], 256, (to_x,))
     sum_ff = reduced(part_ff)
-    to_x, to_y, kept = partial_sums("grad_mid", NT, (grad_ff,), (w_ff,), 256, deps=(part_ff,))
-    by_x, by_y = send_x(to_x), send_y(to_y)
-    for_y, for_x = merge("grad_mid_merge", kept, by_x, by_y)
+    out_for_y, out_for_x = merge("down_merge", kept_out, by_x_out, by_y_out, None, (part_ff,))
+    out_last_y, out_last_x = send_y(out_for_y), send_x(out_for_x)
+    pieces_out = (kept_out, by_x_out, by_y_out, out_last_y, out_last_x)
+    for_y, for_x = merge("grad_mid_merge", kept, by_x, by_y, deps=(out_for_y,))
+    block_out = add_scattered(pieces_out, middle, BF16, width, (for_y,))
     pieces = (kept, by_x, by_y, send_y(for_y), send_x(for_x))
     grad_middle, scaled_mix, grad_mlp_gain = finish_mid(
         pieces,
@@ -1225,13 +1237,10 @@
         scale_mid,
         mid_gain,
         width,
+        (block_out,),
     )
     held = start_gather(scaled_mix)
-    to_x, to_y, kept_out = partial_sums("down", NN, (hidden,), (w_down,), 256, deps=(scaled_mix,))
-    grad_mix = end_gather(held, (to_x,))
-
-    to_x, to_y = after((to_x, to_y), grad_mix)
-    by_x_out, by_y_out = send_x(to_x), send_y(to_y)
+    grad_mix = end_gather(held)
     held_down = start_gather(after(sum_down, grad_mix))
     back, coupling = product_back("back", grad_mix, w_out, 256)
     after_prod, local, ends_back, grad_gate, gain_sum = scan_backward(
@@ -1245,18 +1254,17 @@
         coupling.reshape(8, half, LANE),
     )
     grad_gate = grad_gate.reshape(plane, own)
-    out_sends = []
-
-    def between(deps):
-        out_sends.extend(merge("down_merge", kept_out, by_x_out, by_y_out, None, deps))
-        return out_sends[0], held_down[1], held_down[2]
-
     part_gate_out, _ = outer_gate_out(
-        normed, grad_gate, mix, grad_mix, parts, width, (after_prod,), between
+        normed,
+        grad_gate,
+        mix,
+        grad_mix,
+        parts,
+        width,
+        (after_prod,),
+        lambda deps: (held_down[1], held_down[2]),
     )
     sum_gate_out = reduced(part_gate_out)
-    out_last_y, out_last_x = send_y(out_sends[0]), send_x(out_sends[1])
-    pieces_out = (kept_out, by_x_out, by_y_out, out_last_y, out_last_x)
     ends_back = lax.all_gather(after(ends_back, part_gate_out), "seq")
     grad_pair, bias_sum = finish_backward(
         info, keep, ends_back, after_prod, local, proj, bias, states, enter, (part_gate_out,)
@@ -1267,28 +1275,28 @@
         "grad_in", NT, (grad_pair, grad_gate), (w_first, w_first), 256, firsts=(0, 2 * own)
     )
     by_x, by_y = send_x(to_x), send_y(to_y)
-    part_pair = outer_sum("part_pair", normed, grad_pair, width, 2 * own, 256, (to_x,))
+    down_pieces = second_step(held_down)
+    part_pair = outer_sum(
+        "part_pair", normed, grad_pair, width, 2 * own, 256, (to_x,) + down_pieces[3:]
+    )
     sum_pair = reduced(part_pair)
-    block_out = add_scattered(
-        pieces_out, middle, BF16, width, (part_pair, held_ff[1], held_ff[2])
-    )
-    grad_down = place_rows(mine, second_step(held_down), (block_out,))
+    grad_down = place_rows(mine, down_pieces, (part_pair, held_ff[1], held_ff[2]))
     for_y, for_x = merge("grad_in_merge", kept, by_x, by_y, deps=(grad_down,))
     last_y, last_x = send_y(for_y), send_x(for_x)
     pieces = (kept, by_x, by_y, last_y, last_x)
-    held_go = start_gather(after(sum_gate_out, held_ff[1], held_ff[2]))
+    held_go = start_gather(after(sum_gate_out, pieces[3], pieces[4]))
     grad_mlp_gate, grad_mlp_up = place_columns(
         mine, second_step(held_ff), parts, 2, w_ff.shape[1] // 2, True, (for_y,)
     )
     grad_tokens, grad_norm_gain = finish_in(
-        pieces, tokens, grad_middle, in_gain, width, (grad_mlp_up, held_go[1], held_go[2])
+        pieces, tokens, grad_middle, in_gain, width, (grad_mlp_up,)
     )
     vectors = sum_everywhere(
         jnp.stack(
             [grad_norm_gain[0], all_features(bias_sum), all_features(gain_sum), grad_mlp_gain[0]]
         )
     )
-    held_pair = start_gather(after(sum_pair, held_go[1], held_go[2]))
+    held_pair = start_gather(after(sum_pair, grad_tokens))
     gate_out_pieces = second_step(held_go)
     (grad_gate_proj,) = place_columns(mine, gate_out_pieces, parts, 1, own, True)
     grad_out = place_stacked(mine, gate_out_pieces, own, own, (grad_gate_proj,))

time: 655 us -> 630 us (0.962)
  waiting for transfers between devices: 236 us -> 206 us
    ppermute x25, waiting for transfers between devices: 165 us -> 56.7 us  [send_x(): return lax.ppermute(value, 'grp', SWAP_X)]
    ppermute x25, waiting for transfers between devices: 57 us -> 121 us  [send_y(): return lax.ppermute(value, 'grp', SWAP_Y)]
    reduce_scatter x4, waiting for transfers between devices: 0.02 us -> 9.12 us  [reduced(): return lax.psum_scatter(grads, 'seq', scatter_dimension=0, tiled=True)]
    ppermute x3 -> x5, waiting for transfers between devices: 5.1 us -> 12.7 us  [the longest x1 10.9 us: sum_everywhere(): across = lax.ppermute(value, 'grp', [(one, 3 - one) for one in range(GRP)])]
  transfers between devices with their start and end apart: 64 -> 66, of which waited for: 36 -> 30; matrix products, arithmetic and copies ran while one was open for 3% -> 3% of each run, Pallas kernels for 43% -> 45%
where the time goes in v4:
time: 630 us; the launch traced here: 626 us
  Pallas kernels  293 us (47%)
  waiting for transfers between devices  206 us (33%)
  starting transfers between devices  64.6 us (10%)
  local copies, waits for them, and re-layouts  25.7 us (4%)
  blocking collectives  15.8 us (3%)
  between operations  14.7 us (2%)
    pallas_call x38, Pallas kernels, call(): pl.pallas_call(wrapped, grid=grid, in_specs=list(in_specs) + [ANY] * n_de...  285 us
    ppermute x25, waiting for transfers between devices, send_y(): return lax.ppermute(value, 'grp', SWAP_Y)  121 us
    ppermute x25, waiting for transfers between devices, send_x(): return lax.ppermute(value, 'grp', SWAP_X)  56.7 us
    ppermute x25, starting transfers between devices, send_x(): return lax.ppermute(value, 'grp', SWAP_X)  28.5 us
    ppermute x25, starting transfers between devices, send_y(): return lax.ppermute(value, 'grp', SWAP_Y)  26.1 us
    all_gather x1, blocking collectives, on_device(): ends_back = lax.all_gather(after(ends_back, part_gate_out), 'seq')  15.8 us
    unnamed x104, local copies, waits for them, and re-layouts  13.1 us
  transfers between devices with their start and end apart: 66, of which 30 were waited for; matrix products, arithmetic and copies ran while one was open for 3% of the time, Pallas kernels for 45%

profile of v4, /device:TPU:0, one launch (start us, length us, event | category | flops | bytes accessed | tf_op | source)
XLA Modules:
  0.0 625.8 jit_solution(15187705695573239623)
XLA Ops:
  27.3 23.5 %collective-permute-done.1.refs_2_ = bf16[256,2176]{1,0:T(8,128)(2,1)S(1)} collective-permute-done((bf16[256,2176]{1,0:T(8,128)(2,1)}, bf16[256,2176]{1,0:T(8,128)(2,1)S(1)}, u32[]{:S(2)}, u32[]{:S(2)}) %collective-permute-start.1) | collective-permute-done | bytes 1114144 | tf_op jit(solution)/shard_map/ppermute | solution.py:192
  56.1 17.2 %collective-permute-done.5.refs_4_.refs_2_ = bf16[256,2048]{1,0:T(8,128)(2,1)S(1)} collective-permute-done((bf16[256,2048]{1,0:T(8,128)(2,1)}, bf16[256,2048]{1,0:T(8,128)(2,1)S(1)}, u32[]{:S(2)}, u32[]{:S(2)}) %collective-permute-start.5) | collective-permute-done | bytes 1048608 | tf_op jit(solution)/shard_map/ppermute | solution.py:192
  98.0 9.1 %proj_pair.1 = f32[1024,1024]{1,0:T(8,128)} custom-call(bf16[1024,2176]{1,0:T(8,128)(2,1)} %lay.4.refs_0_, bf16[2048,2048]{1,0:T(8,128)(2,1)} %all-gather.5.cloned.1.call-done.refs_1_.refs_2_.refs_3_, bf16[256,2048]{1,0:T(8,128)(2,1)} %refs_6_.3, bf16[256,2048]{1,0:T(8,128)(2,1)} %copy-done.5, bf16[256,2048]{1,0:T(8,128)(2,1)} %copy-done.4, ...), custom_call_target="tpu_custom_call" | custom-call | flops 1024 | bytes 1024 | tf_op jit(solution)/shard_map/proj_pair/pallas_call | solution.py:42
  158.6 15.9 %collective-permute-done.13.refs_2_ = bf16[256,2176]{1,0:T(8,128)(2,1)S(1)} collective-permute-done((bf16[256,2176]{1,0:T(8,128)(2,1)}, bf16[256,2176]{1,0:T(8,128)(2,1)S(1)}, u32[]{:S(2)}, u32[]{:S(2)}) %collective-permute-start.13) | collective-permute-done | bytes 1114144 | tf_op jit(solution)/shard_map/ppermute | solution.py:192
  182.1 11.8 %collective-permute-done.14.refs_3_ = bf16[128,2176]{1,0:T(8,128)(2,1)S(1)} collective-permute-done((bf16[128,2176]{1,0:T(8,128)(2,1)}, bf16[128,2176]{1,0:T(8,128)(2,1)S(1)}, u32[]{:S(2)}, u32[]{:S(2)}) %collective-permute-start.14) | collective-permute-done | bytes 557088 | tf_op jit(solution)/shard_map/ppermute | solution.py:192
  204.6 21.0 %collective-permute-done.17.refs_2_ = bf16[256,2048]{1,0:T(8,128)(2,1)S(1)} collective-permute-done((bf16[256,2048]{1,0:T(8,128)(2,1)}, bf16[256,2048]{1,0:T(8,128)(2,1)S(1)}, u32[]{:S(2)}, u32[]{:S(2)}) %collective-permute-start.17) | collective-permute-done | bytes 1048608 | tf_op jit(solution)/shard_map/ppermute | solution.py:192
  228.4 8.9 %collective-permute-done.19.refs_4_ = bf16[128,2048]{1,0:T(8,128)(2,1)S(1)} collective-permute-done((bf16[128,2048]{1,0:T(8,128)(2,1)S(1)}, bf16[128,2048]{1,0:T(8,128)(2,1)S(1)}, u32[]{:S(2)}, u32[]{:S(2)}) %collective-permute-start.19) | collective-permute-done | bytes 524320 | tf_op jit(solution)/shard_map/ppermute | solution.py:188
  243.6 20.0 %feed_forward.1 = (bf16[1024,1408]{1,0:T(8,128)(2,1)}, f32[1024,1408]{1,0:T(8,128)}, f32[1024,1408]{1,0:T(8,128)}) custom-call(bf16[1024,2048]{1,0:T(8,128)(2,1)} %lay.6.refs_0_, bf16[2048,2816]{1,0:T(8,128)(2,1)} %all-gather.7.cloned.1.call-done.refs_1_), custom_call_target="tpu_custom_call" | custom-call | flops 1024 | bytes 1024 | tf_op jit(solution)/shard_map/feed_forward/pallas_call | solution.py:42
  263.6 10.2 %part_down.1.refs_2_ = bf16[1408,2048]{1,0:T(8,128)(2,1)} custom-call(bf16[1024,1408]{1,0:T(8,128)(2,1)} %get-tuple-element.82.refs_0_, bf16[1024,2048]{1,0:T(8,128)(2,1)} %lay.5.refs_4_.refs_1_.refs_0_), custom_call_target="tpu_custom_call" | custom-call | flops 1024 | bytes 1024 | tf_op jit(solution)/shard_map/part_down/pallas_call | solution.py:42
  274.0 12.2 %down.1 = (bf16[256,2048]{1,0:T(8,128)(2,1)}, bf16[256,2048]{1,0:T(8,128)(2,1)}, f32[512,2048]{1,0:T(8,128)}) custom-call(bf16[1024,1408]{1,0:T(8,128)(2,1)} %get-tuple-element.82.refs_0_, bf16[1408,2048]{1,0:T(8,128)(2,1)} %all-gather.9.cloned.1.call-done.refs_1_, bf16[1408,2048]{1,0:T(8,128)(2,1)} %part_down.1.refs_2_), custom_call_target="tpu_custom_call" | custom-call | flops 1024 | bytes 1024 | tf_op jit(solution)/shard_map/down/pallas_call | solution.py:42
  288.6 14.0 %feed_back.1.refs_0_.refs_1_ = bf16[1024,2816]{1,0:T(8,128)(2,1)} custom-call(bf16[1024,2048]{1,0:T(8,128)(2,1)} %lay.5.refs_4_.refs_1_.refs_0_, bf16[1408,2048]{1,0:T(8,128)(2,1)} %all-gather.9.cloned.1.call-done.refs_1_, f32[1024,1408]{1,0:T(8,128)} %get-tuple-element.86.refs_2_, f32[1024,1408]{1,0:T(8,128)} %get-tuple-element.87.refs_3_, ...), custom_call_target="tpu_custom_call" | custom-call | flops 1024 | bytes 1024 | tf_op jit(solution)/shard_map/feed_back/pallas_call | solution.py:42
  302.7 18.2 %grad_mid.1 = (bf16[256,2048]{1,0:T(8,128)(2,1)}, bf16[256,2048]{1,0:T(8,128)(2,1)}, f32[512,2048]{1,0:T(8,128)}) custom-call(bf16[1024,2816]{1,0:T(8,128)(2,1)} %feed_back.1.refs_0_.refs_1_, bf16[2048,2816]{1,0:T(8,128)(2,1)} %all-gather.7.cloned.1.call-done.refs_1_), custom_call_target="tpu_custom_call" | custom-call | flops 1024 | bytes 1024 | tf_op jit(solution)/shard_map/grad_mid/pallas_call | solution.py:42
  322.5 17.8 %part_ff.1.refs_3_ = bf16[2048,2816]{1,0:T(8,128)(2,1)} custom-call(bf16[1024,2048]{1,0:T(8,128)(2,1)} %lay.6.refs_0_, bf16[1024,2816]{1,0:T(8,128)(2,1)} %feed_back.1.refs_0_.refs_1_, bf16[256,2048]{1,0:T(8,128)(2,1)} %get-tuple-element.88.refs_2_), custom_call_target="tpu_custom_call" | custom-call | flops 1024 | bytes 1024 | tf_op jit(solution)/shard_map/part_ff/pallas_call | solution.py:42
  351.5 8.1 %collective-permute-done.23.refs_4_ = bf16[128,2048]{1,0:T(8,128)(2,1)S(1)} collective-permute-done((bf16[128,2048]{1,0:T(8,128)(2,1)}, bf16[128,2048]{1,0:T(8,128)(2,1)S(1)}, u32[]{:S(2)}, u32[]{:S(2)}) %collective-permute-start.23) | collective-permute-done | bytes 524320 | tf_op jit(solution)/shard_map/ppermute | solution.py:188
  377.6 21.5 %collective-permute-done.29.refs_2_ = bf16[256,2176]{1,0:T(8,128)(2,1)S(1)} collective-permute-done((bf16[256,2176]{1,0:T(8,128)(2,1)}, bf16[256,2176]{1,0:T(8,128)(2,1)S(1)}, u32[]{:S(2)}, u32[]{:S(2)}) %collective-permute-start.29) | collective-permute-done | bytes 1114144 | tf_op jit(solution)/shard_map/ppermute | solution.py:192
  425.4 9.4 %scan_backward.1 = (f32[8,128,512]{2,1,0:T(8,128)}, f32[8,128,512]{2,1,0:T(8,128)}, f32[8,512]{1,0:T(8,128)}, bf16[8,128,512]{2,1,0:T(8,128)(2,1)}, f32[1,512]{1,0:T(1,128)}) custom-call(f32[8,128,128]{2,1,0:T(8,128)} %convert.1.keep_ref.refs_0_.refs_1_, f32[8,128,1024]{2,1,0:T(8,128)} %bitcast.33, f32[8,128,512]{2,1,0:T(8,128)} %bitcast.38, ...), custom_call_target="tpu_custom_call" | custom-call | flops 1024 | bytes 1024 | tf_op jit(solution)/shard_map/scan_backward/pallas_call | solution.py:42
  448.4 9.1 %reduce-scatter.7.cloned.1.call-done.refs_1_ = bf16[256,2816]{1,0:T(8,128)(2,1)} async-done(((bf16[2048,2816]{1,0:T(8,128)(2,1)}), bf16[256,2816]{1,0:T(8,128)(2,1)}) %reduce-scatter.7.cloned.1.call-update) | async-done | bytes 1441808 | tf_op jit(solution)/shard_map/reduce_scatter | solution.py:1174
  463.6 15.8 %all-gather = f32[64,512]{1,0:T(8,128)} all-gather(f32[8,512]{1,0:T(8,128)S(1)} %copy-done.41), channel_id=2, replica_groups=mesh['grp'=4,'seq'=8] {'seq'}, dimensions={0}, use_global_device_ids=true | all-gather | bytes 147456 | tf_op jit(solution)/shard_map/all_gather | solution.py:1268
  487.1 12.4 %grad_in.1 = (bf16[256,2048]{1,0:T(8,128)(2,1)}, bf16[256,2048]{1,0:T(8,128)(2,1)}, f32[512,2048]{1,0:T(8,128)}) custom-call(bf16[1024,1024]{1,0:T(8,128)(2,1)} %bitcast.39, bf16[1024,512]{1,0:T(8,128)(2,1)} %bitcast.47, bf16[2048,2048]{1,0:T(8,128)(2,1)} %all-gather.5.cloned.1.call-done.refs_1_.refs_2_.refs_3_, ...), custom_call_target="tpu_custom_call" | custom-call | flops 1024 | bytes 1024 | tf_op jit(solution)/shard_map/grad_in/pallas_call | solution.py:42
  503.5 10.2 %part_pair.1.refs_6_ = bf16[2048,1024]{1,0:T(8,128)(2,1)} custom-call(bf16[1024,2176]{1,0:T(8,128)(2,1)} %lay.4.refs_0_, bf16[1024,1024]{1,0:T(8,128)(2,1)} %bitcast.40, bf16[256,2048]{1,0:T(8,128)(2,1)} %get-tuple-element.112.refs_2_, bf16[96,2048]{1,0:T(8,128)(2,1)} %copy-done.22, bf16[80,2048]{1,0:T(8,128)(2,1)} %copy-done.23), custom_call_target="tpu_custom_call" | custom-call | flops 1024 | bytes 1024 | tf_op jit(solution)/shard_map/part_pair/pallas_call | solution.py:42
  516.9 8.1 %place_rows.1 = f32[4,176,2048]{2,1,0:T(8,128)} custom-call(s32[1]{0:T(128)} %bitcast.6.refs_0_, bf16[176,2048]{1,0:T(8,128)(2,1)} %reduce-scatter.5.cloned.1.call-done.refs_1_, bf16[176,2048]{1,0:T(8,128)(2,1)} %copy-done.6, bf16[176,2048]{1,0:T(8,128)(2,1)} %copy-done.9, bf16[96,2048]{1,0:T(8,128)(2,1)} %copy-done.22, bf16[80,2048]{1,0:T(8,128)(2,1)} %copy-done.23, ...), custom_call_target="tpu_custom_call" | custom-call | flops 1024 | bytes 1024 | tf_op jit(solution)/shard_map/place_rows/pallas_call | solution.py:42
  534.8 8.2 %collective-permute-done.43.refs_5_ = bf16[128,2816]{1,0:T(8,128)(2,1)} collective-permute-done((bf16[128,2816]{1,0:T(8,128)(2,1)}, bf16[128,2816]{1,0:T(8,128)(2,1)}, u32[]{:S(2)}, u32[]{:S(2)}) %collective-permute-start.43) | collective-permute-done | bytes 720928 | tf_op jit(solution)/shard_map/ppermute | solution.py:188
  543.0 9.9 %place_columns.3 = (f32[256,5632]{1,0:T(8,128)}, f32[256,5632]{1,0:T(8,128)}) custom-call(s32[1]{0:T(128)} %bitcast.6.refs_0_, bf16[256,2816]{1,0:T(8,128)(2,1)} %reduce-scatter.7.cloned.1.call-done.refs_1_, bf16[256,2816]{1,0:T(8,128)(2,1)} %copy-done.3, bf16[256,2816]{1,0:T(8,128)(2,1)} %copy-done.2, bf16[128,2816]{1,0:T(8,128)(2,1)} %collective-permute-done.42.refs_4_, ...), custom_call_target="tpu_custom_call" | custom-call | flops 1024 | bytes 1024 | tf_op jit(solution)/shard_map/place_columns/pallas_call | solution.py:42
  578.7 10.9 %collective-permute-done.50 = f32[4,2048]{1,0:T(4,128)S(1)} collective-permute-done((f32[4,2048]{1,0:T(4,128)S(1)}, f32[4,2048]{1,0:T(4,128)S(1)}, u32[]{:S(2)}, u32[]{:S(2)}) %collective-permute-start.50) | collective-permute-done | bytes 32800 | tf_op jit(solution)/shard_map/ppermute | solution.py:264
  (305 shorter events, 287.6 us)
Async XLA Ops:
  7.2 89.8 %all-gather.5.cloned.1.call-start = ((), (), s32[]{:S(2)}) async-start(), calls=%async_computation.4 | async-start | bytes 9437184 | tf_op jit(solution)/shard_map/all_gather | solution.py:1171
  11.6 231.9 %all-gather.7.cloned.1.call-start = ((), (), s32[]{:S(2)}) async-start(), calls=%async_computation.5 | async-start | bytes 12976128 | tf_op jit(solution)/shard_map/all_gather | solution.py:1171
  21.0 253.0 %all-gather.9.cloned.1.call-start = ((), (), s32[]{:S(2)}) async-start(), calls=%async_computation.6 | async-start | bytes 6488064 | tf_op jit(solution)/shard_map/all_gather | solution.py:1171
  22.0 396.4 %reduce-scatter.5.cloned.1.call-start = ((), (), s32[]{:S(2)}) async-start(), calls=%async_computation.7 | async-start | bytes 6488064 | tf_op jit(solution)/shard_map/reduce_scatter | solution.py:1174
  22.1 28.7 %collective-permute-start.1 = (bf16[256,2176]{1,0:T(8,128)(2,1)}, bf16[256,2176]{1,0:T(8,128)(2,1)S(1)}, u32[]{:S(2)}, u32[]{:S(2)}) collective-permute-start(bf16[256,2176]{1,0:T(8,128)(2,1)} %norm_in.1.refs_3_.refs_0_), channel_id=1, source_target_pairs={{0,16},{16,0},{8,24},{24,8},{1,17},{17,1},{9,25},{25,9},{2,18},{18... | collective-permute-start | bytes 3342344 | tf_op jit(solution)/shard_map/ppermute | solution.py:192
  25.2 28.6 %collective-permute-start = (bf16[256,2176]{1,0:T(8,128)(2,1)}, bf16[256,2176]{1,0:T(8,128)(2,1)S(1)}, u32[]{:S(2)}, u32[]{:S(2)}) collective-permute-start(bf16[256,2176]{1,0:T(8,128)(2,1)} %norm_in.1.refs_3_.refs_0_), channel_id=1, source_target_pairs={{0,8},{8,0},{16,24},{24,16},{1,9},{9,1},{17,25},{25,17},{2,10},{10... | collective-permute-start | bytes 3342344 | tf_op jit(solution)/shard_map/ppermute | solution.py:188
  26.6 46.7 %collective-permute-start.5 = (bf16[256,2048]{1,0:T(8,128)(2,1)}, bf16[256,2048]{1,0:T(8,128)(2,1)S(1)}, u32[]{:S(2)}, u32[]{:S(2)}) collective-permute-start(bf16[256,2048]{1,0:T(8,128)(2,1)} %refs_6_.3), channel_id=1, source_target_pairs={{0,16},{16,0},{8,24},{24,8},{1,17},{17,1},{9,25},{25,9},{2,18},{18... | collective-permute-start | bytes 3145736 | tf_op jit(solution)/shard_map/ppermute | solution.py:192
  27.2 49.0 %collective-permute-start.4 = (bf16[256,2048]{1,0:T(8,128)(2,1)}, bf16[256,2048]{1,0:T(8,128)(2,1)S(1)}, u32[]{:S(2)}, u32[]{:S(2)}) collective-permute-start(bf16[256,2048]{1,0:T(8,128)(2,1)} %refs_6_.3), channel_id=1, source_target_pairs={{0,8},{8,0},{16,24},{24,16},{1,9},{9,1},{17,25},{25,17},{2,10},{10... | collective-permute-start | bytes 3145736 | tf_op jit(solution)/shard_map/ppermute | solution.py:188
  51.7 35.7 %collective-permute-start.3 = (bf16[128,2176]{1,0:T(8,128)(2,1)}, bf16[128,2176]{1,0:T(8,128)(2,1)}, u32[]{:S(2)}, u32[]{:S(2)}) collective-permute-start(bf16[128,2176]{1,0:T(8,128)(2,1)} %slice.85), channel_id=1, source_target_pairs={{0,8},{8,0},{16,24},{24,16},{1,9},{9,1},{17,25},{25,17},{2,10},{10... | collective-permute-start | bytes 1671176 | tf_op jit(solution)/shard_map/ppermute | solution.py:188
  54.7 32.7 %collective-permute-start.2 = (bf16[128,2176]{1,0:T(8,128)(2,1)}, bf16[128,2176]{1,0:T(8,128)(2,1)}, u32[]{:S(2)}, u32[]{:S(2)}) collective-permute-start(bf16[128,2176]{1,0:T(8,128)(2,1)} %slice.84), channel_id=1, source_target_pairs={{0,16},{16,0},{8,24},{24,8},{1,17},{17,1},{9,25},{25,9},{2,18},{18... | collective-permute-start | bytes 1671176 | tf_op jit(solution)/shard_map/ppermute | solution.py:192
  147.7 26.8 %collective-permute-start.13 = (bf16[256,2176]{1,0:T(8,128)(2,1)}, bf16[256,2176]{1,0:T(8,128)(2,1)S(1)}, u32[]{:S(2)}, u32[]{:S(2)}) collective-permute-start(bf16[256,2176]{1,0:T(8,128)(2,1)} %get-tuple-element.78), channel_id=1, source_target_pairs={{0,16},{16,0},{8,24},{24,8},{1,17},{17,1},{9,25},{25,9},{2,18},{18... | collective-permute-start | bytes 3342344 | tf_op jit(solution)/shard_map/ppermute | solution.py:192
  149.1 26.6 %collective-permute-start.12 = (bf16[256,2176]{1,0:T(8,128)(2,1)}, bf16[256,2176]{1,0:T(8,128)(2,1)S(1)}, u32[]{:S(2)}, u32[]{:S(2)}) collective-permute-start(bf16[256,2176]{1,0:T(8,128)(2,1)} %get-tuple-element.77.refs_1_), channel_id=1, source_target_pairs={{0,8},{8,0},{16,24},{24,16},{1,9},{9,1},{17,25},{25,17},{2,10},{10... | collective-permute-start | bytes 3342344 | tf_op jit(solution)/shard_map/ppermute | solution.py:188
  273.8 183.7 %reduce-scatter.7.cloned.1.call-start = ((), (), s32[]{:S(2)}) async-start(), calls=%async_computation.8 | async-start | bytes 12976128 | tf_op jit(solution)/shard_map/reduce_scatter | solution.py:1174
  286.2 54.1 %collective-permute-start.21 = (bf16[256,2048]{1,0:T(8,128)(2,1)}, bf16[256,2048]{1,0:T(8,128)(2,1)S(1)}, u32[]{:S(2)}, u32[]{:S(2)}) collective-permute-start(bf16[256,2048]{1,0:T(8,128)(2,1)} %get-tuple-element.85), channel_id=1, source_target_pairs={{0,16},{16,0},{8,24},{24,8},{1,17},{17,1},{9,25},{25,9},{2,18},{18... | collective-permute-start | bytes 3145736 | tf_op jit(solution)/shard_map/ppermute | solution.py:192
  287.2 53.2 %collective-permute-start.20 = (bf16[256,2048]{1,0:T(8,128)(2,1)}, bf16[256,2048]{1,0:T(8,128)(2,1)S(1)}, u32[]{:S(2)}, u32[]{:S(2)}) collective-permute-start(bf16[256,2048]{1,0:T(8,128)(2,1)} %get-tuple-element.84.refs_4_), channel_id=1, source_target_pairs={{0,8},{8,0},{16,24},{24,16},{1,9},{9,1},{17,25},{25,17},{2,10},{10... | collective-permute-start | bytes 3145736 | tf_op jit(solution)/shard_map/ppermute | solution.py:188
  340.3 221.3 %reduce-scatter.11.cloned.1.call-start = ((), (), s32[]{:S(2)}) async-start(), calls=%async_computation.10 | async-start | bytes 4718592 | tf_op jit(solution)/shard_map/reduce_scatter | solution.py:1174
  448.3 118.8 %reduce-scatter.9.cloned.1.call-start = ((), (), s32[]{:S(2)}) async-start(), calls=%async_computation.9 | async-start | bytes 4718592 | tf_op jit(solution)/shard_map/reduce_scatter | solution.py:1174
  457.4 56.2 %collective-permute-start.39 = (bf16[256,2816]{1,0:T(8,128)(2,1)}, bf16[256,2816]{1,0:T(8,128)(2,1)S(1)}, u32[]{:S(2)}, u32[]{:S(2)}) collective-permute-start(bf16[256,2816]{1,0:T(8,128)(2,1)} %reduce-scatter.7.cloned.1.call-done.refs_1_), channel_id=1, source_target_pairs={{0,16},{16,0},{8,24},{24,8},{1,17},{17,1},{9,25},{25,9},{2,18},{18... | collective-permute-start | bytes 4325384 | tf_op jit(solution)/shard_map/ppermute | solution.py:192
  458.9 56.5 %collective-permute-start.38 = (bf16[256,2816]{1,0:T(8,128)(2,1)}, bf16[256,2816]{1,0:T(8,128)(2,1)S(1)}, u32[]{:S(2)}, u32[]{:S(2)}) collective-permute-start(bf16[256,2816]{1,0:T(8,128)(2,1)} %reduce-scatter.7.cloned.1.call-done.refs_1_), channel_id=1, source_target_pairs={{0,8},{8,0},{16,24},{24,16},{1,9},{9,1},{17,25},{25,17},{2,10},{10... | collective-permute-start | bytes 4325384 | tf_op jit(solution)/shard_map/ppermute | solution.py:188
  461.4 41.3 %collective-permute-start.36 = (bf16[96,2048]{1,0:T(8,128)(2,1)S(1)}, bf16[96,2048]{1,0:T(8,128)(2,1)S(1)}, u32[]{:S(2)}, u32[]{:S(2)}) collective-permute-start(bf16[96,2048]{1,0:T(8,128)(2,1)S(1)} %slice.93), channel_id=1, source_target_pairs={{0,16},{16,0},{8,24},{24,8},{1,17},{17,1},{9,25},{25,9},{2,18},{18... | collective-permute-start | bytes 1179656 | tf_op jit(solution)/shard_map/ppermute | solution.py:192
  463.0 38.2 %collective-permute-start.37 = (bf16[80,2048]{1,0:T(8,128)(2,1)S(1)}, bf16[80,2048]{1,0:T(8,128)(2,1)S(1)}, u32[]{:S(2)}, u32[]{:S(2)}) collective-permute-start(bf16[80,2048]{1,0:T(8,128)(2,1)S(1)} %slice.94), channel_id=1, source_target_pairs={{0,8},{8,0},{16,24},{24,16},{1,9},{9,1},{17,25},{25,17},{2,10},{10... | collective-permute-start | bytes 983048 | tf_op jit(solution)/shard_map/ppermute | solution.py:188
  501.2 26.3 %collective-permute-start.34 = (bf16[256,2048]{1,0:T(8,128)(2,1)}, bf16[256,2048]{1,0:T(8,128)(2,1)}, u32[]{:S(2)}, u32[]{:S(2)}) collective-permute-start(bf16[256,2048]{1,0:T(8,128)(2,1)} %get-tuple-element.112.refs_2_), channel_id=1, source_target_pairs={{0,8},{8,0},{16,24},{24,16},{1,9},{9,1},{17,25},{25,17},{2,10},{10... | collective-permute-start | bytes 3145736 | tf_op jit(solution)/shard_map/ppermute | solution.py:188
  514.7 28.3 %collective-permute-start.43 = (bf16[128,2816]{1,0:T(8,128)(2,1)}, bf16[128,2816]{1,0:T(8,128)(2,1)}, u32[]{:S(2)}, u32[]{:S(2)}) collective-permute-start(bf16[128,2816]{1,0:T(8,128)(2,1)} %slice.96), channel_id=1, source_target_pairs={{0,8},{8,0},{16,24},{24,16},{1,9},{9,1},{17,25},{25,17},{2,10},{10... | collective-permute-start | bytes 2162696 | tf_op jit(solution)/shard_map/ppermute | solution.py:188
  516.4 26.6 %collective-permute-start.42 = (bf16[128,2816]{1,0:T(8,128)(2,1)}, bf16[128,2816]{1,0:T(8,128)(2,1)}, u32[]{:S(2)}, u32[]{:S(2)}) collective-permute-start(bf16[128,2816]{1,0:T(8,128)(2,1)} %slice.95), channel_id=1, source_target_pairs={{0,16},{16,0},{8,24},{24,8},{1,17},{17,1},{9,25},{25,9},{2,18},{18... | collective-permute-start | bytes 2162696 | tf_op jit(solution)/shard_map/ppermute | solution.py:192
  (93 other events, 1055.6 us)
Sparse Core Ops, SparseCore 0:
  11.7 84.6 all-gather.4
  98.7 109.3 all-gather.6
  209.7 58.5 all-gather.8
  273.9 62.4 reduce-scatter.4
  340.4 116.9 reduce-scatter.6
  459.6 49.2 reduce-scatter.10
  513.8 46.5 reduce-scatter.8

commit v5 on v4

--- a/solution.py
+++ b/solution.py
@@ -23,7 +23,7 @@
 NN = (((1,), (0,)), ((), ()))
 NT = (((1,), (1,)), ((), ()))
 TN = (((0,), (0,)), ((), ()))
-COSTS = {"finish_in": 65, "finish_mid": 210}
+COSTS = {"finish_in": 73, "finish_mid": 210}
 SMALL = pl.CostEstimate(flops=1024, bytes_accessed=1024, transcendentals=0)
 ANY = pl.BlockSpec(memory_space=pl.ANY)
 SMEM = pl.BlockSpec(memory_space=pltpu.SMEM)
@@ -262,7 +262,7 @@
             for step in range(2, count, 2)
         )
     across = lax.ppermute(value, "grp", [(one, 3 - one) for one in range(GRP)])
-    return value + send_x(value) + send_y(value) + across
+    return value, send_x(value), send_y(value), across
 
 
 def split(column):
@@ -1277,7 +1277,7 @@
     by_x, by_y = send_x(to_x), send_y(to_y)
     down_pieces = second_step(held_down)
     part_pair = outer_sum(
-        "part_pair", normed, grad_pair, width, 2 * own, 256, (to_x,) + down_pieces[3:]
+        "part_pair", normed, grad_pair, width, 2 * own, 256, (to_x,) + down_pieces[3:] + held_ff[1:]
     )
     sum_pair = reduced(part_pair)
     grad_down = place_rows(mine, down_pieces, (part_pair, held_ff[1], held_ff[2]))
@@ -1285,11 +1285,9 @@
     last_y, last_x = send_y(for_y), send_x(for_x)
     pieces = (kept, by_x, by_y, last_y, last_x)
     held_go = start_gather(after(sum_gate_out, pieces[3], pieces[4]))
-    grad_mlp_gate, grad_mlp_up = place_columns(
-        mine, second_step(held_ff), parts, 2, w_ff.shape[1] // 2, True, (for_y,)
-    )
+    ff_pieces = second_step(held_ff)
     grad_tokens, grad_norm_gain = finish_in(
-        pieces, tokens, grad_middle, in_gain, width, (grad_mlp_up,)
+        pieces, tokens, grad_middle, in_gain, width, ff_pieces[3:]
     )
     vectors = sum_everywhere(
         jnp.stack(
@@ -1297,12 +1295,18 @@
         )
     )
     held_pair = start_gather(after(sum_pair, grad_tokens))
-    gate_out_pieces = second_step(held_go)
-    (grad_gate_proj,) = place_columns(mine, gate_out_pieces, parts, 1, own, True)
+    grad_mlp_gate, grad_mlp_up = place_columns(
+        mine, ff_pieces, parts, 2, w_ff.shape[1] // 2, True, (grad_tokens,)
+    )
+    gate_out_pieces = second_step(held_go, (grad_mlp_up,))
+    (grad_gate_proj,) = place_columns(
+        mine, gate_out_pieces, parts, 1, own, True, (grad_mlp_up,)
+    )
     grad_out = place_stacked(mine, gate_out_pieces, own, own, (grad_gate_proj,))
     grad_input, grad_forget = place_columns(
-        mine, second_step(held_pair), parts, 2, own, True, (grad_out, vectors)
-    )
+        mine, second_step(held_pair, (grad_mlp_up,)), parts, 2, own, True, (grad_out,)
+    )
+    vectors = sum(after(vectors, grad_input))
     return (
         block_out,
         grad_tokens,

time: 630 us -> 621 us (0.986)
  waiting for transfers between devices: 206 us -> 198 us
    ppermute x25, waiting for transfers between devices: 121 us -> 136 us  [send_y(): return lax.ppermute(value, 'grp', SWAP_Y)]
    ppermute x25, waiting for transfers between devices: 56.7 us -> 44.9 us  [send_x(): return lax.ppermute(value, 'grp', SWAP_X)]
    ppermute x1, waiting for transfers between devices: 10.9 us -> 0.01 us  [sum_everywhere(): across = lax.ppermute(value, 'grp', [(one, 3 - one) for one in range(GRP)])]
    unnamed x104 -> x110, local copies, waits for them, and re-layouts: 13.1 us -> 15.4 us
  transfers between devices with their start and end apart: 66 -> 66, of which waited for: 30 -> 27; matrix products, arithmetic and copies ran while one was open for 3% -> 3% of each run, Pallas kernels for 45% -> 47%
where the time goes in v5:
time: 621 us; the launch traced here: 617 us
  Pallas kernels  293 us (47%)
  waiting for transfers between devices  198 us (32%)
  starting transfers between devices  64 us (10%)
  local copies, waits for them, and re-layouts  27.1 us (4%)
  blocking collectives  15.6 us (3%)
  between operations  14.8 us (2%)
    pallas_call x38, Pallas kernels, call(): pl.pallas_call(wrapped, grid=grid, in_specs=list(in_specs) + [ANY] * n_de...  285 us
    ppermute x25, waiting for transfers between devices, send_y(): return lax.ppermute(value, 'grp', SWAP_Y)  136 us
    ppermute x25, waiting for transfers between devices, send_x(): return lax.ppermute(value, 'grp', SWAP_X)  44.9 us
    ppermute x25, starting transfers between devices, send_x(): return lax.ppermute(value, 'grp', SWAP_X)  28 us
    ppermute x25, starting transfers between devices, send_y(): return lax.ppermute(value, 'grp', SWAP_Y)  26.8 us
    all_gather x1, blocking collectives, on_device(): ends_back = lax.all_gather(after(ends_back, part_gate_out), 'seq')  15.6 us
    unnamed x110, local copies, waits for them, and re-layouts  15.4 us
  transfers between devices with their start and end apart: 66, of which 27 were waited for; matrix products, arithmetic and copies ran while one was open for 3% of the time, Pallas kernels for 47%

profile of v5, /device:TPU:0, one launch (start us, length us, event | category | flops | bytes accessed | tf_op | source)
XLA Modules:
  0.0 616.9 jit_solution(8548857643985817923)
XLA Ops:
  27.3 23.5 %collective-permute-done.1.refs_2_ = bf16[256,2176]{1,0:T(8,128)(2,1)S(1)} collective-permute-done((bf16[256,2176]{1,0:T(8,128)(2,1)}, bf16[256,2176]{1,0:T(8,128)(2,1)S(1)}, u32[]{:S(2)}, u32[]{:S(2)}) %collective-permute-start.1) | collective-permute-done | bytes 1114144 | tf_op jit(solution)/shard_map/ppermute | solution.py:192
  56.1 17.2 %collective-permute-done.5.refs_4_.refs_2_ = bf16[256,2048]{1,0:T(8,128)(2,1)S(1)} collective-permute-done((bf16[256,2048]{1,0:T(8,128)(2,1)}, bf16[256,2048]{1,0:T(8,128)(2,1)S(1)}, u32[]{:S(2)}, u32[]{:S(2)}) %collective-permute-start.5) | collective-permute-done | bytes 1048608 | tf_op jit(solution)/shard_map/ppermute | solution.py:192
  98.0 9.1 %proj_pair.1 = f32[1024,1024]{1,0:T(8,128)} custom-call(bf16[1024,2176]{1,0:T(8,128)(2,1)} %lay.4.refs_0_, bf16[2048,2048]{1,0:T(8,128)(2,1)} %all-gather.5.cloned.1.call-done.refs_1_.refs_2_.refs_3_, bf16[256,2048]{1,0:T(8,128)(2,1)} %refs_6_.3, bf16[256,2048]{1,0:T(8,128)(2,1)} %copy-done.7, bf16[256,2048]{1,0:T(8,128)(2,1)} %copy-done.6, ...), custom_call_target="tpu_custom_call" | custom-call | flops 1024 | bytes 1024 | tf_op jit(solution)/shard_map/proj_pair/pallas_call | solution.py:42
  107.1 8.1 %scan_forward.1 = (f32[8,128,512]{2,1,0:T(8,128)}, f32[8,128,512]{2,1,0:T(8,128)}, f32[8,512]{1,0:T(8,128)}) custom-call(f32[8,128,128]{2,1,0:T(8,128)} %convert.1.keep_ref.refs_0_.refs_1_, f32[8,128,1024]{2,1,0:T(8,128)} %bitcast.32, f32[1,512]{1,0:T(1,128)} %reshape.194.bias_ref.refs_3_.refs_6_), custom_call_target="tpu_custom_call" | custom-call | flops 1024 | bytes 1024 | tf_op jit(solution)/shard_map/scan_forward/pallas_call | solution.py:828
  158.6 15.9 %collective-permute-done.13.refs_2_ = bf16[256,2176]{1,0:T(8,128)(2,1)S(1)} collective-permute-done((bf16[256,2176]{1,0:T(8,128)(2,1)}, bf16[256,2176]{1,0:T(8,128)(2,1)S(1)}, u32[]{:S(2)}, u32[]{:S(2)}) %collective-permute-start.13) | collective-permute-done | bytes 1114144 | tf_op jit(solution)/shard_map/ppermute | solution.py:192
  182.1 11.8 %collective-permute-done.14.refs_3_ = bf16[128,2176]{1,0:T(8,128)(2,1)S(1)} collective-permute-done((bf16[128,2176]{1,0:T(8,128)(2,1)}, bf16[128,2176]{1,0:T(8,128)(2,1)S(1)}, u32[]{:S(2)}, u32[]{:S(2)}) %collective-permute-start.14) | collective-permute-done | bytes 557088 | tf_op jit(solution)/shard_map/ppermute | solution.py:192
  204.5 21.0 %collective-permute-done.17.refs_2_ = bf16[256,2048]{1,0:T(8,128)(2,1)S(1)} collective-permute-done((bf16[256,2048]{1,0:T(8,128)(2,1)}, bf16[256,2048]{1,0:T(8,128)(2,1)S(1)}, u32[]{:S(2)}, u32[]{:S(2)}) %collective-permute-start.17) | collective-permute-done | bytes 1048608 | tf_op jit(solution)/shard_map/ppermute | solution.py:192
  228.4 8.9 %collective-permute-done.19.refs_4_ = bf16[128,2048]{1,0:T(8,128)(2,1)S(1)} collective-permute-done((bf16[128,2048]{1,0:T(8,128)(2,1)S(1)}, bf16[128,2048]{1,0:T(8,128)(2,1)S(1)}, u32[]{:S(2)}, u32[]{:S(2)}) %collective-permute-start.19) | collective-permute-done | bytes 524320 | tf_op jit(solution)/shard_map/ppermute | solution.py:188
  243.5 20.0 %feed_forward.1 = (bf16[1024,1408]{1,0:T(8,128)(2,1)}, f32[1024,1408]{1,0:T(8,128)}, f32[1024,1408]{1,0:T(8,128)}) custom-call(bf16[1024,2048]{1,0:T(8,128)(2,1)} %lay.6.refs_0_, bf16[2048,2816]{1,0:T(8,128)(2,1)} %all-gather.7.cloned.1.call-done.refs_1_), custom_call_target="tpu_custom_call" | custom-call | flops 1024 | bytes 1024 | tf_op jit(solution)/shard_map/feed_forward/pallas_call | solution.py:42
  263.6 10.2 %part_down.1.refs_2_ = bf16[1408,2048]{1,0:T(8,128)(2,1)} custom-call(bf16[1024,1408]{1,0:T(8,128)(2,1)} %get-tuple-element.90.refs_0_, bf16[1024,2048]{1,0:T(8,128)(2,1)} %lay.5.refs_4_.refs_1_.refs_0_), custom_call_target="tpu_custom_call" | custom-call | flops 1024 | bytes 1024 | tf_op jit(solution)/shard_map/part_down/pallas_call | solution.py:42
  274.0 12.2 %down.1 = (bf16[256,2048]{1,0:T(8,128)(2,1)}, bf16[256,2048]{1,0:T(8,128)(2,1)}, f32[512,2048]{1,0:T(8,128)}) custom-call(bf16[1024,1408]{1,0:T(8,128)(2,1)} %get-tuple-element.90.refs_0_, bf16[1408,2048]{1,0:T(8,128)(2,1)} %all-gather.9.cloned.1.call-done.refs_1_, bf16[1408,2048]{1,0:T(8,128)(2,1)} %part_down.1.refs_2_), custom_call_target="tpu_custom_call" | custom-call | flops 1024 | bytes 1024 | tf_op jit(solution)/shard_map/down/pallas_call | solution.py:42
  288.6 14.0 %feed_back.1.refs_0_.refs_1_ = bf16[1024,2816]{1,0:T(8,128)(2,1)} custom-call(bf16[1024,2048]{1,0:T(8,128)(2,1)} %lay.5.refs_4_.refs_1_.refs_0_, bf16[1408,2048]{1,0:T(8,128)(2,1)} %all-gather.9.cloned.1.call-done.refs_1_, f32[1024,1408]{1,0:T(8,128)} %get-tuple-element.94.refs_2_, f32[1024,1408]{1,0:T(8,128)} %get-tuple-element.95.refs_3_, ...), custom_call_target="tpu_custom_call" | custom-call | flops 1024 | bytes 1024 | tf_op jit(solution)/shard_map/feed_back/pallas_call | solution.py:42
  302.7 18.2 %grad_mid.1 = (bf16[256,2048]{1,0:T(8,128)(2,1)}, bf16[256,2048]{1,0:T(8,128)(2,1)}, f32[512,2048]{1,0:T(8,128)}) custom-call(bf16[1024,2816]{1,0:T(8,128)(2,1)} %feed_back.1.refs_0_.refs_1_, bf16[2048,2816]{1,0:T(8,128)(2,1)} %all-gather.7.cloned.1.call-done.refs_1_), custom_call_target="tpu_custom_call" | custom-call | flops 1024 | bytes 1024 | tf_op jit(solution)/shard_map/grad_mid/pallas_call | solution.py:42
  322.4 17.8 %part_ff.1.refs_3_ = bf16[2048,2816]{1,0:T(8,128)(2,1)} custom-call(bf16[1024,2048]{1,0:T(8,128)(2,1)} %lay.6.refs_0_, bf16[1024,2816]{1,0:T(8,128)(2,1)} %feed_back.1.refs_0_.refs_1_, bf16[256,2048]{1,0:T(8,128)(2,1)} %get-tuple-element.96.refs_2_), custom_call_target="tpu_custom_call" | custom-call | flops 1024 | bytes 1024 | tf_op jit(solution)/shard_map/part_ff/pallas_call | solution.py:42
  351.5 8.1 %collective-permute-done.23.refs_4_ = bf16[128,2048]{1,0:T(8,128)(2,1)S(1)} collective-permute-done((bf16[128,2048]{1,0:T(8,128)(2,1)}, bf16[128,2048]{1,0:T(8,128)(2,1)S(1)}, u32[]{:S(2)}, u32[]{:S(2)}) %collective-permute-start.23) | collective-permute-done | bytes 524320 | tf_op jit(solution)/shard_map/ppermute | solution.py:188
  377.6 21.5 %collective-permute-done.29.refs_2_ = bf16[256,2176]{1,0:T(8,128)(2,1)S(1)} collective-permute-done((bf16[256,2176]{1,0:T(8,128)(2,1)}, bf16[256,2176]{1,0:T(8,128)(2,1)S(1)}, u32[]{:S(2)}, u32[]{:S(2)}) %collective-permute-start.29) | collective-permute-done | bytes 1114144 | tf_op jit(solution)/shard_map/ppermute | solution.py:192
  425.5 9.4 %scan_backward.1 = (f32[8,128,512]{2,1,0:T(8,128)}, f32[8,128,512]{2,1,0:T(8,128)}, f32[8,512]{1,0:T(8,128)}, bf16[8,128,512]{2,1,0:T(8,128)(2,1)}, f32[1,512]{1,0:T(1,128)}) custom-call(f32[8,128,128]{2,1,0:T(8,128)} %convert.1.keep_ref.refs_0_.refs_1_, f32[8,128,1024]{2,1,0:T(8,128)} %bitcast.33, f32[8,128,512]{2,1,0:T(8,128)} %bitcast.38, ...), custom_call_target="tpu_custom_call" | custom-call | flops 1024 | bytes 1024 | tf_op jit(solution)/shard_map/scan_backward/pallas_call | solution.py:42
  448.4 9.1 %reduce-scatter.7.cloned.1.call-done.refs_1_ = bf16[256,2816]{1,0:T(8,128)(2,1)} async-done(((bf16[2048,2816]{1,0:T(8,128)(2,1)}), bf16[256,2816]{1,0:T(8,128)(2,1)}) %reduce-scatter.7.cloned.1.call-update) | async-done | bytes 1441808 | tf_op jit(solution)/shard_map/reduce_scatter | solution.py:1174
  463.7 15.6 %all-gather = f32[64,512]{1,0:T(8,128)} all-gather(f32[8,512]{1,0:T(8,128)S(1)} %copy-done.45), channel_id=2, replica_groups=mesh['grp'=4,'seq'=8] {'seq'}, dimensions={0}, use_global_device_ids=true | all-gather | bytes 147456 | tf_op jit(solution)/shard_map/all_gather | solution.py:1268
  486.9 12.4 %grad_in.1 = (bf16[256,2048]{1,0:T(8,128)(2,1)}, bf16[256,2048]{1,0:T(8,128)(2,1)}, f32[512,2048]{1,0:T(8,128)}) custom-call(bf16[1024,1024]{1,0:T(8,128)(2,1)} %bitcast.39, bf16[1024,512]{1,0:T(8,128)(2,1)} %bitcast.47, bf16[2048,2048]{1,0:T(8,128)(2,1)} %all-gather.5.cloned.1.call-done.refs_1_.refs_2_.refs_3_, ...), custom_call_target="tpu_custom_call" | custom-call | flops 1024 | bytes 1024 | tf_op jit(solution)/shard_map/grad_in/pallas_call | solution.py:42
  504.8 10.2 %part_pair.1.refs_6_ = bf16[2048,1024]{1,0:T(8,128)(2,1)} custom-call(bf16[1024,2176]{1,0:T(8,128)(2,1)} %lay.4.refs_0_, bf16[1024,1024]{1,0:T(8,128)(2,1)} %bitcast.40, bf16[256,2048]{1,0:T(8,128)(2,1)} %get-tuple-element.120.refs_2_, bf16[96,2048]{1,0:T(8,128)(2,1)} %copy-done.24, bf16[80,2048]{1,0:T(8,128)(2,1)} %copy-done.25, ...), custom_call_target="tpu_custom_call" | custom-call | flops 1024 | bytes 1024 | tf_op jit(solution)/shard_map/part_pair/pallas_call | solution.py:42
  518.3 8.1 %place_rows.1 = f32[4,176,2048]{2,1,0:T(8,128)} custom-call(s32[1]{0:T(128)} %bitcast.6.refs_0_, bf16[176,2048]{1,0:T(8,128)(2,1)} %reduce-scatter.5.cloned.1.call-done.refs_1_, bf16[176,2048]{1,0:T(8,128)(2,1)} %copy-done.8, bf16[176,2048]{1,0:T(8,128)(2,1)} %copy-done.11, bf16[96,2048]{1,0:T(8,128)(2,1)} %copy-done.24, bf16[80,2048]{1,0:T(8,128)(2,1)} %copy-done.25, ...), custom_call_target="tpu_custom_call" | custom-call | flops 1024 | bytes 1024 | tf_op jit(solution)/shard_map/place_rows/pallas_call | solution.py:42
  534.7 16.9 %collective-permute-done.40.refs_3_ = bf16[128,2048]{1,0:T(8,128)(2,1)S(1)} collective-permute-done((bf16[128,2048]{1,0:T(8,128)(2,1)}, bf16[128,2048]{1,0:T(8,128)(2,1)S(1)}, u32[]{:S(2)}, u32[]{:S(2)}) %collective-permute-start.40) | collective-permute-done | bytes 524320 | tf_op jit(solution)/shard_map/ppermute | solution.py:192
  570.3 9.7 %place_columns.3 = (f32[256,5632]{1,0:T(8,128)}, f32[256,5632]{1,0:T(8,128)}) custom-call(s32[1]{0:T(128)} %bitcast.6.refs_0_, bf16[256,2816]{1,0:T(8,128)(2,1)} %reduce-scatter.7.cloned.1.call-done.refs_1_, bf16[256,2816]{1,0:T(8,128)(2,1)} %copy-done.4, bf16[256,2816]{1,0:T(8,128)(2,1)} %copy-done.2, bf16[128,2816]{1,0:T(8,128)(2,1)} %copy-done.31, ...), custom_call_target="tpu_custom_call" | custom-call | flops 1024 | bytes 1024 | tf_op jit(solution)/shard_map/place_columns/pallas_call | solution.py:42
  (311 shorter events, 273.3 us)
Async XLA Ops:
  7.2 89.8 %all-gather.5.cloned.1.call-start = ((), (), s32[]{:S(2)}) async-start(), calls=%async_computation.4 | async-start | bytes 9437184 | tf_op jit(solution)/shard_map/all_gather | solution.py:1171
  11.6 231.9 %all-gather.7.cloned.1.call-start = ((), (), s32[]{:S(2)}) async-start(), calls=%async_computation.5 | async-start | bytes 12976128 | tf_op jit(solution)/shard_map/all_gather | solution.py:1171
  21.0 253.0 %all-gather.9.cloned.1.call-start = ((), (), s32[]{:S(2)}) async-start(), calls=%async_computation.6 | async-start | bytes 6488064 | tf_op jit(solution)/shard_map/all_gather | solution.py:1171
  22.0 396.4 %reduce-scatter.5.cloned.1.call-start = ((), (), s32[]{:S(2)}) async-start(), calls=%async_computation.7 | async-start | bytes 6488064 | tf_op jit(solution)/shard_map/reduce_scatter | solution.py:1174
  22.1 28.7 %collective-permute-start.1 = (bf16[256,2176]{1,0:T(8,128)(2,1)}, bf16[256,2176]{1,0:T(8,128)(2,1)S(1)}, u32[]{:S(2)}, u32[]{:S(2)}) collective-permute-start(bf16[256,2176]{1,0:T(8,128)(2,1)} %norm_in.1.refs_3_.refs_0_), channel_id=1, source_target_pairs={{0,16},{16,0},{8,24},{24,8},{1,17},{17,1},{9,25},{25,9},{2,18},{18... | collective-permute-start | bytes 3342344 | tf_op jit(solution)/shard_map/ppermute | solution.py:192
  25.2 28.6 %collective-permute-start = (bf16[256,2176]{1,0:T(8,128)(2,1)}, bf16[256,2176]{1,0:T(8,128)(2,1)S(1)}, u32[]{:S(2)}, u32[]{:S(2)}) collective-permute-start(bf16[256,2176]{1,0:T(8,128)(2,1)} %norm_in.1.refs_3_.refs_0_), channel_id=1, source_target_pairs={{0,8},{8,0},{16,24},{24,16},{1,9},{9,1},{17,25},{25,17},{2,10},{10... | collective-permute-start | bytes 3342344 | tf_op jit(solution)/shard_map/ppermute | solution.py:188
  26.6 46.7 %collective-permute-start.5 = (bf16[256,2048]{1,0:T(8,128)(2,1)}, bf16[256,2048]{1,0:T(8,128)(2,1)S(1)}, u32[]{:S(2)}, u32[]{:S(2)}) collective-permute-start(bf16[256,2048]{1,0:T(8,128)(2,1)} %refs_6_.3), channel_id=1, source_target_pairs={{0,16},{16,0},{8,24},{24,8},{1,17},{17,1},{9,25},{25,9},{2,18},{18... | collective-permute-start | bytes 3145736 | tf_op jit(solution)/shard_map/ppermute | solution.py:192
  27.2 49.0 %collective-permute-start.4 = (bf16[256,2048]{1,0:T(8,128)(2,1)}, bf16[256,2048]{1,0:T(8,128)(2,1)S(1)}, u32[]{:S(2)}, u32[]{:S(2)}) collective-permute-start(bf16[256,2048]{1,0:T(8,128)(2,1)} %refs_6_.3), channel_id=1, source_target_pairs={{0,8},{8,0},{16,24},{24,16},{1,9},{9,1},{17,25},{25,17},{2,10},{10... | collective-permute-start | bytes 3145736 | tf_op jit(solution)/shard_map/ppermute | solution.py:188
  51.7 35.7 %collective-permute-start.3 = (bf16[128,2176]{1,0:T(8,128)(2,1)}, bf16[128,2176]{1,0:T(8,128)(2,1)}, u32[]{:S(2)}, u32[]{:S(2)}) collective-permute-start(bf16[128,2176]{1,0:T(8,128)(2,1)} %slice.85), channel_id=1, source_target_pairs={{0,8},{8,0},{16,24},{24,16},{1,9},{9,1},{17,25},{25,17},{2,10},{10... | collective-permute-start | bytes 1671176 | tf_op jit(solution)/shard_map/ppermute | solution.py:188
  54.7 32.7 %collective-permute-start.2 = (bf16[128,2176]{1,0:T(8,128)(2,1)}, bf16[128,2176]{1,0:T(8,128)(2,1)}, u32[]{:S(2)}, u32[]{:S(2)}) collective-permute-start(bf16[128,2176]{1,0:T(8,128)(2,1)} %slice.84), channel_id=1, source_target_pairs={{0,16},{16,0},{8,24},{24,8},{1,17},{17,1},{9,25},{25,9},{2,18},{18... | collective-permute-start | bytes 1671176 | tf_op jit(solution)/shard_map/ppermute | solution.py:192
  147.7 26.9 %collective-permute-start.13 = (bf16[256,2176]{1,0:T(8,128)(2,1)}, bf16[256,2176]{1,0:T(8,128)(2,1)S(1)}, u32[]{:S(2)}, u32[]{:S(2)}) collective-permute-start(bf16[256,2176]{1,0:T(8,128)(2,1)} %get-tuple-element.86), channel_id=1, source_target_pairs={{0,16},{16,0},{8,24},{24,8},{1,17},{17,1},{9,25},{25,9},{2,18},{18... | collective-permute-start | bytes 3342344 | tf_op jit(solution)/shard_map/ppermute | solution.py:192
  149.1 26.6 %collective-permute-start.12 = (bf16[256,2176]{1,0:T(8,128)(2,1)}, bf16[256,2176]{1,0:T(8,128)(2,1)S(1)}, u32[]{:S(2)}, u32[]{:S(2)}) collective-permute-start(bf16[256,2176]{1,0:T(8,128)(2,1)} %get-tuple-element.85.refs_1_), channel_id=1, source_target_pairs={{0,8},{8,0},{16,24},{24,16},{1,9},{9,1},{17,25},{25,17},{2,10},{10... | collective-permute-start | bytes 3342344 | tf_op jit(solution)/shard_map/ppermute | solution.py:188
  273.7 183.7 %reduce-scatter.7.cloned.1.call-start = ((), (), s32[]{:S(2)}) async-start(), calls=%async_computation.8 | async-start | bytes 12976128 | tf_op jit(solution)/shard_map/reduce_scatter | solution.py:1174
  286.2 54.2 %collective-permute-start.21 = (bf16[256,2048]{1,0:T(8,128)(2,1)}, bf16[256,2048]{1,0:T(8,128)(2,1)S(1)}, u32[]{:S(2)}, u32[]{:S(2)}) collective-permute-start(bf16[256,2048]{1,0:T(8,128)(2,1)} %get-tuple-element.93), channel_id=1, source_target_pairs={{0,16},{16,0},{8,24},{24,8},{1,17},{17,1},{9,25},{25,9},{2,18},{18... | collective-permute-start | bytes 3145736 | tf_op jit(solution)/shard_map/ppermute | solution.py:192
  287.2 53.2 %collective-permute-start.20 = (bf16[256,2048]{1,0:T(8,128)(2,1)}, bf16[256,2048]{1,0:T(8,128)(2,1)S(1)}, u32[]{:S(2)}, u32[]{:S(2)}) collective-permute-start(bf16[256,2048]{1,0:T(8,128)(2,1)} %get-tuple-element.92.refs_4_), channel_id=1, source_target_pairs={{0,8},{8,0},{16,24},{24,16},{1,9},{9,1},{17,25},{25,17},{2,10},{10... | collective-permute-start | bytes 3145736 | tf_op jit(solution)/shard_map/ppermute | solution.py:188
  340.3 194.5 %reduce-scatter.11.cloned.1.call-start = ((), (), s32[]{:S(2)}) async-start(), calls=%async_computation.10 | async-start | bytes 4718592 | tf_op jit(solution)/shard_map/reduce_scatter | solution.py:1174
  448.3 114.8 %reduce-scatter.9.cloned.1.call-start = ((), (), s32[]{:S(2)}) async-start(), calls=%async_computation.9 | async-start | bytes 4718592 | tf_op jit(solution)/shard_map/reduce_scatter | solution.py:1174
  457.5 45.1 %collective-permute-start.39 = (bf16[256,2816]{1,0:T(8,128)(2,1)}, bf16[256,2816]{1,0:T(8,128)(2,1)S(1)}, u32[]{:S(2)}, u32[]{:S(2)}) collective-permute-start(bf16[256,2816]{1,0:T(8,128)(2,1)} %reduce-scatter.7.cloned.1.call-done.refs_1_), channel_id=1, source_target_pairs={{0,16},{16,0},{8,24},{24,8},{1,17},{17,1},{9,25},{25,9},{2,18},{18... | collective-permute-start | bytes 4325384 | tf_op jit(solution)/shard_map/ppermute | solution.py:192
  458.9 43.6 %collective-permute-start.38 = (bf16[256,2816]{1,0:T(8,128)(2,1)}, bf16[256,2816]{1,0:T(8,128)(2,1)S(1)}, u32[]{:S(2)}, u32[]{:S(2)}) collective-permute-start(bf16[256,2816]{1,0:T(8,128)(2,1)} %reduce-scatter.7.cloned.1.call-done.refs_1_), channel_id=1, source_target_pairs={{0,8},{8,0},{16,24},{24,16},{1,9},{9,1},{17,25},{25,17},{2,10},{10... | collective-permute-start | bytes 4325384 | tf_op jit(solution)/shard_map/ppermute | solution.py:188
  461.4 41.1 %collective-permute-start.36 = (bf16[96,2048]{1,0:T(8,128)(2,1)S(1)}, bf16[96,2048]{1,0:T(8,128)(2,1)S(1)}, u32[]{:S(2)}, u32[]{:S(2)}) collective-permute-start(bf16[96,2048]{1,0:T(8,128)(2,1)S(1)} %slice.93), channel_id=1, source_target_pairs={{0,16},{16,0},{8,24},{24,8},{1,17},{17,1},{9,25},{25,9},{2,18},{18... | collective-permute-start | bytes 1179656 | tf_op jit(solution)/shard_map/ppermute | solution.py:192
  463.0 38.0 %collective-permute-start.37 = (bf16[80,2048]{1,0:T(8,128)(2,1)S(1)}, bf16[80,2048]{1,0:T(8,128)(2,1)S(1)}, u32[]{:S(2)}, u32[]{:S(2)}) collective-permute-start(bf16[80,2048]{1,0:T(8,128)(2,1)S(1)} %slice.94), channel_id=1, source_target_pairs={{0,8},{8,0},{16,24},{24,16},{1,9},{9,1},{17,25},{25,17},{2,10},{10... | collective-permute-start | bytes 983048 | tf_op jit(solution)/shard_map/ppermute | solution.py:188
  499.3 27.0 %collective-permute-start.35 = (bf16[256,2048]{1,0:T(8,128)(2,1)}, bf16[256,2048]{1,0:T(8,128)(2,1)}, u32[]{:S(2)}, u32[]{:S(2)}) collective-permute-start(bf16[256,2048]{1,0:T(8,128)(2,1)} %get-tuple-element.121), channel_id=1, source_target_pairs={{0,16},{16,0},{8,24},{24,8},{1,17},{17,1},{9,25},{25,9},{2,18},{18... | collective-permute-start | bytes 3145736 | tf_op jit(solution)/shard_map/ppermute | solution.py:192
  517.3 38.3 %collective-permute-start.43 = (bf16[128,2816]{1,0:T(8,128)(2,1)}, bf16[128,2816]{1,0:T(8,128)(2,1)S(1)}, u32[]{:S(2)}, u32[]{:S(2)}) collective-permute-start(bf16[128,2816]{1,0:T(8,128)(2,1)} %slice.96), channel_id=1, source_target_pairs={{0,8},{8,0},{16,24},{24,16},{1,9},{9,1},{17,25},{25,17},{2,10},{10... | collective-permute-start | bytes 2162696 | tf_op jit(solution)/shard_map/ppermute | solution.py:188
  517.9 37.7 %collective-permute-start.42 = (bf16[128,2816]{1,0:T(8,128)(2,1)S(1)}, bf16[128,2816]{1,0:T(8,128)(2,1)S(1)}, u32[]{:S(2)}, u32[]{:S(2)}) collective-permute-start(bf16[128,2816]{1,0:T(8,128)(2,1)S(1)} %slice.95), channel_id=1, source_target_pairs={{0,16},{16,0},{8,24},{24,8},{1,17},{17,1},{9,25},{25,9},{2,18},{18... | collective-permute-start | bytes 2162696 | tf_op jit(solution)/shard_map/ppermute | solution.py:192
  (96 other events, 1062.3 us)
Sparse Core Ops, SparseCore 0:
  11.7 84.6 all-gather.4
  98.7 109.3 all-gather.6
  209.7 58.5 all-gather.8
  273.9 62.5 reduce-scatter.4
  340.4 116.9 reduce-scatter.6
  460.2 49.2 reduce-scatter.10
  515.2 46.5 reduce-scatter.8

commit v6 on v5

--- a/solution.py
+++ b/solution.py
@@ -19,7 +19,7 @@
 SWAP_Y = [(0, 2), (2, 0), (1, 3), (3, 1)]
 TO_X, TO_Y, KEPT = (2, 6), (5, 7), (0, 1, 3, 4)
 VMEM_LIMIT = 56 * 1024 * 1024
-PLACE_STEP = 32
+PLACE_STEP = 64
 NN = (((1,), (0,)), ((), ()))
 NT = (((1,), (1,)), ((), ()))
 TN = (((0,), (0,)), ((), ()))

time: 621 us -> 615 us (level)
  transfers between devices with their start and end apart: 66 -> 66, of which waited for: 27 -> 27; matrix products, arithmetic and copies ran while one was open for 3% -> 3% of each run, Pallas kernels for 47% -> 46%
where the time goes in v6:
time: 615 us; the launch traced here: 612 us
  Pallas kernels  288 us (47%)
  waiting for transfers between devices  198 us (32%)
  starting transfers between devices  64 us (10%)
  local copies, waits for them, and re-layouts  27.1 us (4%)
  blocking collectives  15.6 us (3%)
  between operations  14.8 us (2%)
    pallas_call x38, Pallas kernels, call(): pl.pallas_call(wrapped, grid=grid, in_specs=list(in_specs) + [ANY] * n_de...  280 us
    ppermute x25, waiting for transfers between devices, send_y(): return lax.ppermute(value, 'grp', SWAP_Y)  136 us
    ppermute x25, waiting for transfers between devices, send_x(): return lax.ppermute(value, 'grp', SWAP_X)  44.9 us
    ppermute x25, starting transfers between devices, send_x(): return lax.ppermute(value, 'grp', SWAP_X)  28.1 us
    ppermute x25, starting transfers between devices, send_y(): return lax.ppermute(value, 'grp', SWAP_Y)  26.8 us
    all_gather x1, blocking collectives, on_device(): ends_back = lax.all_gather(after(ends_back, part_gate_out), 'seq')  15.6 us
    unnamed x110, local copies, waits for them, and re-layouts  15.4 us
  transfers between devices with their start and end apart: 66, of which 27 were waited for; matrix products, arithmetic and copies ran while one was open for 3% of the time, Pallas kernels for 46%

profile of v6, /device:TPU:0, one launch (start us, length us, event | category | flops | bytes accessed | tf_op | source)
XLA Modules:
  0.0 611.9 jit_solution(6791187986210987000)
XLA Ops:
  27.3 23.5 %collective-permute-done.1.refs_2_ = bf16[256,2176]{1,0:T(8,128)(2,1)S(1)} collective-permute-done((bf16[256,2176]{1,0:T(8,128)(2,1)}, bf16[256,2176]{1,0:T(8,128)(2,1)S(1)}, u32[]{:S(2)}, u32[]{:S(2)}) %collective-permute-start.1) | collective-permute-done | bytes 1114144 | tf_op jit(solution)/shard_map/ppermute | solution.py:192
  56.1 17.2 %collective-permute-done.5.refs_4_.refs_2_ = bf16[256,2048]{1,0:T(8,128)(2,1)S(1)} collective-permute-done((bf16[256,2048]{1,0:T(8,128)(2,1)}, bf16[256,2048]{1,0:T(8,128)(2,1)S(1)}, u32[]{:S(2)}, u32[]{:S(2)}) %collective-permute-start.5) | collective-permute-done | bytes 1048608 | tf_op jit(solution)/shard_map/ppermute | solution.py:192
  98.0 9.1 %proj_pair.1 = f32[1024,1024]{1,0:T(8,128)} custom-call(bf16[1024,2176]{1,0:T(8,128)(2,1)} %lay.4.refs_0_, bf16[2048,2048]{1,0:T(8,128)(2,1)} %all-gather.5.cloned.1.call-done.refs_1_.refs_2_.refs_3_, bf16[256,2048]{1,0:T(8,128)(2,1)} %refs_6_.3, bf16[256,2048]{1,0:T(8,128)(2,1)} %copy-done.7, bf16[256,2048]{1,0:T(8,128)(2,1)} %copy-done.6, ...), custom_call_target="tpu_custom_call" | custom-call | flops 1024 | bytes 1024 | tf_op jit(solution)/shard_map/proj_pair/pallas_call | solution.py:42
  107.1 8.1 %scan_forward.1 = (f32[8,128,512]{2,1,0:T(8,128)}, f32[8,128,512]{2,1,0:T(8,128)}, f32[8,512]{1,0:T(8,128)}) custom-call(f32[8,128,128]{2,1,0:T(8,128)} %convert.1.keep_ref.refs_0_.refs_1_, f32[8,128,1024]{2,1,0:T(8,128)} %bitcast.32, f32[1,512]{1,0:T(1,128)} %reshape.194.bias_ref.refs_3_.refs_6_), custom_call_target="tpu_custom_call" | custom-call | flops 1024 | bytes 1024 | tf_op jit(solution)/shard_map/scan_forward/pallas_call | solution.py:828
  158.6 15.9 %collective-permute-done.13.refs_2_ = bf16[256,2176]{1,0:T(8,128)(2,1)S(1)} collective-permute-done((bf16[256,2176]{1,0:T(8,128)(2,1)}, bf16[256,2176]{1,0:T(8,128)(2,1)S(1)}, u32[]{:S(2)}, u32[]{:S(2)}) %collective-permute-start.13) | collective-permute-done | bytes 1114144 | tf_op jit(solution)/shard_map/ppermute | solution.py:192
  182.1 11.8 %collective-permute-done.14.refs_3_ = bf16[128,2176]{1,0:T(8,128)(2,1)S(1)} collective-permute-done((bf16[128,2176]{1,0:T(8,128)(2,1)}, bf16[128,2176]{1,0:T(8,128)(2,1)S(1)}, u32[]{:S(2)}, u32[]{:S(2)}) %collective-permute-start.14) | collective-permute-done | bytes 557088 | tf_op jit(solution)/shard_map/ppermute | solution.py:192
  204.5 21.0 %collective-permute-done.17.refs_2_ = bf16[256,2048]{1,0:T(8,128)(2,1)S(1)} collective-permute-done((bf16[256,2048]{1,0:T(8,128)(2,1)}, bf16[256,2048]{1,0:T(8,128)(2,1)S(1)}, u32[]{:S(2)}, u32[]{:S(2)}) %collective-permute-start.17) | collective-permute-done | bytes 1048608 | tf_op jit(solution)/shard_map/ppermute | solution.py:192
  228.4 8.9 %collective-permute-done.19.refs_4_ = bf16[128,2048]{1,0:T(8,128)(2,1)S(1)} collective-permute-done((bf16[128,2048]{1,0:T(8,128)(2,1)S(1)}, bf16[128,2048]{1,0:T(8,128)(2,1)S(1)}, u32[]{:S(2)}, u32[]{:S(2)}) %collective-permute-start.19) | collective-permute-done | bytes 524320 | tf_op jit(solution)/shard_map/ppermute | solution.py:188
  243.5 20.0 %feed_forward.1 = (bf16[1024,1408]{1,0:T(8,128)(2,1)}, f32[1024,1408]{1,0:T(8,128)}, f32[1024,1408]{1,0:T(8,128)}) custom-call(bf16[1024,2048]{1,0:T(8,128)(2,1)} %lay.6.refs_0_, bf16[2048,2816]{1,0:T(8,128)(2,1)} %all-gather.7.cloned.1.call-done.refs_1_), custom_call_target="tpu_custom_call" | custom-call | flops 1024 | bytes 1024 | tf_op jit(solution)/shard_map/feed_forward/pallas_call | solution.py:42
  263.6 10.2 %part_down.1.refs_2_ = bf16[1408,2048]{1,0:T(8,128)(2,1)} custom-call(bf16[1024,1408]{1,0:T(8,128)(2,1)} %get-tuple-element.90.refs_0_, bf16[1024,2048]{1,0:T(8,128)(2,1)} %lay.5.refs_4_.refs_1_.refs_0_), custom_call_target="tpu_custom_call" | custom-call | flops 1024 | bytes 1024 | tf_op jit(solution)/shard_map/part_down/pallas_call | solution.py:42
  274.0 12.2 %down.1 = (bf16[256,2048]{1,0:T(8,128)(2,1)}, bf16[256,2048]{1,0:T(8,128)(2,1)}, f32[512,2048]{1,0:T(8,128)}) custom-call(bf16[1024,1408]{1,0:T(8,128)(2,1)} %get-tuple-element.90.refs_0_, bf16[1408,2048]{1,0:T(8,128)(2,1)} %all-gather.9.cloned.1.call-done.refs_1_, bf16[1408,2048]{1,0:T(8,128)(2,1)} %part_down.1.refs_2_), custom_call_target="tpu_custom_call" | custom-call | flops 1024 | bytes 1024 | tf_op jit(solution)/shard_map/down/pallas_call | solution.py:42
  288.6 14.0 %feed_back.1.refs_0_.refs_1_ = bf16[1024,2816]{1,0:T(8,128)(2,1)} custom-call(bf16[1024,2048]{1,0:T(8,128)(2,1)} %lay.5.refs_4_.refs_1_.refs_0_, bf16[1408,2048]{1,0:T(8,128)(2,1)} %all-gather.9.cloned.1.call-done.refs_1_, f32[1024,1408]{1,0:T(8,128)} %get-tuple-element.94.refs_2_, f32[1024,1408]{1,0:T(8,128)} %get-tuple-element.95.refs_3_, ...), custom_call_target="tpu_custom_call" | custom-call | flops 1024 | bytes 1024 | tf_op jit(solution)/shard_map/feed_back/pallas_call | solution.py:42
  302.7 18.2 %grad_mid.1 = (bf16[256,2048]{1,0:T(8,128)(2,1)}, bf16[256,2048]{1,0:T(8,128)(2,1)}, f32[512,2048]{1,0:T(8,128)}) custom-call(bf16[1024,2816]{1,0:T(8,128)(2,1)} %feed_back.1.refs_0_.refs_1_, bf16[2048,2816]{1,0:T(8,128)(2,1)} %all-gather.7.cloned.1.call-done.refs_1_), custom_call_target="tpu_custom_call" | custom-call | flops 1024 | bytes 1024 | tf_op jit(solution)/shard_map/grad_mid/pallas_call | solution.py:42
  322.4 17.8 %part_ff.1.refs_3_ = bf16[2048,2816]{1,0:T(8,128)(2,1)} custom-call(bf16[1024,2048]{1,0:T(8,128)(2,1)} %lay.6.refs_0_, bf16[1024,2816]{1,0:T(8,128)(2,1)} %feed_back.1.refs_0_.refs_1_, bf16[256,2048]{1,0:T(8,128)(2,1)} %get-tuple-element.96.refs_2_), custom_call_target="tpu_custom_call" | custom-call | flops 1024 | bytes 1024 | tf_op jit(solution)/shard_map/part_ff/pallas_call | solution.py:42
  351.5 8.1 %collective-permute-done.23.refs_4_ = bf16[128,2048]{1,0:T(8,128)(2,1)S(1)} collective-permute-done((bf16[128,2048]{1,0:T(8,128)(2,1)}, bf16[128,2048]{1,0:T(8,128)(2,1)S(1)}, u32[]{:S(2)}, u32[]{:S(2)}) %collective-permute-start.23) | collective-permute-done | bytes 524320 | tf_op jit(solution)/shard_map/ppermute | solution.py:188
  377.6 21.5 %collective-permute-done.29.refs_2_ = bf16[256,2176]{1,0:T(8,128)(2,1)S(1)} collective-permute-done((bf16[256,2176]{1,0:T(8,128)(2,1)}, bf16[256,2176]{1,0:T(8,128)(2,1)S(1)}, u32[]{:S(2)}, u32[]{:S(2)}) %collective-permute-start.29) | collective-permute-done | bytes 1114144 | tf_op jit(solution)/shard_map/ppermute | solution.py:192
  425.5 9.4 %scan_backward.1 = (f32[8,128,512]{2,1,0:T(8,128)}, f32[8,128,512]{2,1,0:T(8,128)}, f32[8,512]{1,0:T(8,128)}, bf16[8,128,512]{2,1,0:T(8,128)(2,1)}, f32[1,512]{1,0:T(1,128)}) custom-call(f32[8,128,128]{2,1,0:T(8,128)} %convert.1.keep_ref.refs_0_.refs_1_, f32[8,128,1024]{2,1,0:T(8,128)} %bitcast.33, f32[8,128,512]{2,1,0:T(8,128)} %bitcast.38, ...), custom_call_target="tpu_custom_call" | custom-call | flops 1024 | bytes 1024 | tf_op jit(solution)/shard_map/scan_backward/pallas_call | solution.py:42
  448.4 9.1 %reduce-scatter.7.cloned.1.call-done.refs_1_ = bf16[256,2816]{1,0:T(8,128)(2,1)} async-done(((bf16[2048,2816]{1,0:T(8,128)(2,1)}), bf16[256,2816]{1,0:T(8,128)(2,1)}) %reduce-scatter.7.cloned.1.call-update) | async-done | bytes 1441808 | tf_op jit(solution)/shard_map/reduce_scatter | solution.py:1174
  463.7 15.6 %all-gather = f32[64,512]{1,0:T(8,128)} all-gather(f32[8,512]{1,0:T(8,128)S(1)} %copy-done.45), channel_id=2, replica_groups=mesh['grp'=4,'seq'=8] {'seq'}, dimensions={0}, use_global_device_ids=true | all-gather | bytes 147456 | tf_op jit(solution)/shard_map/all_gather | solution.py:1268
  486.9 12.4 %grad_in.1 = (bf16[256,2048]{1,0:T(8,128)(2,1)}, bf16[256,2048]{1,0:T(8,128)(2,1)}, f32[512,2048]{1,0:T(8,128)}) custom-call(bf16[1024,1024]{1,0:T(8,128)(2,1)} %bitcast.39, bf16[1024,512]{1,0:T(8,128)(2,1)} %bitcast.47, bf16[2048,2048]{1,0:T(8,128)(2,1)} %all-gather.5.cloned.1.call-done.refs_1_.refs_2_.refs_3_, ...), custom_call_target="tpu_custom_call" | custom-call | flops 1024 | bytes 1024 | tf_op jit(solution)/shard_map/grad_in/pallas_call | solution.py:42
  504.8 10.2 %part_pair.1.refs_6_ = bf16[2048,1024]{1,0:T(8,128)(2,1)} custom-call(bf16[1024,2176]{1,0:T(8,128)(2,1)} %lay.4.refs_0_, bf16[1024,1024]{1,0:T(8,128)(2,1)} %bitcast.40, bf16[256,2048]{1,0:T(8,128)(2,1)} %get-tuple-element.120.refs_2_, bf16[96,2048]{1,0:T(8,128)(2,1)} %copy-done.24, bf16[80,2048]{1,0:T(8,128)(2,1)} %copy-done.25, ...), custom_call_target="tpu_custom_call" | custom-call | flops 1024 | bytes 1024 | tf_op jit(solution)/shard_map/part_pair/pallas_call | solution.py:42
  518.3 8.1 %place_rows.1 = f32[4,176,2048]{2,1,0:T(8,128)} custom-call(s32[1]{0:T(128)} %bitcast.6.refs_0_, bf16[176,2048]{1,0:T(8,128)(2,1)} %reduce-scatter.5.cloned.1.call-done.refs_1_, bf16[176,2048]{1,0:T(8,128)(2,1)} %copy-done.8, bf16[176,2048]{1,0:T(8,128)(2,1)} %copy-done.11, bf16[96,2048]{1,0:T(8,128)(2,1)} %copy-done.24, bf16[80,2048]{1,0:T(8,128)(2,1)} %copy-done.25, ...), custom_call_target="tpu_custom_call" | custom-call | flops 1024 | bytes 1024 | tf_op jit(solution)/shard_map/place_rows/pallas_call | solution.py:42
  534.7 16.9 %collective-permute-done.40.refs_3_ = bf16[128,2048]{1,0:T(8,128)(2,1)S(1)} collective-permute-done((bf16[128,2048]{1,0:T(8,128)(2,1)}, bf16[128,2048]{1,0:T(8,128)(2,1)S(1)}, u32[]{:S(2)}, u32[]{:S(2)}) %collective-permute-start.40) | collective-permute-done | bytes 524320 | tf_op jit(solution)/shard_map/ppermute | solution.py:192
  570.3 8.1 %place_columns.3 = (f32[256,5632]{1,0:T(8,128)}, f32[256,5632]{1,0:T(8,128)}) custom-call(s32[1]{0:T(128)} %bitcast.6.refs_0_, bf16[256,2816]{1,0:T(8,128)(2,1)} %reduce-scatter.7.cloned.1.call-done.refs_1_, bf16[256,2816]{1,0:T(8,128)(2,1)} %copy-done.4, bf16[256,2816]{1,0:T(8,128)(2,1)} %copy-done.2, bf16[128,2816]{1,0:T(8,128)(2,1)} %copy-done.31, ...), custom_call_target="tpu_custom_call" | custom-call | flops 1024 | bytes 1024 | tf_op jit(solution)/shard_map/place_columns/pallas_call | solution.py:42
  (311 shorter events, 269.9 us)
Async XLA Ops:
  7.2 89.8 %all-gather.5.cloned.1.call-start = ((), (), s32[]{:S(2)}) async-start(), calls=%async_computation.4 | async-start | bytes 9437184 | tf_op jit(solution)/shard_map/all_gather | solution.py:1171
  11.6 231.9 %all-gather.7.cloned.1.call-start = ((), (), s32[]{:S(2)}) async-start(), calls=%async_computation.5 | async-start | bytes 12976128 | tf_op jit(solution)/shard_map/all_gather | solution.py:1171
  21.0 253.0 %all-gather.9.cloned.1.call-start = ((), (), s32[]{:S(2)}) async-start(), calls=%async_computation.6 | async-start | bytes 6488064 | tf_op jit(solution)/shard_map/all_gather | solution.py:1171
  22.0 396.4 %reduce-scatter.5.cloned.1.call-start = ((), (), s32[]{:S(2)}) async-start(), calls=%async_computation.7 | async-start | bytes 6488064 | tf_op jit(solution)/shard_map/reduce_scatter | solution.py:1174
  22.1 28.7 %collective-permute-start.1 = (bf16[256,2176]{1,0:T(8,128)(2,1)}, bf16[256,2176]{1,0:T(8,128)(2,1)S(1)}, u32[]{:S(2)}, u32[]{:S(2)}) collective-permute-start(bf16[256,2176]{1,0:T(8,128)(2,1)} %norm_in.1.refs_3_.refs_0_), channel_id=1, source_target_pairs={{0,16},{16,0},{8,24},{24,8},{1,17},{17,1},{9,25},{25,9},{2,18},{18... | collective-permute-start | bytes 3342344 | tf_op jit(solution)/shard_map/ppermute | solution.py:192
  25.2 28.6 %collective-permute-start = (bf16[256,2176]{1,0:T(8,128)(2,1)}, bf16[256,2176]{1,0:T(8,128)(2,1)S(1)}, u32[]{:S(2)}, u32[]{:S(2)}) collective-permute-start(bf16[256,2176]{1,0:T(8,128)(2,1)} %norm_in.1.refs_3_.refs_0_), channel_id=1, source_target_pairs={{0,8},{8,0},{16,24},{24,16},{1,9},{9,1},{17,25},{25,17},{2,10},{10... | collective-permute-start | bytes 3342344 | tf_op jit(solution)/shard_map/ppermute | solution.py:188
  26.6 46.7 %collective-permute-start.5 = (bf16[256,2048]{1,0:T(8,128)(2,1)}, bf16[256,2048]{1,0:T(8,128)(2,1)S(1)}, u32[]{:S(2)}, u32[]{:S(2)}) collective-permute-start(bf16[256,2048]{1,0:T(8,128)(2,1)} %refs_6_.3), channel_id=1, source_target_pairs={{0,16},{16,0},{8,24},{24,8},{1,17},{17,1},{9,25},{25,9},{2,18},{18... | collective-permute-start | bytes 3145736 | tf_op jit(solution)/shard_map/ppermute | solution.py:192
  27.2 49.0 %collective-permute-start.4 = (bf16[256,2048]{1,0:T(8,128)(2,1)}, bf16[256,2048]{1,0:T(8,128)(2,1)S(1)}, u32[]{:S(2)}, u32[]{:S(2)}) collective-permute-start(bf16[256,2048]{1,0:T(8,128)(2,1)} %refs_6_.3), channel_id=1, source_target_pairs={{0,8},{8,0},{16,24},{24,16},{1,9},{9,1},{17,25},{25,17},{2,10},{10... | collective-permute-start | bytes 3145736 | tf_op jit(solution)/shard_map/ppermute | solution.py:188
  51.7 35.7 %collective-permute-start.3 = (bf16[128,2176]{1,0:T(8,128)(2,1)}, bf16[128,2176]{1,0:T(8,128)(2,1)}, u32[]{:S(2)}, u32[]{:S(2)}) collective-permute-start(bf16[128,2176]{1,0:T(8,128)(2,1)} %slice.85), channel_id=1, source_target_pairs={{0,8},{8,0},{16,24},{24,16},{1,9},{9,1},{17,25},{25,17},{2,10},{10... | collective-permute-start | bytes 1671176 | tf_op jit(solution)/shard_map/ppermute | solution.py:188
  54.7 32.7 %collective-permute-start.2 = (bf16[128,2176]{1,0:T(8,128)(2,1)}, bf16[128,2176]{1,0:T(8,128)(2,1)}, u32[]{:S(2)}, u32[]{:S(2)}) collective-permute-start(bf16[128,2176]{1,0:T(8,128)(2,1)} %slice.84), channel_id=1, source_target_pairs={{0,16},{16,0},{8,24},{24,8},{1,17},{17,1},{9,25},{25,9},{2,18},{18... | collective-permute-start | bytes 1671176 | tf_op jit(solution)/shard_map/ppermute | solution.py:192
  147.7 26.9 %collective-permute-start.13 = (bf16[256,2176]{1,0:T(8,128)(2,1)}, bf16[256,2176]{1,0:T(8,128)(2,1)S(1)}, u32[]{:S(2)}, u32[]{:S(2)}) collective-permute-start(bf16[256,2176]{1,0:T(8,128)(2,1)} %get-tuple-element.86), channel_id=1, source_target_pairs={{0,16},{16,0},{8,24},{24,8},{1,17},{17,1},{9,25},{25,9},{2,18},{18... | collective-permute-start | bytes 3342344 | tf_op jit(solution)/shard_map/ppermute | solution.py:192
  149.1 26.6 %collective-permute-start.12 = (bf16[256,2176]{1,0:T(8,128)(2,1)}, bf16[256,2176]{1,0:T(8,128)(2,1)S(1)}, u32[]{:S(2)}, u32[]{:S(2)}) collective-permute-start(bf16[256,2176]{1,0:T(8,128)(2,1)} %get-tuple-element.85.refs_1_), channel_id=1, source_target_pairs={{0,8},{8,0},{16,24},{24,16},{1,9},{9,1},{17,25},{25,17},{2,10},{10... | collective-permute-start | bytes 3342344 | tf_op jit(solution)/shard_map/ppermute | solution.py:188
  273.7 183.7 %reduce-scatter.7.cloned.1.call-start = ((), (), s32[]{:S(2)}) async-start(), calls=%async_computation.8 | async-start | bytes 12976128 | tf_op jit(solution)/shard_map/reduce_scatter | solution.py:1174
  286.2 54.2 %collective-permute-start.21 = (bf16[256,2048]{1,0:T(8,128)(2,1)}, bf16[256,2048]{1,0:T(8,128)(2,1)S(1)}, u32[]{:S(2)}, u32[]{:S(2)}) collective-permute-start(bf16[256,2048]{1,0:T(8,128)(2,1)} %get-tuple-element.93), channel_id=1, source_target_pairs={{0,16},{16,0},{8,24},{24,8},{1,17},{17,1},{9,25},{25,9},{2,18},{18... | collective-permute-start | bytes 3145736 | tf_op jit(solution)/shard_map/ppermute | solution.py:192
  287.2 53.2 %collective-permute-start.20 = (bf16[256,2048]{1,0:T(8,128)(2,1)}, bf16[256,2048]{1,0:T(8,128)(2,1)S(1)}, u32[]{:S(2)}, u32[]{:S(2)}) collective-permute-start(bf16[256,2048]{1,0:T(8,128)(2,1)} %get-tuple-element.92.refs_4_), channel_id=1, source_target_pairs={{0,8},{8,0},{16,24},{24,16},{1,9},{9,1},{17,25},{25,17},{2,10},{10... | collective-permute-start | bytes 3145736 | tf_op jit(solution)/shard_map/ppermute | solution.py:188
  340.3 194.5 %reduce-scatter.11.cloned.1.call-start = ((), (), s32[]{:S(2)}) async-start(), calls=%async_computation.10 | async-start | bytes 4718592 | tf_op jit(solution)/shard_map/reduce_scatter | solution.py:1174
  448.3 114.8 %reduce-scatter.9.cloned.1.call-start = ((), (), s32[]{:S(2)}) async-start(), calls=%async_computation.9 | async-start | bytes 4718592 | tf_op jit(solution)/shard_map/reduce_scatter | solution.py:1174
  457.5 45.1 %collective-permute-start.39 = (bf16[256,2816]{1,0:T(8,128)(2,1)}, bf16[256,2816]{1,0:T(8,128)(2,1)S(1)}, u32[]{:S(2)}, u32[]{:S(2)}) collective-permute-start(bf16[256,2816]{1,0:T(8,128)(2,1)} %reduce-scatter.7.cloned.1.call-done.refs_1_), channel_id=1, source_target_pairs={{0,16},{16,0},{8,24},{24,8},{1,17},{17,1},{9,25},{25,9},{2,18},{18... | collective-permute-start | bytes 4325384 | tf_op jit(solution)/shard_map/ppermute | solution.py:192
  458.9 43.6 %collective-permute-start.38 = (bf16[256,2816]{1,0:T(8,128)(2,1)}, bf16[256,2816]{1,0:T(8,128)(2,1)S(1)}, u32[]{:S(2)}, u32[]{:S(2)}) collective-permute-start(bf16[256,2816]{1,0:T(8,128)(2,1)} %reduce-scatter.7.cloned.1.call-done.refs_1_), channel_id=1, source_target_pairs={{0,8},{8,0},{16,24},{24,16},{1,9},{9,1},{17,25},{25,17},{2,10},{10... | collective-permute-start | bytes 4325384 | tf_op jit(solution)/shard_map/ppermute | solution.py:188
  461.4 41.1 %collective-permute-start.36 = (bf16[96,2048]{1,0:T(8,128)(2,1)S(1)}, bf16[96,2048]{1,0:T(8,128)(2,1)S(1)}, u32[]{:S(2)}, u32[]{:S(2)}) collective-permute-start(bf16[96,2048]{1,0:T(8,128)(2,1)S(1)} %slice.93), channel_id=1, source_target_pairs={{0,16},{16,0},{8,24},{24,8},{1,17},{17,1},{9,25},{25,9},{2,18},{18... | collective-permute-start | bytes 1179656 | tf_op jit(solution)/shard_map/ppermute | solution.py:192
  463.0 38.0 %collective-permute-start.37 = (bf16[80,2048]{1,0:T(8,128)(2,1)S(1)}, bf16[80,2048]{1,0:T(8,128)(2,1)S(1)}, u32[]{:S(2)}, u32[]{:S(2)}) collective-permute-start(bf16[80,2048]{1,0:T(8,128)(2,1)S(1)} %slice.94), channel_id=1, source_target_pairs={{0,8},{8,0},{16,24},{24,16},{1,9},{9,1},{17,25},{25,17},{2,10},{10... | collective-permute-start | bytes 983048 | tf_op jit(solution)/shard_map/ppermute | solution.py:188
  499.3 27.0 %collective-permute-start.35 = (bf16[256,2048]{1,0:T(8,128)(2,1)}, bf16[256,2048]{1,0:T(8,128)(2,1)}, u32[]{:S(2)}, u32[]{:S(2)}) collective-permute-start(bf16[256,2048]{1,0:T(8,128)(2,1)} %get-tuple-element.121), channel_id=1, source_target_pairs={{0,16},{16,0},{8,24},{24,8},{1,17},{17,1},{9,25},{25,9},{2,18},{18... | collective-permute-start | bytes 3145736 | tf_op jit(solution)/shard_map/ppermute | solution.py:192
  517.3 38.3 %collective-permute-start.43 = (bf16[128,2816]{1,0:T(8,128)(2,1)}, bf16[128,2816]{1,0:T(8,128)(2,1)S(1)}, u32[]{:S(2)}, u32[]{:S(2)}) collective-permute-start(bf16[128,2816]{1,0:T(8,128)(2,1)} %slice.96), channel_id=1, source_target_pairs={{0,8},{8,0},{16,24},{24,16},{1,9},{9,1},{17,25},{25,17},{2,10},{10... | collective-permute-start | bytes 2162696 | tf_op jit(solution)/shard_map/ppermute | solution.py:188
  517.9 37.7 %collective-permute-start.42 = (bf16[128,2816]{1,0:T(8,128)(2,1)S(1)}, bf16[128,2816]{1,0:T(8,128)(2,1)S(1)}, u32[]{:S(2)}, u32[]{:S(2)}) collective-permute-start(bf16[128,2816]{1,0:T(8,128)(2,1)S(1)} %slice.95), channel_id=1, source_target_pairs={{0,16},{16,0},{8,24},{24,8},{1,17},{17,1},{9,25},{25,9},{2,18},{18... | collective-permute-start | bytes 2162696 | tf_op jit(solution)/shard_map/ppermute | solution.py:192
  (96 other events, 1032.9 us)
Sparse Core Ops, SparseCore 0:
  11.7 84.6 all-gather.4
  98.7 109.3 all-gather.6
  209.7 58.5 all-gather.8
  273.9 62.5 reduce-scatter.4
  340.4 116.9 reduce-scatter.6
  460.2 49.2 reduce-scatter.10
  515.2 46.5 reduce-scatter.8
